TPU v7x, 32 devices: a whole 2x2x4 slice. The times are simulated.
32 devices in a mesh: replica: 2 (over x), section: 4 (over y, core), shard: 4 (over z).
Axes of the slice: x: 2, y: 2, z: 4, core: 2. Of those that a mesh axis runs over, the one named last changes fastest.
Arguments:
- inputs: bfloat16 [2, 1, 128, 1024], P('replica', None, None, 'shard'), may hold values from -17 to 17
- targets: bfloat16 [2, 1, 128, 1024], P('replica', None, None, 'shard'), may hold values from -6 to 6
- weight_a: bfloat16 [2, 4, 1024, 3072], P('replica', 'section', None, 'shard'), may hold values from -6 to 6
- weight_b: bfloat16 [2, 4, 3072, 1024], P('replica', 'section', 'shard'), may hold values from -6 to 6
- moment_a: bfloat16 [2, 4, 1024, 3072], P('replica', 'section', None, 'shard'), may hold values from -3 to 3
- moment_b: bfloat16 [2, 4, 3072, 1024], P('replica', 'section', 'shard'), may hold values from -3 to 3
- routes: int32 [1, 3, 2, 2], replicated, may hold values from 0 to 1, each once within a row
- partners: int32 [4, 2, 2, 2], replicated, may hold values from 0 to 1, as said below
Outputs:
- new_weight_a: bfloat16 [2, 4, 1024, 3072], P('replica', 'section', None, 'shard')
- new_weight_b: bfloat16 [2, 4, 3072, 1024], P('replica', 'section', 'shard')
- new_moment_a: bfloat16 [2, 4, 1024, 3072], P('replica', 'section', None, 'shard')
- new_moment_b: bfloat16 [2, 4, 3072, 1024], P('replica', 'section', 'shard')
Inputs may be any that keep to these rules, and one draw needn't show every extreme that they name: Each routes[m, s, q, :] names every replica once, so each replica of section s + 1 receives exactly one block from every replica of section s. For each section s, projection t and piece k, partners[s, t, k, :] is its own inverse (the partner of the partner is the replica itself); for each s, t and replica r, partners[s, t, :, r] names every replica once, and exactly one piece pairs r with itself.
All inputs are finite; a program needn't handle non-finite values.
Results may differ from a plain program's by a relative error of at most 0.022.
Values may be sent and summed in bfloat16 or wider, within the bound.
No kernel may reach another device: no remote copies, remote signals or barrier semaphores. Data moves between devices by JAX's collectives and lax.ppermute only.
A program may use at most 128 MiB of HBM per device.

v0:
```python
import functools
import math

import jax
import jax.numpy as jnp
from jax import lax
from jax.experimental import pallas as pl
from jax.experimental.pallas import tpu as pltpu
from jax.sharding import PartitionSpec as P

epsilon = 1e-05
inner_rate = 0.5
momentum_decay = 0.9
outer_rate = 0.7

axes = ("replica", "section", "shard")
contract_rows = (((0,), (0,)), ((), ()))
contract_last = (((1,), (1,)), ((), ()))


def dot(left, right, dims=(((1,), (0,)), ((), ()))):
    return lax.dot_general(left, right, dims, preferred_element_type=jnp.float32)


def outer_mix(weight, moment, delta):
    new_moment = momentum_decay * moment + delta
    new_weight = weight - outer_rate * (momentum_decay * new_moment + delta)
    return new_weight.astype(jnp.bfloat16), new_moment.astype(jnp.bfloat16)


def pack_kernel(size, starts, *refs):
    sources, (packed, buffer, read_sems, write_sems) = refs[:-4], refs[-4:]
    rows = pl.ds(pl.multiple_of(starts[0], size), size)
    reads, writes = [], []
    for k, source in enumerate(sources):
        there = pl.ds(k * size, size)
        reads.append(
            pltpu.make_async_copy(source.at[rows], buffer.at[there], read_sems.at[k])
        )
        writes.append(
            pltpu.make_async_copy(buffer.at[there], packed.at[there], write_sems.at[k])
        )
    for copy in reads:
        copy.start()
    for read, write in zip(reads, writes):
        read.wait()
        write.start()
    for copy in writes:
        copy.wait()


def pack(arrays, start, size):
    shape = (len(arrays) * size, arrays[0].shape[1])
    anywhere = pl.BlockSpec(memory_space=pl.ANY)
    return pl.pallas_call(
        functools.partial(pack_kernel, size),
        out_shape=jax.ShapeDtypeStruct(shape, arrays[0].dtype),
        in_specs=[pl.BlockSpec(memory_space=pltpu.SMEM)] + [anywhere] * len(arrays),
        out_specs=anywhere,
        scratch_shapes=[
            pltpu.VMEM(shape, arrays[0].dtype),
            pltpu.SemaphoreType.DMA((len(arrays),)),
            pltpu.SemaphoreType.DMA((len(arrays),)),
        ],
        compiler_params=pltpu.CompilerParams(vmem_limit_bytes=16 * 1024 * 1024),
        cost_estimate=pl.CostEstimate(
            flops=0, bytes_accessed=4 * shape[0] * shape[1], transcendentals=0
        ),
    )(start.reshape(1), *arrays)


class Sizes:
    def __init__(self, sections, row_count, width, local_hidden, panel, hidden_total, blocks):
        self.sections, self.row_count = sections, row_count
        self.width, self.local_hidden, self.panel = width, local_hidden, panel
        self.blocks = blocks
        self.block_rows = row_count // blocks
        self.panels_in = local_hidden // panel
        self.panels_out = width // panel
        self.scale_in = 1.0 / math.sqrt(width)
        self.scale_out = 1.0 / math.sqrt(hidden_total)


def chain_kernel(sz, step, forward, counts, *refs):
    refs = list(refs)

    def take(count):
        taken = refs[:count]
        del refs[:count]
        return taken

    first = forward and step == 0
    parts = 1 if first else 2
    (table,) = take(1)
    received, edges, sources = take(counts[0]), take(counts[1]), take(2 * parts)
    take(0 if first else 1)
    sends = take(counts[2])
    fresh_hbm, state = take(2)
    weights_in, weights_out, landing, rows, up, out, slope, wide_store = take(8)
    weight_sems, block_sems, edge_sems, send_sems, state_sems = take(5)
    panel, width, hidden_size = sz.panel, sz.width, sz.local_hidden
    links = sz.sections - 1
    whole = pl.ds(0, sz.row_count)

    def weight_copy(d, which):
        weights = (weights_in, weights_out)[which]
        return pltpu.make_async_copy(
            sources[2 * d + which], weights.at[d], weight_sems.at[d, which]
        )

    def place(line, e):
        return pl.ds(pl.multiple_of(table[line, e], sz.block_rows), sz.block_rows)

    def state_part(k, columns):
        return state.at[pl.ds(k * sz.row_count, sz.row_count), pl.ds(0, columns)]

    rows_hbm, slope_hbm = state_part(0, width), state_part(1, 2 * hidden_size)

    @pl.when(table[links + 1, step] == 1)
    def _():
        sequence = [
            (d, which if forward else 1 - which) for d in range(parts) for which in range(2)
        ]
        arrive = links if forward else step
        first_copies = []
        for i, source in enumerate(received):
            e, a = divmod(i, 2)
            rows_there = whole if len(received) == 2 else place(arrive, e)
            first_copies.append(
                pltpu.make_async_copy(source, landing.at[a, rows_there], block_sems.at[i])
            )
        for d, source in enumerate(edges):
            column = pl.ds(pl.multiple_of(table[links + 2, d], panel), panel)
            first_copies.append(
                pltpu.make_async_copy(source, out.at[:, column], edge_sems.at[d])
            )
        if not forward:
            first_copies.append(pltpu.make_async_copy(rows_hbm, wide_store, state_sems.at[0]))
            first_copies.append(pltpu.make_async_copy(slope_hbm, slope, state_sems.at[1]))
        for copy in first_copies:
            copy.start()
        for item in sequence[:2]:
            weight_copy(*item).start()

        def arrived(item):
            weight_copy(*item).wait()
            later = sequence.index(item) + 2
            if later < len(sequence):
                weight_copy(*sequence[later]).start()

        for copy in first_copies:
            copy.wait()
        if received:
            total = landing[0].astype(jnp.float32) + landing[1].astype(jnp.float32)
            total = total.astype(jnp.bfloat16)
        if forward:
            rows[...] = total if received else out[...]
        elif edges:
            goal = out[...].astype(jnp.float32)
            up[...] = (total.astype(jnp.float32) - goal).astype(jnp.bfloat16)
        else:
            up[...] = total
        fresh = rows if forward else up
        store_copies = [pltpu.make_async_copy(fresh, fresh_hbm, state_sems.at[2])]
        if forward:
            wide = rows[...].astype(jnp.float32)
            wide_store[...] = wide
            store_copies.append(pltpu.make_async_copy(wide_store, rows_hbm, state_sems.at[0]))
        else:
            wide = wide_store[...]
        inverse_rms = lax.rsqrt(jnp.mean(wide * wide, axis=1, keepdims=True) + epsilon)
        leads = table[links + 2, 4] == 1
        if forward:
            normed = (wide * inverse_rms).astype(jnp.bfloat16)
            total = [jnp.zeros((sz.row_count, panel), jnp.float32) for _ in range(sz.panels_out)]
            for d in range(parts):
                arrived((d, 0))
                hidden = []
                for p in range(sz.panels_in):
                    weight = weights_in[d, :, p * panel : (p + 1) * panel]
                    preact = dot(normed, weight) * sz.scale_in
                    gate = jax.nn.sigmoid(preact)
                    hidden.append((preact * gate).astype(jnp.bfloat16))
                    column = d * hidden_size + p * panel
                    slope[:, column : column + panel] = gate * (1.0 + preact * (1.0 - gate))
                hidden = jnp.concatenate(hidden, axis=1)
                arrived((d, 1))
                for n in range(sz.panels_out):
                    weight = weights_out[d, :, n * panel : (n + 1) * panel]
                    total[n] = total[n] + dot(hidden, weight)
            total = jnp.concatenate(total, axis=1) * sz.scale_out
            out[...] = (total + jnp.where(leads, wide, 0.0)).astype(jnp.bfloat16)
            store_copies.append(pltpu.make_async_copy(slope, slope_hbm, state_sems.at[1]))
        else:
            up_turned = up[...].T
            total = jnp.zeros((width, sz.row_count), jnp.float32)
            for d in range(parts):
                arrived((d, 1))
                grad_hidden = dot(weights_out[d], up_turned)
                local_slope = slope[:, d * hidden_size : (d + 1) * hidden_size].T
                grad_pre = (grad_hidden * sz.scale_out * local_slope).astype(jnp.bfloat16)
                arrived((d, 0))
                total = total + dot(weights_in[d], grad_pre)
            total = total.T * sz.scale_in
            exact = wide * inverse_rms
            along = jnp.mean(total * exact, axis=1, keepdims=True)
            own = jnp.where(leads, up[...].astype(jnp.float32), 0.0)
            out[...] = (own + inverse_rms * (total - exact * along)).astype(jnp.bfloat16)
        leave = step if forward else links
        send_copies = []
        for e, target in enumerate(sends):
            rows_here = whole if len(sends) == 1 else place(leave, e)
            send_copies.append(
                pltpu.make_async_copy(out.at[rows_here], target, send_sems.at[e])
            )
        for copy in send_copies + store_copies:
            copy.start()
        for copy in send_copies + store_copies:
            copy.wait()


def chain_step(sz, step, forward, table, received, edges, weights, state):
    first = forward and step == 0
    count = 1 if forward and step in (0, sz.sections - 1) else sz.blocks
    anywhere = pl.BlockSpec(memory_space=pl.ANY)
    operands = [table, *received, *edges, *(weights[:2] if first else [*weights, state])]
    block = jax.ShapeDtypeStruct((sz.row_count // count, sz.width), jnp.bfloat16)
    kept = jax.ShapeDtypeStruct((2 * sz.row_count, 2 * sz.local_hidden), jnp.float32)
    fresh = jax.ShapeDtypeStruct((sz.row_count, sz.width), jnp.bfloat16)
    shapes = [block] * count + [fresh, kept]
    in_hbm = pl.BlockSpec(memory_space=pltpu.HBM)
    in_specs = [pl.BlockSpec(memory_space=pltpu.SMEM)] + [anywhere] * (len(operands) - 1)
    if not first:
        in_specs[-1] = in_hbm
    whole = (sz.row_count, sz.width)
    results = pl.pallas_call(
        functools.partial(
            chain_kernel, sz, step, forward, (len(received), len(edges), count)
        ),
        out_shape=shapes,
        in_specs=in_specs,
        out_specs=[anywhere] * (count + 1) + [in_hbm],
        input_output_aliases={} if first else {len(operands) - 1: count + 1},
        scratch_shapes=[
            pltpu.VMEM((2, sz.width, sz.local_hidden), jnp.bfloat16),
            pltpu.VMEM((2, sz.local_hidden, sz.width), jnp.bfloat16),
            pltpu.VMEM((2,) + whole, jnp.bfloat16),
            pltpu.VMEM(whole, jnp.bfloat16),
            pltpu.VMEM(whole, jnp.bfloat16),
            pltpu.VMEM(whole, jnp.bfloat16),
            pltpu.VMEM((sz.row_count, 2 * sz.local_hidden), jnp.float32),
            pltpu.VMEM(whole, jnp.float32),
            pltpu.SemaphoreType.DMA((2, 2)),
            pltpu.SemaphoreType.DMA((max(1, len(received)),)),
            pltpu.SemaphoreType.DMA((4,)),
            pltpu.SemaphoreType.DMA((count,)),
            pltpu.SemaphoreType.DMA((3,)),
        ],
        compiler_params=pltpu.CompilerParams(vmem_limit_bytes=32 * 1024 * 1024),
        cost_estimate=pl.CostEstimate(
            flops=8 * sz.row_count * sz.width * sz.local_hidden,
            bytes_accessed=8 * sz.width * sz.local_hidden,
            transcendentals=0,
        ),
    )(*operands)
    return list(results[:count]), results[count], results[count + 1]


def share_kernel(sz, whole, *refs):
    if whole:
        known, source, normed_ref, hidden_ref, slope, weights, sem = refs
    else:
        known, slope, source, grad_pre, weights, sem = refs
    panel = sz.panel
    copy = pltpu.make_async_copy(source, weights, sem)
    copy.start()
    if whole:
        wide = known[...].astype(jnp.float32)
        inverse_rms = lax.rsqrt(jnp.mean(wide * wide, axis=1, keepdims=True) + epsilon)
        normed = (wide * inverse_rms).astype(jnp.bfloat16)
        normed_ref[...] = normed
        copy.wait()
        for p in range(sz.panels_in):
            here = slice(p * panel, (p + 1) * panel)
            preact = dot(normed, weights[:, here]) * sz.scale_in
            gate = jax.nn.sigmoid(preact)
            hidden_ref[:, here] = (preact * gate).astype(jnp.bfloat16)
            slope[:, here] = gate * (1.0 + preact * (1.0 - gate))
    else:
        copy.wait()
        grad_hidden = dot(known[...], weights[...], contract_last)
        grad_pre[...] = (grad_hidden * sz.scale_out * slope[...]).astype(jnp.bfloat16)


def share_call(sz, operands, weight):
    whole = len(operands) == 1
    rows_count, hidden_size = sz.row_count, sz.local_hidden
    narrow = jax.ShapeDtypeStruct((rows_count, hidden_size), jnp.bfloat16)
    shapes = [narrow]
    if whole:
        shapes = [
            jax.ShapeDtypeStruct((rows_count, sz.width), jnp.bfloat16),
            narrow,
            jax.ShapeDtypeStruct((rows_count, hidden_size), jnp.float32),
        ]
    inside = pl.BlockSpec(memory_space=pltpu.VMEM)
    return pl.pallas_call(
        functools.partial(share_kernel, sz, whole),
        out_shape=shapes,
        in_specs=[inside] * len(operands) + [pl.BlockSpec(memory_space=pl.ANY)],
        out_specs=[inside] * len(shapes),
        scratch_shapes=[
            pltpu.VMEM(weight.shape, jnp.bfloat16),
            pltpu.SemaphoreType.DMA,
        ],
        compiler_params=pltpu.CompilerParams(vmem_limit_bytes=24 * 1024 * 1024),
        cost_estimate=pl.CostEstimate(
            flops=2 * rows_count * sz.width * hidden_size,
            bytes_accessed=2 * sz.width * hidden_size,
            transcendentals=0,
        ),
    )(*operands, weight)


def per_device(inputs, targets, weight_a, weight_b, moment_a, moment_b, routes, partners):
    replicas = lax.axis_size("replica")
    sections = lax.axis_size("section")
    shards = lax.axis_size("shard")
    replica_id = lax.axis_index("replica")
    section_id = lax.axis_index("section")
    shard_id = lax.axis_index("shard")
    row_count = inputs.shape[2]
    panel = inputs.shape[3]
    width = weight_a.shape[2]
    local_hidden = weight_a.shape[3]
    assert inputs.shape[1] == 1 and shards == 4
    assert local_hidden % panel == 0 and sections > 2
    hidden_total = local_hidden * shards
    scale_in = 1.0 / math.sqrt(width)
    scale_out = 1.0 / math.sqrt(hidden_total)
    weight_in = weight_a[0, 0]
    weight_out = weight_b[0, 0]
    block_rows = row_count // replicas
    links = sections - 1
    in_kernel = block_rows % 16 == 0
    blocks = replicas if in_kernel else 1
    sz = Sizes(sections, row_count, width, local_hidden, panel, hidden_total, blocks)

    def flat(replica, section, shard):
        return (replica * sections + section) * shards + shard

    def turn(section):
        return (section ^ (section >> 1)) & 1

    def holders(section):
        return [j for j in range(shards) if (j & 1) != turn(section)]

    def move(array, sources, target):
        pairs = [
            (flat(r, s, j), flat(*target(r, s, j)))
            for r in range(replicas)
            for s, j in sources
        ]
        return lax.ppermute(array, axes, pairs)

    def holder_sources(active):
        return [(s, j) for s in active for j in holders(s)]

    def to_holders(array, offset, active):
        sources = [(s, j ^ offset) for s, j in holder_sources(active)]
        return move(array, sources, lambda r, s, j: (r, s, j ^ offset))

    def from_holders(array, offset, active):
        return move(array, holder_sources(active), lambda r, s, j: (r, s, j ^ offset))

    def between_holders(array, offset, other_half, section, step):
        shift = turn(section) ^ turn(section + step) ^ (2 * other_half)
        return move(
            array,
            holder_sources([section]),
            lambda r, s, j: ((r + offset) % replicas, s + step, j ^ shift),
        )

    def across_replicas(array, offset, active):
        return move(
            array,
            [(s, j) for s in active for j in range(shards)],
            lambda r, s, j: ((r + offset) % replicas, s, j),
        )

    every = range(sections)
    others = range(1, replicas)
    is_holder = (shard_id & 1) != turn(section_id)

    edge = jnp.where(section_id == 0, inputs[0, 0], targets[0, 0])
    ends = [(s, j) for s in (0, links) for j in range(shards)]
    edges = [edge] + [
        move(edge, ends, lambda r, s, j, d=d: (r, s, j ^ d)) for d in range(1, shards)
    ]
    rest = range(1, sections)
    near = [to_holders(weight_in, 1, rest), to_holders(weight_out, 1, rest)]

    tables = lax.dynamic_index_in_dim(partners, section_id, 0, keepdims=False)

    def piece_of(table, offset):
        wanted = (replica_id + offset) % replicas
        return jnp.argmax(table[:, replica_id] == wanted).astype(jnp.int32)

    pieces_in = [piece_of(tables[0], e) for e in range(replicas)]
    pieces_out = [piece_of(tables[1], e) for e in range(replicas)]
    size_in = width // replicas
    size_out = local_hidden // replicas

    def piece(array, index, size, axis=0):
        return lax.dynamic_slice_in_dim(array, index * size, size, axis)

    def exchange(arrays, active):
        return [across_replicas(array, e, active) for e, array in zip(others, arrays)]

    packed_in = [
        pack([weight_in, moment_a[0, 0]], pieces_in[e] * size_in, size_in) for e in others
    ]
    packed_out = [
        pack([weight_out, moment_b[0, 0]], pieces_out[e] * size_out, size_out) for e in others
    ]
    early = range(sections // 2, sections)
    late = range(sections // 2)
    far_states_in = exchange(packed_in, every)

    offsets = jnp.arange(replicas, dtype=jnp.int32)
    there = (replica_id + offsets) % replicas
    back = (replica_id - offsets) % replicas
    own_routes = routes[0, :, replica_id, :]
    slots = jnp.sum(
        (own_routes[:, None, :] == there[None, :, None]).astype(jnp.int32)
        * offsets[None, None, :],
        axis=2,
    )
    columns = max(replicas, sections, shards + 1)
    steps = jnp.arange(sections)
    ours = ((is_holder | (steps == 0)) & (section_id == steps)).astype(jnp.int32)
    features = (shard_id ^ jnp.arange(shards, dtype=jnp.int32)) * panel
    leads = (is_holder & ((shard_id & 2) == 0)).astype(jnp.int32)
    features = jnp.append(features, leads)

    def line(values):
        return jnp.pad(values, ((0, 0), (0, columns - values.shape[1])))

    starts = jnp.concatenate([slots, back[None]]) * block_rows
    if not in_kernel:
        starts = jnp.zeros_like(starts)
    table = jnp.concatenate([line(starts), line(ours[None]), line(features[None])])
    table = table.astype(jnp.int32)

    def send_blocks(sends, arrived, left, section, step):
        sign = step
        if in_kernel:
            return [
                between_holders(sends[e], sign * e, a, section, step)
                for e in range(replicas)
                for a in range(2)
            ]
        parts = sends[0].reshape(replicas, block_rows, width)
        moved = [jnp.zeros_like(parts), jnp.zeros_like(parts)]
        for e in range(replicas):
            chosen = lax.dynamic_index_in_dim(parts, left[e], 0, keepdims=False)
            for a in range(2):
                got = between_holders(chosen, sign * e, a, section, step)
                moved[a] = lax.dynamic_update_index_in_dim(moved[a], got, arrived[e], 0)
        return [one.reshape(row_count, width) for one in moved]

    row_parts = []

    def spread_rows(received, rows, active):
        received, rows, row_parts[:] = lax.optimization_barrier(
            (received, rows, row_parts)
        )
        row_parts.append(from_holders(rows, 1, active))
        return received

    weights = [weight_in, weight_out, *near]
    received, state = [], None
    for step in every:
        sends, fresh, state = chain_step(
            sz, step, True, table, received, edges if step == 0 else [], weights, state
        )
        rows = fresh if step == 0 else jnp.where(section_id == step, fresh, rows)
        if step == 0:
            total = sends[0].astype(jnp.float32)
            total = total + to_holders(sends[0], 1, [0]).astype(jnp.float32)
            sends = [total.astype(jnp.bfloat16)]
            if in_kernel:
                sends = [piece(sends[0], slots[0, e], block_rows) for e in range(replicas)]
        if step < links:
            received = send_blocks(sends, back, slots[step], step, 1)
            if step == 0:
                received, far_states_in, packed_out = lax.optimization_barrier(
                    (received, far_states_in, packed_out)
                )
                far_states_out = exchange(packed_out, early)
        else:
            received = [sends[0], from_holders(sends[0], 2, [links])]
        if len(late) - 1 <= step < links:
            received = spread_rows(received, rows, late if step < len(late) else [step])
        if step == len(late) - 1:
            received, packed_out = lax.optimization_barrier((received, packed_out))
            far_late = exchange(packed_out, late)
        if step == len(late):
            received, far_states_out = lax.optimization_barrier((received, far_states_out))

    for step in reversed(range(1, sections)):
        sends, fresh, state = chain_step(
            sz, step, False, table, received, edges if step == links else [], weights, state
        )
        upstream = fresh if step == links else jnp.where(section_id == step, fresh, upstream)
        received = send_blocks(sends, slots[step - 1], back, step, -1)
        if step == links:
            received = spread_rows(received, rows, [links])
        if step == len(late):
            received, far_late, row_parts = lax.optimization_barrier(
                (received, far_late, row_parts)
            )

    own_rows = jnp.where(is_holder, rows, sum(row_parts[1:], row_parts[0]))
    normed, hidden, slope = share_call(sz, [own_rows], weight_in)

    def bundle(e):
        first, second = normed, hidden
        first = piece(first, pieces_in[e], size_in, 1)
        return jnp.concatenate([first, piece(second, pieces_out[e], size_out, 1)], axis=1)

    bundles = exchange([bundle(e) for e in others], every)
    received, bundles = lax.optimization_barrier((received, bundles))
    far_normed = [one[:, :size_in] for one in bundles]
    far_hidden = [one[:, size_in:] for one in bundles]

    halves = []
    for a in range(2):
        half = received[a]
        if in_kernel:
            half = jnp.zeros((row_count, width), jnp.bfloat16)
            for e in range(replicas):
                half = lax.dynamic_update_slice_in_dim(
                    half, received[2 * e + a], slots[0, e] * block_rows, 0
                )
        halves.append(half.astype(jnp.float32))
    first_up = (halves[0] + halves[1]).astype(jnp.bfloat16)
    upstream = jnp.where(section_id == 0, first_up, upstream)
    upstream = jnp.where(is_holder, upstream, from_holders(upstream, 1, every))
    far_up = exchange([upstream] * len(others), every)
    (grad_pre,) = share_call(sz, [upstream, slope], weight_out)
    far_pre = exchange([grad_pre] * len(others), every)
    far_states_out = [
        jnp.where(section_id < len(late), one, two)
        for one, two in zip(far_late, far_states_out)
    ]
    far_states = {0: far_states_in, 2: far_states_out}

    def far_part(e, which):
        size = size_out if which & 2 else size_in
        both = far_states[which & 2][e - 1]
        return both[size:] if which & 1 else both[:size]

    def as_delta(left, right, scale):
        return (inner_rate * (dot(left, right, contract_rows) * scale)).astype(jnp.bfloat16)

    def finish(weight, moment, left, right, which, far_left, far_right, scale, pieces, size):
        new_weight, new_moment = outer_mix(
            weight.astype(jnp.float32),
            moment.astype(jnp.float32),
            as_delta(left, right, scale).astype(jnp.float32),
        )
        for e in others:
            back = replicas - e

            def mean(own_array, far_array):
                return 0.5 * (own_array.astype(jnp.float32) + far_array.astype(jnp.float32))

            index = pieces[back]
            own_left = piece(left, index, size, 1)
            part_weight, part_moment = outer_mix(
                mean(piece(weight, index, size), far_part(e, which)),
                mean(piece(moment, index, size), far_part(e, which + 1)),
                mean(
                    as_delta(own_left, right, scale),
                    as_delta(far_left[e - 1], far_right[e - 1], scale),
                ),
            )
            new_weight = lax.dynamic_update_slice_in_dim(new_weight, part_weight, index * size, 0)
            new_moment = lax.dynamic_update_slice_in_dim(new_moment, part_moment, index * size, 0)
        return new_weight[None, None], new_moment[None, None]

    new_weight_b, new_moment_b = finish(
        weight_out, moment_b[0, 0], hidden, upstream, 2, far_hidden, far_up,
        scale_out, pieces_out, size_out,
    )
    new_weight_a, new_moment_a = finish(
        weight_in, moment_a[0, 0], normed, grad_pre, 0, far_normed, far_pre,
        scale_in, pieces_in, size_in,
    )
    return (new_weight_a, new_weight_b, new_moment_a, new_moment_b)


def solution(mesh):
    placed = (
        P("replica", None, None, "shard"),
        P("replica", None, None, "shard"),
        P("replica", "section", None, "shard"),
        P("replica", "section", "shard", None),
        P("replica", "section", None, "shard"),
        P("replica", "section", "shard", None),
        P(),
        P(),
    )
    return jax.shard_map(
        per_device,
        mesh=mesh,
        in_specs=placed,
        out_specs=(
            P("replica", "section", None, "shard"),
            P("replica", "section", "shard", None),
            P("replica", "section", None, "shard"),
            P("replica", "section", "shard", None),
        ),
        check_vma=False,
    )
```

profile of v0, /device:TPU:0, one launch (start us, length us, event | category | flops | bytes accessed | tf_op | source)
XLA Modules:
  0.0 227.5 jit_solution(4169235641698082038)
XLA Ops:
  1.5 7.0 %collective-permute-start.2 = (bf16[128,256]{1,0:T(8,128)(2,1)S(1)}, bf16[128,256]{1,0:T(8,128)(2,1)S(1)}, u32[]{:S(2)}, u32[]{:S(2)}) collective-permute-start(bf16[128,256]{1,0:T(8,128)(2,1)S(1)} %select_bitcast_fusion.refs_1_.refs_3_), channel_id=1, source_target_pairs={{0,3},{1,2},{2,1},{3,0},{12,15},{13,14},{14,13},{15,12},{16,19},{1... | collective-permute-start | bytes 196616 | tf_op jit(solution)/shard_map/ppermute | solution.py:364
  8.5 1.9 collective-permute-start.1
  10.4 2.5 %collective-permute-start = (bf16[128,256]{1,0:T(8,128)(2,1)S(1)}, bf16[128,256]{1,0:T(8,128)(2,1)S(1)}, u32[]{:S(2)}, u32[]{:S(2)}) collective-permute-start(bf16[128,256]{1,0:T(8,128)(2,1)S(1)} %select_bitcast_fusion.refs_1_.refs_3_), channel_id=1, source_target_pairs={{0,1},{1,0},{2,3},{3,2},{12,13},{13,12},{14,15},{15,14},{16,17},{1... | collective-permute-start | bytes 196616 | tf_op jit(solution)/shard_map/ppermute | solution.py:364
  12.9 1.8 collective-permute-start.9
  21.1 1.8 collective-permute-start.8
  23.2 1.9 collective-permute-start.10
  28.0 2.2 shard_map.111
  32.1 3.9 %collective-permute-start.3 = (bf16[128,1024]{1,0:T(8,128)(2,1)S(1)}, bf16[128,1024]{1,0:T(8,128)(2,1)}, u32[]{:S(2)}, u32[]{:S(2)}) collective-permute-start(bf16[128,1024]{1,0:T(8,128)(2,1)S(1)} %get-tuple-element.81), channel_id=1, source_target_pairs={{0,1},{2,3},{16,17},{18,19}} | collective-permute-start | bytes 786440 | tf_op jit(solution)/shard_map/ppermute | solution.py:364
  37.7 1.4 collective-permute-done.3
  48.8 2.9 %collective-permute-done.8 = bf16[1024,768]{1,0:T(8,128)(2,1)} collective-permute-done((bf16[1024,768]{1,0:T(8,128)(2,1)}, bf16[1024,768]{1,0:T(8,128)(2,1)}, u32[]{:S(2)}, u32[]{:S(2)}) %collective-permute-start.8) | collective-permute-done | bytes 1572896 | tf_op jit(solution)/shard_map/ppermute | solution.py:364
  51.7 13.0 %collective-permute-start.20 = (bf16[768,1024]{1,0:T(8,128)(2,1)}, bf16[768,1024]{1,0:T(8,128)(2,1)}, u32[]{:S(2)}, u32[]{:S(2)}) collective-permute-start(bf16[768,1024]{1,0:T(8,128)(2,1)} %shard_map.113), channel_id=1, source_target_pairs={{8,24},{9,25},{10,26},{11,27},{12,28},{13,29},{14,30},{15,31},{24,... | collective-permute-start | bytes 4718600 | tf_op jit(solution)/shard_map/ppermute | solution.py:364
  64.7 1.4 copy-done.5
  72.2 3.8 %collective-permute-start.31 = (bf16[768,1024]{1,0:T(8,128)(2,1)}, bf16[768,1024]{1,0:T(8,128)(2,1)}, u32[]{:S(2)}, u32[]{:S(2)}) collective-permute-start(bf16[768,1024]{1,0:T(8,128)(2,1)} %shard_map.113), channel_id=1, source_target_pairs={{0,16},{1,17},{2,18},{3,19},{4,20},{5,21},{6,22},{7,23},{16,0},{17... | collective-permute-start | bytes 4718600 | tf_op jit(solution)/shard_map/ppermute | solution.py:364
  83.8 1.7 broadcast_select_fusion.1
  85.5 4.2 %collective-permute-done.19 = bf16[128,1024]{1,0:T(8,128)(2,1)} collective-permute-done((bf16[128,1024]{1,0:T(8,128)(2,1)}, bf16[128,1024]{1,0:T(8,128)(2,1)}, u32[]{:S(2)}, u32[]{:S(2)}) %collective-permute-start.19) | collective-permute-done | bytes 262176 | tf_op jit(solution)/shard_map/ppermute | solution.py:364
  104.9 1.7 broadcast_select_fusion.3
  129.0 68.2 %collective-permute-start.38 = (bf16[128,1024]{1,0:T(8,128)(2,1)S(1)}, bf16[128,1024]{1,0:T(8,128)(2,1)S(1)}, u32[]{:S(2)}, u32[]{:S(2)}) collective-permute-start(bf16[128,1024]{1,0:T(8,128)(2,1)S(1)} %fusion.28), channel_id=1, source_target_pairs={{1,0},{3,2},{4,5},{6,7},{8,9},{10,11},{13,12},{15,14},{17,16},{19,... | collective-permute-start | bytes 786440 | tf_op jit(solution)/shard_map/ppermute | solution.py:364
  197.2 1.6 broadcast_select_fusion
  198.8 5.2 %collective-permute-done.38 = bf16[128,1024]{1,0:T(8,128)(2,1)S(1)} collective-permute-done((bf16[128,1024]{1,0:T(8,128)(2,1)S(1)}, bf16[128,1024]{1,0:T(8,128)(2,1)S(1)}, u32[]{:S(2)}, u32[]{:S(2)}) %collective-permute-start.38) | collective-permute-done | bytes 262176 | tf_op jit(solution)/shard_map/ppermute | solution.py:364
  204.1 4.6 %collective-permute-start.40 = (bf16[128,1024]{1,0:T(8,128)(2,1)S(1)}, bf16[128,1024]{1,0:T(8,128)(2,1)S(1)}, u32[]{:S(2)}, u32[]{:S(2)}) collective-permute-start(bf16[128,1024]{1,0:T(8,128)(2,1)S(1)} %broadcast_select_fusion.4.refs_0_), channel_id=1, source_target_pairs={{0,16},{1,17},{2,18},{3,19},{4,20},{5,21},{6,22},{7,23},{8,24},{9,... | collective-permute-start | bytes 786440 | tf_op jit(solution)/shard_map/ppermute | solution.py:364
  211.1 1.7 collective-permute-start.39
  214.5 6.7 %collective-permute-done.39 = bf16[128,768]{1,0:T(8,128)(2,1)S(1)} collective-permute-done((bf16[128,768]{1,0:T(8,128)(2,1)S(1)}, bf16[128,768]{1,0:T(8,128)(2,1)S(1)}, u32[]{:S(2)}, u32[]{:S(2)}) %collective-permute-start.39) | collective-permute-done | bytes 196640 | tf_op jit(solution)/shard_map/ppermute | solution.py:364
  221.2 2.5 %fusion.27 = (bf16[1,1,1024,768]{3,2,1,0:T(8,128)(2,1)S(1)}, bf16[1,1,1024,768]{3,2,1,0:T(8,128)(2,1)S(1)}) fusion(bf16[1,1,1024,768]{3,2,1,0:T(8,128)(2,1)S(1)} %get-tuple-element.166, s32[]{:T(128)S(6)} %select_n.152, bf16[1024,768]{1,0:T(8,128)(2,1)} %collective-permute-done.8, bf16[1,1,1024,768]{3,2,1,0:T(8,128)(2,1)S(1)} %copy-done.13, ...), kind=kOutput, calls=%fused_computation.44 | convolution fusion | flops 108920832 | bytes 5832708 | tf_op jit(solution)/shard_map/dot_general | solution.py:22
  223.7 2.1 fusion.25
  (222 shorter events, 77.7 us)
Async XLA Ops:
  1.5 21.7 %collective-permute-start.2 = (bf16[128,256]{1,0:T(8,128)(2,1)S(1)}, bf16[128,256]{1,0:T(8,128)(2,1)S(1)}, u32[]{:S(2)}, u32[]{:S(2)}) collective-permute-start(bf16[128,256]{1,0:T(8,128)(2,1)S(1)} %select_bitcast_fusion.refs_1_.refs_3_), channel_id=1, source_target_pairs={{0,3},{1,2},{2,1},{3,0},{12,15},{13,14},{14,13},{15,12},{16,19},{1... | collective-permute-start | bytes 196616 | tf_op jit(solution)/shard_map/ppermute | solution.py:364
  8.5 16.6 %collective-permute-start.1 = (bf16[128,256]{1,0:T(8,128)(2,1)S(1)}, bf16[128,256]{1,0:T(8,128)(2,1)S(1)}, u32[]{:S(2)}, u32[]{:S(2)}) collective-permute-start(bf16[128,256]{1,0:T(8,128)(2,1)S(1)} %select_bitcast_fusion.refs_1_.refs_3_), channel_id=1, source_target_pairs={{0,2},{1,3},{2,0},{3,1},{12,14},{13,15},{14,12},{15,13},{16,18},{1... | collective-permute-start | bytes 196616 | tf_op jit(solution)/shard_map/ppermute | solution.py:364
  10.4 15.3 %collective-permute-start = (bf16[128,256]{1,0:T(8,128)(2,1)S(1)}, bf16[128,256]{1,0:T(8,128)(2,1)S(1)}, u32[]{:S(2)}, u32[]{:S(2)}) collective-permute-start(bf16[128,256]{1,0:T(8,128)(2,1)S(1)} %select_bitcast_fusion.refs_1_.refs_3_), channel_id=1, source_target_pairs={{0,1},{1,0},{2,3},{3,2},{12,13},{13,12},{14,15},{15,14},{16,17},{1... | collective-permute-start | bytes 196616 | tf_op jit(solution)/shard_map/ppermute | solution.py:364
  12.9 51.8 %collective-permute-start.9 = (bf16[1024,768]{1,0:T(8,128)(2,1)}, bf16[1024,768]{1,0:T(8,128)(2,1)}, u32[]{:S(2)}, u32[]{:S(2)}) collective-permute-start(bf16[1024,768]{1,0:T(8,128)(2,1)} %bitcast.73), channel_id=1, source_target_pairs={{5,4},{7,6},{9,8},{11,10},{12,13},{14,15},{21,20},{23,22},{25,24},... | collective-permute-start | bytes 4718600 | tf_op jit(solution)/shard_map/ppermute | solution.py:364
  21.1 30.7 %collective-permute-start.8 = (bf16[1024,768]{1,0:T(8,128)(2,1)}, bf16[1024,768]{1,0:T(8,128)(2,1)}, u32[]{:S(2)}, u32[]{:S(2)}) collective-permute-start(bf16[1024,768]{1,0:T(8,128)(2,1)} %shard_map.112), channel_id=1, source_target_pairs={{0,16},{1,17},{2,18},{3,19},{4,20},{5,21},{6,22},{7,23},{8,24},{9,... | collective-permute-start | bytes 4718600 | tf_op jit(solution)/shard_map/ppermute | solution.py:364
  23.2 41.5 %collective-permute-start.10 = (bf16[768,1024]{1,0:T(8,128)(2,1)S(1)}, bf16[768,1024]{1,0:T(8,128)(2,1)}, u32[]{:S(2)}, u32[]{:S(2)}) collective-permute-start(bf16[768,1024]{1,0:T(8,128)(2,1)S(1)} %bitcast.83), channel_id=1, source_target_pairs={{5,4},{7,6},{9,8},{11,10},{12,13},{14,15},{21,20},{23,22},{25,24},... | collective-permute-start | bytes 4718600 | tf_op jit(solution)/shard_map/ppermute | solution.py:364
  32.1 7.0 %collective-permute-start.3 = (bf16[128,1024]{1,0:T(8,128)(2,1)S(1)}, bf16[128,1024]{1,0:T(8,128)(2,1)}, u32[]{:S(2)}, u32[]{:S(2)}) collective-permute-start(bf16[128,1024]{1,0:T(8,128)(2,1)S(1)} %get-tuple-element.81), channel_id=1, source_target_pairs={{0,1},{2,3},{16,17},{18,19}} | collective-permute-start | bytes 786440 | tf_op jit(solution)/shard_map/ppermute | solution.py:364
  42.2 6.6 %collective-permute-start.5 = (bf16[64,1024]{1,0:T(8,128)(2,1)}, bf16[64,1024]{1,0:T(8,128)(2,1)}, u32[]{:S(2)}, u32[]{:S(2)}) collective-permute-start(bf16[64,1024]{1,0:T(8,128)(2,1)} %get-tuple-element.169), channel_id=1, source_target_pairs={{1,6},{3,4},{17,22},{19,20}} | collective-permute-start | bytes 393224 | tf_op jit(solution)/shard_map/ppermute | solution.py:364
  43.5 5.2 %collective-permute-start.4 = (bf16[64,1024]{1,0:T(8,128)(2,1)}, bf16[64,1024]{1,0:T(8,128)(2,1)}, u32[]{:S(2)}, u32[]{:S(2)}) collective-permute-start(bf16[64,1024]{1,0:T(8,128)(2,1)} %get-tuple-element.169), channel_id=1, source_target_pairs={{1,4},{3,6},{17,20},{19,22}} | collective-permute-start | bytes 393224 | tf_op jit(solution)/shard_map/ppermute | solution.py:364
  51.7 38.0 %collective-permute-start.20 = (bf16[768,1024]{1,0:T(8,128)(2,1)}, bf16[768,1024]{1,0:T(8,128)(2,1)}, u32[]{:S(2)}, u32[]{:S(2)}) collective-permute-start(bf16[768,1024]{1,0:T(8,128)(2,1)} %shard_map.113), channel_id=1, source_target_pairs={{8,24},{9,25},{10,26},{11,27},{12,28},{13,29},{14,30},{15,31},{24,... | collective-permute-start | bytes 4718600 | tf_op jit(solution)/shard_map/ppermute | solution.py:364
  68.7 3.5 %collective-permute-start.12 = (bf16[64,1024]{1,0:T(8,128)(2,1)S(1)}, bf16[64,1024]{1,0:T(8,128)(2,1)S(1)}, u32[]{:S(2)}, u32[]{:S(2)}) collective-permute-start(bf16[64,1024]{1,0:T(8,128)(2,1)S(1)} %get-tuple-element.89), channel_id=1, source_target_pairs={{4,10},{6,8},{20,26},{22,24}} | collective-permute-start | bytes 393224 | tf_op jit(solution)/shard_map/ppermute | solution.py:364
  72.2 40.4 %collective-permute-start.31 = (bf16[768,1024]{1,0:T(8,128)(2,1)}, bf16[768,1024]{1,0:T(8,128)(2,1)}, u32[]{:S(2)}, u32[]{:S(2)}) collective-permute-start(bf16[768,1024]{1,0:T(8,128)(2,1)} %shard_map.113), channel_id=1, source_target_pairs={{0,16},{1,17},{2,18},{3,19},{4,20},{5,21},{6,22},{7,23},{16,0},{17... | collective-permute-start | bytes 4718600 | tf_op jit(solution)/shard_map/ppermute | solution.py:364
  78.6 3.9 %collective-permute-start.16 = (bf16[64,1024]{1,0:T(8,128)(2,1)}, bf16[64,1024]{1,0:T(8,128)(2,1)}, u32[]{:S(2)}, u32[]{:S(2)}) collective-permute-start(bf16[64,1024]{1,0:T(8,128)(2,1)} %get-tuple-element.103), channel_id=1, source_target_pairs={{8,15},{10,13},{24,31},{26,29}} | collective-permute-start | bytes 393224 | tf_op jit(solution)/shard_map/ppermute | solution.py:364
  81.2 8.6 %collective-permute-start.19 = (bf16[128,1024]{1,0:T(8,128)(2,1)}, bf16[128,1024]{1,0:T(8,128)(2,1)}, u32[]{:S(2)}, u32[]{:S(2)}) collective-permute-start(bf16[128,1024]{1,0:T(8,128)(2,1)} %broadcast_select_fusion.2), channel_id=1, source_target_pairs={{1,0},{3,2},{4,5},{6,7},{17,16},{19,18},{20,21},{22,23}} | collective-permute-start | bytes 786440 | tf_op jit(solution)/shard_map/ppermute | solution.py:364
  95.8 8.4 %collective-permute-start.26 = (bf16[128,1024]{1,0:T(8,128)(2,1)}, bf16[128,1024]{1,0:T(8,128)(2,1)}, u32[]{:S(2)}, u32[]{:S(2)}) collective-permute-start(bf16[128,1024]{1,0:T(8,128)(2,1)} %broadcast_select_fusion.1), channel_id=1, source_target_pairs={{8,9},{10,11},{24,25},{26,27}} | collective-permute-start | bytes 786440 | tf_op jit(solution)/shard_map/ppermute | solution.py:364
  102.2 4.4 %collective-permute-start.23 = (bf16[64,1024]{1,0:T(8,128)(2,1)S(1)}, bf16[64,1024]{1,0:T(8,128)(2,1)S(1)}, u32[]{:S(2)}, u32[]{:S(2)}) collective-permute-start(bf16[64,1024]{1,0:T(8,128)(2,1)S(1)} %get-tuple-element.119), channel_id=1, source_target_pairs={{13,10},{15,8},{29,26},{31,24}} | collective-permute-start | bytes 393224 | tf_op jit(solution)/shard_map/ppermute | solution.py:364
  102.9 3.7 %collective-permute-start.22 = (bf16[64,1024]{1,0:T(8,128)(2,1)S(1)}, bf16[64,1024]{1,0:T(8,128)(2,1)S(1)}, u32[]{:S(2)}, u32[]{:S(2)}) collective-permute-start(bf16[64,1024]{1,0:T(8,128)(2,1)S(1)} %get-tuple-element.119), channel_id=1, source_target_pairs={{13,8},{15,10},{29,24},{31,26}} | collective-permute-start | bytes 393224 | tf_op jit(solution)/shard_map/ppermute | solution.py:364
  106.6 9.3 %collective-permute-start.32 = (bf16[128,1024]{1,0:T(8,128)(2,1)}, bf16[128,1024]{1,0:T(8,128)(2,1)}, u32[]{:S(2)}, u32[]{:S(2)}) collective-permute-start(bf16[128,1024]{1,0:T(8,128)(2,1)} %broadcast_select_fusion.3), channel_id=1, source_target_pairs={{13,12},{15,14},{29,28},{31,30}} | collective-permute-start | bytes 786440 | tf_op jit(solution)/shard_map/ppermute | solution.py:364
  118.8 6.9 %collective-permute-start.37 = (bf16[128,896]{1,0:T(8,128)(2,1)}, bf16[128,896]{1,0:T(8,128)(2,1)}, u32[]{:S(2)}, u32[]{:S(2)}) collective-permute-start(bf16[128,896]{1,0:T(8,128)(2,1)} %pad_maximum_fusion), channel_id=1, source_target_pairs={{0,16},{1,17},{2,18},{3,19},{4,20},{5,21},{6,22},{7,23},{8,24},{9,... | collective-permute-start | bytes 688136 | tf_op jit(solution)/shard_map/ppermute | solution.py:364
  120.5 5.2 %collective-permute-start.34 = (bf16[64,1024]{1,0:T(8,128)(2,1)}, bf16[64,1024]{1,0:T(8,128)(2,1)}, u32[]{:S(2)}, u32[]{:S(2)}) collective-permute-start(bf16[64,1024]{1,0:T(8,128)(2,1)} %get-tuple-element.143), channel_id=1, source_target_pairs={{4,3},{6,1},{20,19},{22,17}} | collective-permute-start | bytes 393224 | tf_op jit(solution)/shard_map/ppermute | solution.py:364
  121.8 3.9 %collective-permute-start.33 = (bf16[64,1024]{1,0:T(8,128)(2,1)}, bf16[64,1024]{1,0:T(8,128)(2,1)}, u32[]{:S(2)}, u32[]{:S(2)}) collective-permute-start(bf16[64,1024]{1,0:T(8,128)(2,1)} %get-tuple-element.143), channel_id=1, source_target_pairs={{4,1},{6,3},{20,17},{22,19}} | collective-permute-start | bytes 393224 | tf_op jit(solution)/shard_map/ppermute | solution.py:364
  129.0 75.1 %collective-permute-start.38 = (bf16[128,1024]{1,0:T(8,128)(2,1)S(1)}, bf16[128,1024]{1,0:T(8,128)(2,1)S(1)}, u32[]{:S(2)}, u32[]{:S(2)}) collective-permute-start(bf16[128,1024]{1,0:T(8,128)(2,1)S(1)} %fusion.28), channel_id=1, source_target_pairs={{1,0},{3,2},{4,5},{6,7},{8,9},{10,11},{13,12},{15,14},{17,16},{19,... | collective-permute-start | bytes 786440 | tf_op jit(solution)/shard_map/ppermute | solution.py:364
  204.1 19.6 %collective-permute-start.40 = (bf16[128,1024]{1,0:T(8,128)(2,1)S(1)}, bf16[128,1024]{1,0:T(8,128)(2,1)S(1)}, u32[]{:S(2)}, u32[]{:S(2)}) collective-permute-start(bf16[128,1024]{1,0:T(8,128)(2,1)S(1)} %broadcast_select_fusion.4.refs_0_), channel_id=1, source_target_pairs={{0,16},{1,17},{2,18},{3,19},{4,20},{5,21},{6,22},{7,23},{8,24},{9,... | collective-permute-start | bytes 786440 | tf_op jit(solution)/shard_map/ppermute | solution.py:364
  211.1 10.1 %collective-permute-start.39 = (bf16[128,768]{1,0:T(8,128)(2,1)S(1)}, bf16[128,768]{1,0:T(8,128)(2,1)S(1)}, u32[]{:S(2)}, u32[]{:S(2)}) collective-permute-start(bf16[128,768]{1,0:T(8,128)(2,1)S(1)} %shard_map.121), channel_id=1, source_target_pairs={{0,16},{1,17},{2,18},{3,19},{4,20},{5,21},{6,22},{7,23},{8,24},{9,... | collective-permute-start | bytes 589832 | tf_op jit(solution)/shard_map/ppermute | solution.py:364
  (74 other events, 264.9 us)
where the time goes:
time: 229 us; the launch traced here: 227 us
  starting transfers between devices  139 us (61%)
  local copies, waits for them, and re-layouts  32.5 us (14%)
  waiting for transfers between devices  20.6 us (9%)
  other arithmetic  12.3 us (5%)
  Pallas kernels  11 us (5%)
  matrix products  7.76 us (3%)
  between operations  4.06 us (2%)
    ppermute x41, starting transfers between devices, move(): return lax.ppermute(array, axes, pairs)  139 us
    unnamed x114, local copies, waits for them, and re-layouts  28.2 us
    ppermute x41, waiting for transfers between devices, move(): return lax.ppermute(array, axes, pairs)  20.6 us
    dot_general x6, matrix products, dot(): lax.dot_general(left, right, dims, preferred_element_type=jnp.float32)  7.76 us
    pallas_call x7, Pallas kernels, chain_step(): pl.pallas_call(functools.partial(chain_kernel, sz, step, forward, (len(re...  6.95 us
  transfers between devices with their start and end apart: 41, of which 5 were waited for; matrix products, arithmetic and copies ran while one was open for 7% of the time, Pallas kernels for 5%

commit v1 on v0

--- a/solution.py
+++ b/solution.py
@@ -62,7 +62,7 @@
             pltpu.SemaphoreType.DMA((len(arrays),)),
             pltpu.SemaphoreType.DMA((len(arrays),)),
         ],
-        compiler_params=pltpu.CompilerParams(vmem_limit_bytes=16 * 1024 * 1024),
+        compiler_params=pltpu.CompilerParams(vmem_limit_bytes=62 * 1024 * 1024),
         cost_estimate=pl.CostEstimate(
             flops=0, bytes_accessed=4 * shape[0] * shape[1], transcendentals=0
         ),
@@ -225,7 +225,7 @@
     anywhere = pl.BlockSpec(memory_space=pl.ANY)
     operands = [table, *received, *edges, *(weights[:2] if first else [*weights, state])]
     block = jax.ShapeDtypeStruct((sz.row_count // count, sz.width), jnp.bfloat16)
-    kept = jax.ShapeDtypeStruct((2 * sz.row_count, 2 * sz.local_hidden), jnp.float32)
+    kept = jax.ShapeDtypeStruct((4 * sz.row_count, 2 * sz.local_hidden), jnp.float32)
     fresh = jax.ShapeDtypeStruct((sz.row_count, sz.width), jnp.bfloat16)
     shapes = [block] * count + [fresh, kept]
     in_hbm = pl.BlockSpec(memory_space=pltpu.HBM)
@@ -256,7 +256,7 @@
             pltpu.SemaphoreType.DMA((count,)),
             pltpu.SemaphoreType.DMA((3,)),
         ],
-        compiler_params=pltpu.CompilerParams(vmem_limit_bytes=32 * 1024 * 1024),
+        compiler_params=pltpu.CompilerParams(vmem_limit_bytes=62 * 1024 * 1024),
         cost_estimate=pl.CostEstimate(
             flops=8 * sz.row_count * sz.width * sz.local_hidden,
             bytes_accessed=8 * sz.width * sz.local_hidden,
@@ -313,7 +313,7 @@
             pltpu.VMEM(weight.shape, jnp.bfloat16),
             pltpu.SemaphoreType.DMA,
         ],
-        compiler_params=pltpu.CompilerParams(vmem_limit_bytes=24 * 1024 * 1024),
+        compiler_params=pltpu.CompilerParams(vmem_limit_bytes=62 * 1024 * 1024),
         cost_estimate=pl.CostEstimate(
             flops=2 * rows_count * sz.width * hidden_size,
             bytes_accessed=2 * sz.width * hidden_size,

time: 229 us -> 225 us (0.983)
  local copies, waits for them, and re-layouts: 32.5 us -> 9.24 us
  Pallas kernels: 11 us -> 22 us
  matrix products: 7.76 us -> 12.3 us
  waiting for transfers between devices: 20.6 us -> 23.8 us
    unnamed x114 -> x92, local copies, waits for them, and re-layouts: 28.2 us -> 5.91 us
    pallas_call x2, Pallas kernels: 1.47 us -> 7.53 us  [share_call(): pl.pallas_call(functools.partial(share_kernel, sz, whole), out_shape=shap...]
    dot_general x6, matrix products: 7.76 us -> 12.3 us  [dot(): lax.dot_general(left, right, dims, preferred_element_type=jnp.float32)]
    ppermute x41, waiting for transfers between devices: 20.6 us -> 23.8 us  [move(): return lax.ppermute(array, axes, pairs)]
    dynamic_update_slice x3, local copies, waits for them, and re-layouts: 2.89 us -> 0.06 us  [per_device(): lax.dynamic_update_slice_in_dim(half, received[2 * e + a], slots[0, e] *...]
    pallas_call x7, Pallas kernels: 6.95 us -> 9.73 us  [chain_step(): pl.pallas_call(functools.partial(chain_kernel, sz, step, forward, (len(re...]
  transfers between devices with their start and end apart: 41 -> 41, of which waited for: 5 -> 7; matrix products, arithmetic and copies ran while one was open for 7% -> 9% of each run, Pallas kernels for 5% -> 8%
where the time goes in v1:
time: 225 us; the launch traced here: 224 us
  starting transfers between devices  140 us (62%)
  waiting for transfers between devices  23.8 us (11%)
  Pallas kernels  22 us (10%)
  matrix products  12.3 us (5%)
  other arithmetic  12 us (5%)
  local copies, waits for them, and re-layouts  9.24 us (4%)
  between operations  4.4 us (2%)
    ppermute x41, starting transfers between devices, move(): return lax.ppermute(array, axes, pairs)  140 us
    ppermute x41, waiting for transfers between devices, move(): return lax.ppermute(array, axes, pairs)  23.8 us
    dot_general x6, matrix products, dot(): lax.dot_general(left, right, dims, preferred_element_type=jnp.float32)  12.3 us
    pallas_call x7, Pallas kernels, chain_step(): pl.pallas_call(functools.partial(chain_kernel, sz, step, forward, (len(re...  9.73 us
    pallas_call x2, Pallas kernels, share_call(): pl.pallas_call(functools.partial(share_kernel, sz, whole), out_shape=shap...  7.53 us
    unnamed x92, local copies, waits for them, and re-layouts  5.91 us
    pallas_call x2, Pallas kernels, pack(): pl.pallas_call(functools.partial(pack_kernel, size), out_shape=jax.ShapeD...  4.73 us
  transfers between devices with their start and end apart: 41, of which 7 were waited for; matrix products, arithmetic and copies ran while one was open for 9% of the time, Pallas kernels for 8%

profile of v1, /device:TPU:0, one launch (start us, length us, event | category | flops | bytes accessed | tf_op | source)
XLA Modules:
  0.0 223.8 jit_solution(4510509169378346883)
XLA Ops:
  1.5 7.0 %collective-permute-start.2 = (bf16[128,256]{1,0:T(8,128)(2,1)S(1)}, bf16[128,256]{1,0:T(8,128)(2,1)S(1)}, u32[]{:S(2)}, u32[]{:S(2)}) collective-permute-start(bf16[128,256]{1,0:T(8,128)(2,1)S(1)} %select_bitcast_fusion.refs_1_.refs_3_), channel_id=1, source_target_pairs={{0,3},{1,2},{2,1},{3,0},{12,15},{13,14},{14,13},{15,12},{16,19},{1... | collective-permute-start | bytes 196616 | tf_op jit(solution)/shard_map/ppermute | solution.py:364
  8.5 1.9 collective-permute-start.1
  10.4 2.5 %collective-permute-start = (bf16[128,256]{1,0:T(8,128)(2,1)S(1)}, bf16[128,256]{1,0:T(8,128)(2,1)S(1)}, u32[]{:S(2)}, u32[]{:S(2)}) collective-permute-start(bf16[128,256]{1,0:T(8,128)(2,1)S(1)} %select_bitcast_fusion.refs_1_.refs_3_), channel_id=1, source_target_pairs={{0,1},{1,0},{2,3},{3,2},{12,13},{13,12},{14,15},{15,14},{16,17},{1... | collective-permute-start | bytes 196616 | tf_op jit(solution)/shard_map/ppermute | solution.py:364
  17.0 2.4 %shard_map.112 = bf16[1024,768]{1,0:T(8,128)(2,1)} custom-call(s32[1]{0:T(128)} %bitcast.9.starts, bf16[1024,768]{1,0:T(8,128)(2,1)} %bitcast.74, bf16[1024,768]{1,0:T(8,128)(2,1)} %bitcast.93), custom_call_target="tpu_custom_call" | custom-call | bytes 3145728 | tf_op jit(solution)/shard_map/pallas_call | solution.py:55
  25.4 4.1 %shard_map.111 = (bf16[128,1024]{1,0:T(8,128)(2,1)}, bf16[128,1024]{1,0:T(8,128)(2,1)}, f32[512,1536]{1,0:T(8,128)}) custom-call(s32[6,5]{1,0:T(8,128)} %fusion.31.refs_0_, bf16[128,256]{1,0:T(8,128)(2,1)} %copy-done.15, bf16[128,256]{1,0:T(8,128)(2,1)} %copy-done.21, bf16[128,256]{1,0:T(8,128)(2,1)} %copy-done.20, bf16[128,256]{1,0:T(8,128)(2,1)} %copy-done.19, ...), custom_call_target="tpu_custom_call" | custom-call | flops 805306368 | bytes 6291456 | tf_op jit(solution)/shard_map/pallas_call | solution.py:236
  29.5 3.2 %collective-permute-start.3 = (bf16[128,1024]{1,0:T(8,128)(2,1)}, bf16[128,1024]{1,0:T(8,128)(2,1)S(1)}, u32[]{:S(2)}, u32[]{:S(2)}) collective-permute-start(bf16[128,1024]{1,0:T(8,128)(2,1)} %get-tuple-element.81), channel_id=1, source_target_pairs={{0,1},{2,3},{16,17},{18,19}} | collective-permute-start | bytes 786440 | tf_op jit(solution)/shard_map/ppermute | solution.py:364
  34.6 2.3 %collective-permute-done.3 = bf16[128,1024]{1,0:T(8,128)(2,1)S(1)} collective-permute-done((bf16[128,1024]{1,0:T(8,128)(2,1)}, bf16[128,1024]{1,0:T(8,128)(2,1)S(1)}, u32[]{:S(2)}, u32[]{:S(2)}) %collective-permute-start.3) | collective-permute-done | bytes 262176 | tf_op jit(solution)/shard_map/ppermute | solution.py:364
  43.4 2.3 %shard_map.113 = bf16[768,1024]{1,0:T(8,128)(2,1)} custom-call(s32[1]{0:T(128)} %bitcast.10.starts, bf16[768,1024]{1,0:T(8,128)(2,1)} %bitcast.84, bf16[768,1024]{1,0:T(8,128)(2,1)} %bitcast.94), custom_call_target="tpu_custom_call" | custom-call | bytes 3145728 | tf_op jit(solution)/shard_map/pallas_call | solution.py:55
  45.8 4.3 %collective-permute-done.8 = bf16[1024,768]{1,0:T(8,128)(2,1)} collective-permute-done((bf16[1024,768]{1,0:T(8,128)(2,1)}, bf16[1024,768]{1,0:T(8,128)(2,1)}, u32[]{:S(2)}, u32[]{:S(2)}) %collective-permute-start.8) | collective-permute-done | bytes 1572896 | tf_op jit(solution)/shard_map/ppermute | solution.py:364
  50.1 11.8 %collective-permute-start.20 = (bf16[768,1024]{1,0:T(8,128)(2,1)}, bf16[768,1024]{1,0:T(8,128)(2,1)}, u32[]{:S(2)}, u32[]{:S(2)}) collective-permute-start(bf16[768,1024]{1,0:T(8,128)(2,1)} %shard_map.113), channel_id=1, source_target_pairs={{8,24},{9,25},{10,26},{11,27},{12,28},{13,29},{14,30},{15,31},{24,... | collective-permute-start | bytes 4718600 | tf_op jit(solution)/shard_map/ppermute | solution.py:364
  67.2 3.8 %collective-permute-start.31 = (bf16[768,1024]{1,0:T(8,128)(2,1)}, bf16[768,1024]{1,0:T(8,128)(2,1)S(1)}, u32[]{:S(2)}, u32[]{:S(2)}) collective-permute-start(bf16[768,1024]{1,0:T(8,128)(2,1)} %shard_map.113), channel_id=1, source_target_pairs={{0,16},{1,17},{2,18},{3,19},{4,20},{5,21},{6,22},{7,23},{16,0},{17... | collective-permute-start | bytes 4718600 | tf_op jit(solution)/shard_map/ppermute | solution.py:364
  78.2 3.6 %collective-permute-done.19 = bf16[128,1024]{1,0:T(8,128)(2,1)} collective-permute-done((bf16[128,1024]{1,0:T(8,128)(2,1)}, bf16[128,1024]{1,0:T(8,128)(2,1)}, u32[]{:S(2)}, u32[]{:S(2)}) %collective-permute-start.19) | collective-permute-done | bytes 262176 | tf_op jit(solution)/shard_map/ppermute | solution.py:364
  95.9 5.2 %collective-permute-done.31 = bf16[768,1024]{1,0:T(8,128)(2,1)S(1)} collective-permute-done((bf16[768,1024]{1,0:T(8,128)(2,1)}, bf16[768,1024]{1,0:T(8,128)(2,1)S(1)}, u32[]{:S(2)}, u32[]{:S(2)}) %collective-permute-start.31) | collective-permute-done | bytes 1572896 | tf_op jit(solution)/shard_map/ppermute | solution.py:364
  104.5 3.6 %shard_map.119 = (bf16[128,1024]{1,0:T(8,128)(2,1)}, bf16[128,768]{1,0:T(8,128)(2,1)}, f32[128,768]{1,0:T(8,128)}) custom-call(bf16[128,1024]{1,0:T(8,128)(2,1)} %add_select_fusion.refs_0_, bf16[1024,768]{1,0:T(8,128)(2,1)} %bitcast.81), custom_call_target="tpu_custom_call" | custom-call | flops 201326592 | bytes 1572864 | tf_op jit(solution)/shard_map/pallas_call | solution.py:307
  110.7 2.1 collective-permute-start.37
  117.5 71.9 %collective-permute-start.38 = (bf16[128,1024]{1,0:T(8,128)(2,1)S(1)}, bf16[128,1024]{1,0:T(8,128)(2,1)S(1)}, u32[]{:S(2)}, u32[]{:S(2)}) collective-permute-start(bf16[128,1024]{1,0:T(8,128)(2,1)S(1)} %fusion.28), channel_id=1, source_target_pairs={{1,0},{3,2},{4,5},{6,7},{8,9},{10,11},{13,12},{15,14},{17,16},{19,... | collective-permute-start | bytes 786440 | tf_op jit(solution)/shard_map/ppermute | solution.py:364
  190.8 5.5 %collective-permute-done.38 = bf16[128,1024]{1,0:T(8,128)(2,1)S(1)} collective-permute-done((bf16[128,1024]{1,0:T(8,128)(2,1)S(1)}, bf16[128,1024]{1,0:T(8,128)(2,1)S(1)}, u32[]{:S(2)}, u32[]{:S(2)}) %collective-permute-start.38) | collective-permute-done | bytes 262176 | tf_op jit(solution)/shard_map/ppermute | solution.py:364
  196.3 4.6 %collective-permute-start.40 = (bf16[128,1024]{1,0:T(8,128)(2,1)S(1)}, bf16[128,1024]{1,0:T(8,128)(2,1)}, u32[]{:S(2)}, u32[]{:S(2)}) collective-permute-start(bf16[128,1024]{1,0:T(8,128)(2,1)S(1)} %broadcast_select_fusion.4.refs_0_), channel_id=1, source_target_pairs={{0,16},{1,17},{2,18},{3,19},{4,20},{5,21},{6,22},{7,23},{8,24},{9,... | collective-permute-start | bytes 786440 | tf_op jit(solution)/shard_map/ppermute | solution.py:364
  202.2 2.9 %fusion.9 = (bf16[1,1,768,1024]{3,2,1,0:T(8,128)(2,1)}, bf16[1,1,768,1024]{3,2,1,0:T(8,128)(2,1)}) fusion(bf16[1,1,768,1024]{3,2,1,0:T(8,128)(2,1)S(1)} %copy-done.7, bf16[1,1,768,1024]{3,2,1,0:T(8,128)(2,1)S(1)} %copy-done.3, bf16[128,768]{1,0:T(8,128)(2,1)S(1)} %copy-done.39, bf16[128,1024]{1,0:T(8,128)(2,1)S(1)} %broadcast_select_fusion.4.refs_0_), kind=kOutput, calls=%fused_computation.15 | convolution fusion | flops 211550208 | bytes 6750208 | tf_op jit(solution)/shard_map/dot_general | solution.py:22
  205.1 3.9 %shard_map.121 = bf16[128,768]{1,0:T(8,128)(2,1)} custom-call(bf16[128,1024]{1,0:T(8,128)(2,1)} %copy-done.5, f32[128,768]{1,0:T(8,128)} %get-tuple-element.153.refs_1_, bf16[768,1024]{1,0:T(8,128)(2,1)} %bitcast.91), custom_call_target="tpu_custom_call" | custom-call | flops 201326592 | bytes 1572864 | tf_op jit(solution)/shard_map/pallas_call | solution.py:307
  210.8 2.8 %fusion.8 = (bf16[1,1,1024,768]{3,2,1,0:T(8,128)(2,1)S(1)}, bf16[1,1,1024,768]{3,2,1,0:T(8,128)(2,1)S(1)}) fusion(bf16[1,1,1024,768]{3,2,1,0:T(8,128)(2,1)} %param.12, bf16[1,1,1024,768]{3,2,1,0:T(8,128)(2,1)S(1)} %copy-done.1, bf16[128,1024]{1,0:T(8,128)(2,1)} %get-tuple-element.137, bf16[128,768]{1,0:T(8,128)(2,1)} %shard_map.121), kind=kOutput, calls=%fused_computation.14 | convolution fusion | flops 211550208 | bytes 6750208 | tf_op jit(solution)/shard_map/dot_general | solution.py:22
  214.0 2.3 %collective-permute-done.39 = bf16[128,768]{1,0:T(8,128)(2,1)S(1)} collective-permute-done((bf16[128,768]{1,0:T(8,128)(2,1)}, bf16[128,768]{1,0:T(8,128)(2,1)S(1)}, u32[]{:S(2)}, u32[]{:S(2)}) %collective-permute-start.39) | collective-permute-done | bytes 196640 | tf_op jit(solution)/shard_map/ppermute | solution.py:364
  216.3 2.7 %fusion.27 = (bf16[1,1,1024,768]{3,2,1,0:T(8,128)(2,1)S(1)}, bf16[1,1,1024,768]{3,2,1,0:T(8,128)(2,1)S(1)}) fusion(bf16[1,1,1024,768]{3,2,1,0:T(8,128)(2,1)S(1)} %get-tuple-element.166, s32[]{:T(128)S(6)} %select_n.152, bf16[1024,768]{1,0:T(8,128)(2,1)} %collective-permute-done.8, bf16[1,1,1024,768]{3,2,1,0:T(8,128)(2,1)S(1)} %copy-done.6, ...), kind=kOutput, calls=%fused_computation.44 | convolution fusion | flops 108920832 | bytes 5832708 | tf_op jit(solution)/shard_map/dot_general | solution.py:22
  219.9 2.3 %fusion.25 = (bf16[1,1,768,1024]{3,2,1,0:T(8,128)(2,1)S(1)}, bf16[1,1,768,1024]{3,2,1,0:T(8,128)(2,1)S(1)}) fusion(bf16[1,1,768,1024]{3,2,1,0:T(8,128)(2,1)S(1)} %copy-done.40, s32[]{:T(128)S(6)} %select_n.153, bf16[768,1024]{1,0:T(8,128)(2,1)S(1)} %copy-done.9, bf16[1,1,768,1024]{3,2,1,0:T(8,128)(2,1)S(1)} %copy-done.8, ...), kind=kOutput, calls=%fused_computation.42 | convolution fusion | flops 108920832 | bytes 5865476 | tf_op jit(solution)/shard_map/dot_general | solution.py:22
  (200 shorter events, 60.5 us)
Async XLA Ops:
  1.5 20.1 %collective-permute-start.2 = (bf16[128,256]{1,0:T(8,128)(2,1)S(1)}, bf16[128,256]{1,0:T(8,128)(2,1)S(1)}, u32[]{:S(2)}, u32[]{:S(2)}) collective-permute-start(bf16[128,256]{1,0:T(8,128)(2,1)S(1)} %select_bitcast_fusion.refs_1_.refs_3_), channel_id=1, source_target_pairs={{0,3},{1,2},{2,1},{3,0},{12,15},{13,14},{14,13},{15,12},{16,19},{1... | collective-permute-start | bytes 196616 | tf_op jit(solution)/shard_map/ppermute | solution.py:364
  8.5 15.6 %collective-permute-start.1 = (bf16[128,256]{1,0:T(8,128)(2,1)S(1)}, bf16[128,256]{1,0:T(8,128)(2,1)S(1)}, u32[]{:S(2)}, u32[]{:S(2)}) collective-permute-start(bf16[128,256]{1,0:T(8,128)(2,1)S(1)} %select_bitcast_fusion.refs_1_.refs_3_), channel_id=1, source_target_pairs={{0,2},{1,3},{2,0},{3,1},{12,14},{13,15},{14,12},{15,13},{16,18},{1... | collective-permute-start | bytes 196616 | tf_op jit(solution)/shard_map/ppermute | solution.py:364
  10.4 13.7 %collective-permute-start = (bf16[128,256]{1,0:T(8,128)(2,1)S(1)}, bf16[128,256]{1,0:T(8,128)(2,1)S(1)}, u32[]{:S(2)}, u32[]{:S(2)}) collective-permute-start(bf16[128,256]{1,0:T(8,128)(2,1)S(1)} %select_bitcast_fusion.refs_1_.refs_3_), channel_id=1, source_target_pairs={{0,1},{1,0},{2,3},{3,2},{12,13},{13,12},{14,15},{15,14},{16,17},{1... | collective-permute-start | bytes 196616 | tf_op jit(solution)/shard_map/ppermute | solution.py:364
  12.9 49.0 %collective-permute-start.9 = (bf16[1024,768]{1,0:T(8,128)(2,1)}, bf16[1024,768]{1,0:T(8,128)(2,1)}, u32[]{:S(2)}, u32[]{:S(2)}) collective-permute-start(bf16[1024,768]{1,0:T(8,128)(2,1)} %bitcast.73), channel_id=1, source_target_pairs={{5,4},{7,6},{9,8},{11,10},{12,13},{14,15},{21,20},{23,22},{25,24},... | collective-permute-start | bytes 4718600 | tf_op jit(solution)/shard_map/ppermute | solution.py:364
  19.4 30.6 %collective-permute-start.8 = (bf16[1024,768]{1,0:T(8,128)(2,1)}, bf16[1024,768]{1,0:T(8,128)(2,1)}, u32[]{:S(2)}, u32[]{:S(2)}) collective-permute-start(bf16[1024,768]{1,0:T(8,128)(2,1)} %shard_map.112), channel_id=1, source_target_pairs={{0,16},{1,17},{2,18},{3,19},{4,20},{5,21},{6,22},{7,23},{8,24},{9,... | collective-permute-start | bytes 4718600 | tf_op jit(solution)/shard_map/ppermute | solution.py:364
  21.6 40.3 %collective-permute-start.10 = (bf16[768,1024]{1,0:T(8,128)(2,1)S(1)}, bf16[768,1024]{1,0:T(8,128)(2,1)}, u32[]{:S(2)}, u32[]{:S(2)}) collective-permute-start(bf16[768,1024]{1,0:T(8,128)(2,1)S(1)} %bitcast.92), channel_id=1, source_target_pairs={{5,4},{7,6},{9,8},{11,10},{12,13},{14,15},{21,20},{23,22},{25,24},... | collective-permute-start | bytes 4718600 | tf_op jit(solution)/shard_map/ppermute | solution.py:364
  29.5 7.4 %collective-permute-start.3 = (bf16[128,1024]{1,0:T(8,128)(2,1)}, bf16[128,1024]{1,0:T(8,128)(2,1)S(1)}, u32[]{:S(2)}, u32[]{:S(2)}) collective-permute-start(bf16[128,1024]{1,0:T(8,128)(2,1)} %get-tuple-element.81), channel_id=1, source_target_pairs={{0,1},{2,3},{16,17},{18,19}} | collective-permute-start | bytes 786440 | tf_op jit(solution)/shard_map/ppermute | solution.py:364
  40.0 5.8 %collective-permute-start.5 = (bf16[64,1024]{1,0:T(8,128)(2,1)}, bf16[64,1024]{1,0:T(8,128)(2,1)S(1)}, u32[]{:S(2)}, u32[]{:S(2)}) collective-permute-start(bf16[64,1024]{1,0:T(8,128)(2,1)} %get-tuple-element.169), channel_id=1, source_target_pairs={{1,6},{3,4},{17,22},{19,20}} | collective-permute-start | bytes 393224 | tf_op jit(solution)/shard_map/ppermute | solution.py:364
  40.7 5.1 %collective-permute-start.4 = (bf16[64,1024]{1,0:T(8,128)(2,1)}, bf16[64,1024]{1,0:T(8,128)(2,1)}, u32[]{:S(2)}, u32[]{:S(2)}) collective-permute-start(bf16[64,1024]{1,0:T(8,128)(2,1)} %get-tuple-element.169), channel_id=1, source_target_pairs={{1,4},{3,6},{17,20},{19,22}} | collective-permute-start | bytes 393224 | tf_op jit(solution)/shard_map/ppermute | solution.py:364
  50.1 31.7 %collective-permute-start.20 = (bf16[768,1024]{1,0:T(8,128)(2,1)}, bf16[768,1024]{1,0:T(8,128)(2,1)}, u32[]{:S(2)}, u32[]{:S(2)}) collective-permute-start(bf16[768,1024]{1,0:T(8,128)(2,1)} %shard_map.113), channel_id=1, source_target_pairs={{8,24},{9,25},{10,26},{11,27},{12,28},{13,29},{14,30},{15,31},{24,... | collective-permute-start | bytes 4718600 | tf_op jit(solution)/shard_map/ppermute | solution.py:364
  63.0 4.1 %collective-permute-start.12 = (bf16[64,1024]{1,0:T(8,128)(2,1)}, bf16[64,1024]{1,0:T(8,128)(2,1)S(1)}, u32[]{:S(2)}, u32[]{:S(2)}) collective-permute-start(bf16[64,1024]{1,0:T(8,128)(2,1)} %get-tuple-element.89), channel_id=1, source_target_pairs={{4,10},{6,8},{20,26},{22,24}} | collective-permute-start | bytes 393224 | tf_op jit(solution)/shard_map/ppermute | solution.py:364
  67.2 34.0 %collective-permute-start.31 = (bf16[768,1024]{1,0:T(8,128)(2,1)}, bf16[768,1024]{1,0:T(8,128)(2,1)S(1)}, u32[]{:S(2)}, u32[]{:S(2)}) collective-permute-start(bf16[768,1024]{1,0:T(8,128)(2,1)} %shard_map.113), channel_id=1, source_target_pairs={{0,16},{1,17},{2,18},{3,19},{4,20},{5,21},{6,22},{7,23},{16,0},{17... | collective-permute-start | bytes 4718600 | tf_op jit(solution)/shard_map/ppermute | solution.py:364
  73.2 8.6 %collective-permute-start.19 = (bf16[128,1024]{1,0:T(8,128)(2,1)}, bf16[128,1024]{1,0:T(8,128)(2,1)}, u32[]{:S(2)}, u32[]{:S(2)}) collective-permute-start(bf16[128,1024]{1,0:T(8,128)(2,1)} %broadcast_select_fusion.2), channel_id=1, source_target_pairs={{1,0},{3,2},{4,5},{6,7},{17,16},{19,18},{20,21},{22,23}} | collective-permute-start | bytes 786440 | tf_op jit(solution)/shard_map/ppermute | solution.py:364
  74.6 3.6 %collective-permute-start.18 = (bf16[64,1024]{1,0:T(8,128)(2,1)}, bf16[64,1024]{1,0:T(8,128)(2,1)}, u32[]{:S(2)}, u32[]{:S(2)}) collective-permute-start(bf16[64,1024]{1,0:T(8,128)(2,1)} %get-tuple-element.104), channel_id=1, source_target_pairs={{8,31},{10,29},{24,15},{26,13}} | collective-permute-start | bytes 393224 | tf_op jit(solution)/shard_map/ppermute | solution.py:364
  84.1 4.3 %collective-permute-start.26 = (bf16[128,1024]{1,0:T(8,128)(2,1)S(1)}, bf16[128,1024]{1,0:T(8,128)(2,1)}, u32[]{:S(2)}, u32[]{:S(2)}) collective-permute-start(bf16[128,1024]{1,0:T(8,128)(2,1)S(1)} %broadcast_select_fusion.1), channel_id=1, source_target_pairs={{8,9},{10,11},{24,25},{26,27}} | collective-permute-start | bytes 786440 | tf_op jit(solution)/shard_map/ppermute | solution.py:364
  86.3 3.7 %collective-permute-start.23 = (bf16[64,1024]{1,0:T(8,128)(2,1)}, bf16[64,1024]{1,0:T(8,128)(2,1)S(1)}, u32[]{:S(2)}, u32[]{:S(2)}) collective-permute-start(bf16[64,1024]{1,0:T(8,128)(2,1)} %get-tuple-element.119), channel_id=1, source_target_pairs={{13,10},{15,8},{29,26},{31,24}} | collective-permute-start | bytes 393224 | tf_op jit(solution)/shard_map/ppermute | solution.py:364
  91.4 10.5 %collective-permute-start.32 = (bf16[128,1024]{1,0:T(8,128)(2,1)S(1)}, bf16[128,1024]{1,0:T(8,128)(2,1)}, u32[]{:S(2)}, u32[]{:S(2)}) collective-permute-start(bf16[128,1024]{1,0:T(8,128)(2,1)S(1)} %broadcast_select_fusion.3), channel_id=1, source_target_pairs={{13,12},{15,14},{29,28},{31,30}} | collective-permute-start | bytes 786440 | tf_op jit(solution)/shard_map/ppermute | solution.py:364
  93.8 7.9 %collective-permute-start.28 = (bf16[64,1024]{1,0:T(8,128)(2,1)}, bf16[64,1024]{1,0:T(8,128)(2,1)S(1)}, u32[]{:S(2)}, u32[]{:S(2)}) collective-permute-start(bf16[64,1024]{1,0:T(8,128)(2,1)} %get-tuple-element.128), channel_id=1, source_target_pairs={{8,6},{10,4},{24,22},{26,20}} | collective-permute-start | bytes 393224 | tf_op jit(solution)/shard_map/ppermute | solution.py:364
  94.5 7.3 %collective-permute-start.27 = (bf16[64,1024]{1,0:T(8,128)(2,1)}, bf16[64,1024]{1,0:T(8,128)(2,1)S(1)}, u32[]{:S(2)}, u32[]{:S(2)}) collective-permute-start(bf16[64,1024]{1,0:T(8,128)(2,1)} %get-tuple-element.128), channel_id=1, source_target_pairs={{8,4},{10,6},{24,20},{26,22}} | collective-permute-start | bytes 393224 | tf_op jit(solution)/shard_map/ppermute | solution.py:364
  95.2 6.6 %collective-permute-start.30 = (bf16[64,1024]{1,0:T(8,128)(2,1)}, bf16[64,1024]{1,0:T(8,128)(2,1)S(1)}, u32[]{:S(2)}, u32[]{:S(2)}) collective-permute-start(bf16[64,1024]{1,0:T(8,128)(2,1)} %get-tuple-element.129), channel_id=1, source_target_pairs={{8,22},{10,20},{24,6},{26,4}} | collective-permute-start | bytes 393224 | tf_op jit(solution)/shard_map/ppermute | solution.py:364
  110.7 6.4 %collective-permute-start.37 = (bf16[128,896]{1,0:T(8,128)(2,1)}, bf16[128,896]{1,0:T(8,128)(2,1)}, u32[]{:S(2)}, u32[]{:S(2)}) collective-permute-start(bf16[128,896]{1,0:T(8,128)(2,1)} %pad_maximum_fusion), channel_id=1, source_target_pairs={{0,16},{1,17},{2,18},{3,19},{4,20},{5,21},{6,22},{7,23},{8,24},{9,... | collective-permute-start | bytes 688136 | tf_op jit(solution)/shard_map/ppermute | solution.py:364
  117.5 78.7 %collective-permute-start.38 = (bf16[128,1024]{1,0:T(8,128)(2,1)S(1)}, bf16[128,1024]{1,0:T(8,128)(2,1)S(1)}, u32[]{:S(2)}, u32[]{:S(2)}) collective-permute-start(bf16[128,1024]{1,0:T(8,128)(2,1)S(1)} %fusion.28), channel_id=1, source_target_pairs={{1,0},{3,2},{4,5},{6,7},{8,9},{10,11},{13,12},{15,14},{17,16},{19,... | collective-permute-start | bytes 786440 | tf_op jit(solution)/shard_map/ppermute | solution.py:364
  196.3 22.7 %collective-permute-start.40 = (bf16[128,1024]{1,0:T(8,128)(2,1)S(1)}, bf16[128,1024]{1,0:T(8,128)(2,1)}, u32[]{:S(2)}, u32[]{:S(2)}) collective-permute-start(bf16[128,1024]{1,0:T(8,128)(2,1)S(1)} %broadcast_select_fusion.4.refs_0_), channel_id=1, source_target_pairs={{0,16},{1,17},{2,18},{3,19},{4,20},{5,21},{6,22},{7,23},{8,24},{9,... | collective-permute-start | bytes 786440 | tf_op jit(solution)/shard_map/ppermute | solution.py:364
  209.1 7.2 %collective-permute-start.39 = (bf16[128,768]{1,0:T(8,128)(2,1)}, bf16[128,768]{1,0:T(8,128)(2,1)S(1)}, u32[]{:S(2)}, u32[]{:S(2)}) collective-permute-start(bf16[128,768]{1,0:T(8,128)(2,1)} %shard_map.121), channel_id=1, source_target_pairs={{0,16},{1,17},{2,18},{3,19},{4,20},{5,21},{6,22},{7,23},{8,24},{9,... | collective-permute-start | bytes 589832 | tf_op jit(solution)/shard_map/ppermute | solution.py:364
  (63 other events, 340.6 us)

commit v2 on v0

--- a/solution.py
+++ b/solution.py
@@ -62,7 +62,7 @@
             pltpu.SemaphoreType.DMA((len(arrays),)),
             pltpu.SemaphoreType.DMA((len(arrays),)),
         ],
-        compiler_params=pltpu.CompilerParams(vmem_limit_bytes=16 * 1024 * 1024),
+        compiler_params=pltpu.CompilerParams(vmem_limit_bytes=32 * 1024 * 1024),
         cost_estimate=pl.CostEstimate(
             flops=0, bytes_accessed=4 * shape[0] * shape[1], transcendentals=0
         ),
@@ -93,7 +93,7 @@
     parts = 1 if first else 2
     (table,) = take(1)
     received, edges, sources = take(counts[0]), take(counts[1]), take(2 * parts)
-    take(0 if first else 1)
+    take(1)
     sends = take(counts[2])
     fresh_hbm, state = take(2)
     weights_in, weights_out, landing, rows, up, out, slope, wide_store = take(8)
@@ -223,15 +223,12 @@
     first = forward and step == 0
     count = 1 if forward and step in (0, sz.sections - 1) else sz.blocks
     anywhere = pl.BlockSpec(memory_space=pl.ANY)
-    operands = [table, *received, *edges, *(weights[:2] if first else [*weights, state])]
+    operands = [table, *received, *edges, *(weights[:2] if first else weights), state]
     block = jax.ShapeDtypeStruct((sz.row_count // count, sz.width), jnp.bfloat16)
-    kept = jax.ShapeDtypeStruct((2 * sz.row_count, 2 * sz.local_hidden), jnp.float32)
+    kept = jax.ShapeDtypeStruct(state.shape, state.dtype)
     fresh = jax.ShapeDtypeStruct((sz.row_count, sz.width), jnp.bfloat16)
     shapes = [block] * count + [fresh, kept]
-    in_hbm = pl.BlockSpec(memory_space=pltpu.HBM)
     in_specs = [pl.BlockSpec(memory_space=pltpu.SMEM)] + [anywhere] * (len(operands) - 1)
-    if not first:
-        in_specs[-1] = in_hbm
     whole = (sz.row_count, sz.width)
     results = pl.pallas_call(
         functools.partial(
@@ -239,8 +236,8 @@
         ),
         out_shape=shapes,
         in_specs=in_specs,
-        out_specs=[anywhere] * (count + 1) + [in_hbm],
-        input_output_aliases={} if first else {len(operands) - 1: count + 1},
+        out_specs=[anywhere] * len(shapes),
+        input_output_aliases={len(operands) - 1: count + 1},
         scratch_shapes=[
             pltpu.VMEM((2, sz.width, sz.local_hidden), jnp.bfloat16),
             pltpu.VMEM((2, sz.local_hidden, sz.width), jnp.bfloat16),
@@ -313,7 +310,7 @@
             pltpu.VMEM(weight.shape, jnp.bfloat16),
             pltpu.SemaphoreType.DMA,
         ],
-        compiler_params=pltpu.CompilerParams(vmem_limit_bytes=24 * 1024 * 1024),
+        compiler_params=pltpu.CompilerParams(vmem_limit_bytes=32 * 1024 * 1024),
         cost_estimate=pl.CostEstimate(
             flops=2 * rows_count * sz.width * hidden_size,
             bytes_accessed=2 * sz.width * hidden_size,
@@ -479,7 +476,8 @@
         return received
 
     weights = [weight_in, weight_out, *near]
-    received, state = [], None
+    state = jnp.zeros((5 * row_count, 2 * local_hidden), jnp.float32)
+    received = []
     for step in every:
         sends, fresh, state = chain_step(
             sz, step, True, table, received, edges if step == 0 else [], weights, state
@@ -521,6 +519,7 @@
                 (received, far_late, row_parts)
             )
 
+    upstream, rows, row_parts = lax.optimization_barrier((upstream, rows, row_parts))
     own_rows = jnp.where(is_holder, rows, sum(row_parts[1:], row_parts[0]))
     normed, hidden, slope = share_call(sz, [own_rows], weight_in)
 

time: 229 us -> 240 us (1.048)
  starting transfers between devices: 139 us -> 144 us
  local copies, waits for them, and re-layouts: 32.5 us -> 37.4 us
    ppermute x41, starting transfers between devices: 139 us -> 144 us  [move(): return lax.ppermute(array, axes, pairs)]
    unnamed x114 -> x82, local copies, waits for them, and re-layouts: 28.2 us -> 32.6 us
  transfers between devices with their start and end apart: 41 -> 41, of which waited for: 5 -> 5; matrix products, arithmetic and copies ran while one was open for 7% -> 6% of each run, Pallas kernels for 5% -> 4%
where the time goes in v2:
time: 240 us; the launch traced here: 238 us
  starting transfers between devices  144 us (60%)
  local copies, waits for them, and re-layouts  37.4 us (16%)
  waiting for transfers between devices  20.4 us (8%)
  other arithmetic  12.9 us (5%)
  Pallas kernels  11.6 us (5%)
  matrix products  7.75 us (3%)
  between operations  4.07 us (2%)
    ppermute x41, starting transfers between devices, move(): return lax.ppermute(array, axes, pairs)  144 us
    unnamed x82, local copies, waits for them, and re-layouts  32.6 us
    ppermute x41, waiting for transfers between devices, move(): return lax.ppermute(array, axes, pairs)  20.4 us
    dot_general x6, matrix products, dot(): lax.dot_general(left, right, dims, preferred_element_type=jnp.float32)  7.75 us
    pallas_call x7, Pallas kernels, chain_step(): pl.pallas_call(functools.partial(chain_kernel, sz, step, forward, (len(re...  7.52 us
  transfers between devices with their start and end apart: 41, of which 5 were waited for; matrix products, arithmetic and copies ran while one was open for 6% of the time, Pallas kernels for 4%

profile of v2, /device:TPU:0, one launch (start us, length us, event | category | flops | bytes accessed | tf_op | source)
XLA Modules:
  0.0 238.2 jit_solution(9459735111769710950)
XLA Ops:
  1.5 4.9 %collective-permute-start = (bf16[128,256]{1,0:T(8,128)(2,1)S(1)}, bf16[128,256]{1,0:T(8,128)(2,1)S(1)}, u32[]{:S(2)}, u32[]{:S(2)}) collective-permute-start(bf16[128,256]{1,0:T(8,128)(2,1)S(1)} %select_bitcast_fusion.refs_1_.refs_3_), channel_id=1, source_target_pairs={{0,1},{1,0},{2,3},{3,2},{12,13},{13,12},{14,15},{15,14},{16,17},{1... | collective-permute-start | bytes 196616 | tf_op jit(solution)/shard_map/ppermute | solution.py:361
  6.5 4.5 %collective-permute-start.1 = (bf16[128,256]{1,0:T(8,128)(2,1)S(1)}, bf16[128,256]{1,0:T(8,128)(2,1)S(1)}, u32[]{:S(2)}, u32[]{:S(2)}) collective-permute-start(bf16[128,256]{1,0:T(8,128)(2,1)S(1)} %select_bitcast_fusion.refs_1_.refs_3_), channel_id=1, source_target_pairs={{0,2},{1,3},{2,0},{3,1},{12,14},{13,15},{14,12},{15,13},{16,18},{1... | collective-permute-start | bytes 196616 | tf_op jit(solution)/shard_map/ppermute | solution.py:361
  11.0 1.9 collective-permute-start.2
  26.4 2.8 %shard_map.111 = (bf16[128,1024]{1,0:T(8,128)(2,1)}, bf16[128,1024]{1,0:T(8,128)(2,1)S(1)}, f32[640,1536]{1,0:T(8,128)S(1)}) custom-call(s32[6,5]{1,0:T(8,128)S(1)} %fusion.31.refs_0_, bf16[128,256]{1,0:T(8,128)(2,1)S(1)} %select_bitcast_fusion.refs_1_.refs_3_, ...), custom_call_target="tpu_custom_call", output_to_operand_aliasing={{2}: (7, {})} | custom-call | flops 805306368 | bytes 6291456 | tf_op jit(solution)/shard_map/pallas_call | solution.py:233
  29.3 1.9 copy-done.1
  31.9 3.3 %collective-permute-start.3 = (bf16[128,1024]{1,0:T(8,128)(2,1)}, bf16[128,1024]{1,0:T(8,128)(2,1)}, u32[]{:S(2)}, u32[]{:S(2)}) collective-permute-start(bf16[128,1024]{1,0:T(8,128)(2,1)} %get-tuple-element.86), channel_id=1, source_target_pairs={{0,1},{2,3},{16,17},{18,19}} | collective-permute-start | bytes 786440 | tf_op jit(solution)/shard_map/ppermute | solution.py:361
  49.0 15.7 %collective-permute-start.20 = (bf16[768,1024]{1,0:T(8,128)(2,1)}, bf16[768,1024]{1,0:T(8,128)(2,1)}, u32[]{:S(2)}, u32[]{:S(2)}) collective-permute-start(bf16[768,1024]{1,0:T(8,128)(2,1)} %shard_map.113), channel_id=1, source_target_pairs={{8,24},{9,25},{10,26},{11,27},{12,28},{13,29},{14,30},{15,31},{24,... | collective-permute-start | bytes 4718600 | tf_op jit(solution)/shard_map/ppermute | solution.py:361
  64.7 2.1 copy-done.2
  72.0 3.8 %collective-permute-start.31 = (bf16[768,1024]{1,0:T(8,128)(2,1)}, bf16[768,1024]{1,0:T(8,128)(2,1)}, u32[]{:S(2)}, u32[]{:S(2)}) collective-permute-start(bf16[768,1024]{1,0:T(8,128)(2,1)} %shard_map.113), channel_id=1, source_target_pairs={{0,16},{1,17},{2,18},{3,19},{4,20},{5,21},{6,22},{7,23},{16,0},{17... | collective-permute-start | bytes 4718600 | tf_op jit(solution)/shard_map/ppermute | solution.py:361
  76.6 1.9 copy-done.3
  86.2 4.2 %collective-permute-done.19 = bf16[128,1024]{1,0:T(8,128)(2,1)} collective-permute-done((bf16[128,1024]{1,0:T(8,128)(2,1)}, bf16[128,1024]{1,0:T(8,128)(2,1)}, u32[]{:S(2)}, u32[]{:S(2)}) %collective-permute-start.19) | collective-permute-done | bytes 262176 | tf_op jit(solution)/shard_map/ppermute | solution.py:361
  90.4 2.1 copy-done.4
  93.2 1.9 copy-done.5
  98.6 2.1 copy-done.6
  101.6 1.9 copy-done.7
  109.3 2.1 copy-done.8
  112.2 1.9 copy-done.9
  119.4 2.1 copy-done.10
  136.6 69.7 %collective-permute-start.38 = (bf16[128,1024]{1,0:T(8,128)(2,1)S(1)}, bf16[128,1024]{1,0:T(8,128)(2,1)S(1)}, u32[]{:S(2)}, u32[]{:S(2)}) collective-permute-start(bf16[128,1024]{1,0:T(8,128)(2,1)S(1)} %fusion.28), channel_id=1, source_target_pairs={{1,0},{3,2},{4,5},{6,7},{8,9},{10,11},{13,12},{15,14},{17,16},{19,... | collective-permute-start | bytes 786440 | tf_op jit(solution)/shard_map/ppermute | solution.py:361
  207.8 5.2 %collective-permute-done.38 = bf16[128,1024]{1,0:T(8,128)(2,1)S(1)} collective-permute-done((bf16[128,1024]{1,0:T(8,128)(2,1)S(1)}, bf16[128,1024]{1,0:T(8,128)(2,1)S(1)}, u32[]{:S(2)}, u32[]{:S(2)}) %collective-permute-start.38) | collective-permute-done | bytes 262176 | tf_op jit(solution)/shard_map/ppermute | solution.py:361
  214.8 4.6 %collective-permute-start.40 = (bf16[128,1024]{1,0:T(8,128)(2,1)S(1)}, bf16[128,1024]{1,0:T(8,128)(2,1)S(1)}, u32[]{:S(2)}, u32[]{:S(2)}) collective-permute-start(bf16[128,1024]{1,0:T(8,128)(2,1)S(1)} %broadcast_select_fusion.4.refs_0_), channel_id=1, source_target_pairs={{0,16},{1,17},{2,18},{3,19},{4,20},{5,21},{6,22},{7,23},{8,24},{9,... | collective-permute-start | bytes 786440 | tf_op jit(solution)/shard_map/ppermute | solution.py:361
  223.6 8.3 %collective-permute-done.39 = bf16[128,768]{1,0:T(8,128)(2,1)S(1)} collective-permute-done((bf16[128,768]{1,0:T(8,128)(2,1)S(1)}, bf16[128,768]{1,0:T(8,128)(2,1)S(1)}, u32[]{:S(2)}, u32[]{:S(2)}) %collective-permute-start.39) | collective-permute-done | bytes 196640 | tf_op jit(solution)/shard_map/ppermute | solution.py:361
  231.9 2.5 %fusion.27 = (bf16[1,1,1024,768]{3,2,1,0:T(8,128)(2,1)S(1)}, bf16[1,1,1024,768]{3,2,1,0:T(8,128)(2,1)S(1)}) fusion(bf16[1,1,1024,768]{3,2,1,0:T(8,128)(2,1)S(1)} %get-tuple-element.176, s32[]{:T(128)S(6)} %select_n.154, bf16[1024,768]{1,0:T(8,128)(2,1)} %collective-permute-done.8, bf16[1,1,1024,768]{3,2,1,0:T(8,128)(2,1)S(1)} %copy-done.15, ...), kind=kOutput, calls=%fused_computation.44 | convolution fusion | flops 108920832 | bytes 5832708 | tf_op jit(solution)/shard_map/dot_general | solution.py:22
  234.4 2.1 fusion.25
  (192 shorter events, 80.6 us)
Async XLA Ops:
  1.5 21.7 %collective-permute-start = (bf16[128,256]{1,0:T(8,128)(2,1)S(1)}, bf16[128,256]{1,0:T(8,128)(2,1)S(1)}, u32[]{:S(2)}, u32[]{:S(2)}) collective-permute-start(bf16[128,256]{1,0:T(8,128)(2,1)S(1)} %select_bitcast_fusion.refs_1_.refs_3_), channel_id=1, source_target_pairs={{0,1},{1,0},{2,3},{3,2},{12,13},{13,12},{14,15},{15,14},{16,17},{1... | collective-permute-start | bytes 196616 | tf_op jit(solution)/shard_map/ppermute | solution.py:361
  6.5 18.6 %collective-permute-start.1 = (bf16[128,256]{1,0:T(8,128)(2,1)S(1)}, bf16[128,256]{1,0:T(8,128)(2,1)S(1)}, u32[]{:S(2)}, u32[]{:S(2)}) collective-permute-start(bf16[128,256]{1,0:T(8,128)(2,1)S(1)} %select_bitcast_fusion.refs_1_.refs_3_), channel_id=1, source_target_pairs={{0,2},{1,3},{2,0},{3,1},{12,14},{13,15},{14,12},{15,13},{16,18},{1... | collective-permute-start | bytes 196616 | tf_op jit(solution)/shard_map/ppermute | solution.py:361
  11.0 14.1 %collective-permute-start.2 = (bf16[128,256]{1,0:T(8,128)(2,1)S(1)}, bf16[128,256]{1,0:T(8,128)(2,1)S(1)}, u32[]{:S(2)}, u32[]{:S(2)}) collective-permute-start(bf16[128,256]{1,0:T(8,128)(2,1)S(1)} %select_bitcast_fusion.refs_1_.refs_3_), channel_id=1, source_target_pairs={{0,3},{1,2},{2,1},{3,0},{12,15},{13,14},{14,13},{15,12},{16,19},{1... | collective-permute-start | bytes 196616 | tf_op jit(solution)/shard_map/ppermute | solution.py:361
  12.9 51.8 %collective-permute-start.9 = (bf16[1024,768]{1,0:T(8,128)(2,1)}, bf16[1024,768]{1,0:T(8,128)(2,1)}, u32[]{:S(2)}, u32[]{:S(2)}) collective-permute-start(bf16[1024,768]{1,0:T(8,128)(2,1)} %bitcast.83), channel_id=1, source_target_pairs={{5,4},{7,6},{9,8},{11,10},{12,13},{14,15},{21,20},{23,22},{25,24},... | collective-permute-start | bytes 4718600 | tf_op jit(solution)/shard_map/ppermute | solution.py:361
  21.0 28.0 %collective-permute-start.8 = (bf16[1024,768]{1,0:T(8,128)(2,1)}, bf16[1024,768]{1,0:T(8,128)(2,1)}, u32[]{:S(2)}, u32[]{:S(2)}) collective-permute-start(bf16[1024,768]{1,0:T(8,128)(2,1)} %shard_map.112), channel_id=1, source_target_pairs={{0,16},{1,17},{2,18},{3,19},{4,20},{5,21},{6,22},{7,23},{8,24},{9,... | collective-permute-start | bytes 4718600 | tf_op jit(solution)/shard_map/ppermute | solution.py:361
  23.2 41.5 %collective-permute-start.10 = (bf16[768,1024]{1,0:T(8,128)(2,1)S(1)}, bf16[768,1024]{1,0:T(8,128)(2,1)}, u32[]{:S(2)}, u32[]{:S(2)}) collective-permute-start(bf16[768,1024]{1,0:T(8,128)(2,1)S(1)} %bitcast.73), channel_id=1, source_target_pairs={{5,4},{7,6},{9,8},{11,10},{12,13},{14,15},{21,20},{23,22},{25,24},... | collective-permute-start | bytes 4718600 | tf_op jit(solution)/shard_map/ppermute | solution.py:361
  31.9 6.8 %collective-permute-start.3 = (bf16[128,1024]{1,0:T(8,128)(2,1)}, bf16[128,1024]{1,0:T(8,128)(2,1)}, u32[]{:S(2)}, u32[]{:S(2)}) collective-permute-start(bf16[128,1024]{1,0:T(8,128)(2,1)} %get-tuple-element.86), channel_id=1, source_target_pairs={{0,1},{2,3},{16,17},{18,19}} | collective-permute-start | bytes 786440 | tf_op jit(solution)/shard_map/ppermute | solution.py:361
  41.8 7.2 %collective-permute-start.6 = (bf16[64,1024]{1,0:T(8,128)(2,1)}, bf16[64,1024]{1,0:T(8,128)(2,1)}, u32[]{:S(2)}, u32[]{:S(2)}) collective-permute-start(bf16[64,1024]{1,0:T(8,128)(2,1)} %get-tuple-element.178), channel_id=1, source_target_pairs={{1,20},{3,22},{17,4},{19,6}} | collective-permute-start | bytes 393224 | tf_op jit(solution)/shard_map/ppermute | solution.py:361
  43.7 5.3 %collective-permute-start.7 = (bf16[64,1024]{1,0:T(8,128)(2,1)}, bf16[64,1024]{1,0:T(8,128)(2,1)}, u32[]{:S(2)}, u32[]{:S(2)}) collective-permute-start(bf16[64,1024]{1,0:T(8,128)(2,1)} %get-tuple-element.178), channel_id=1, source_target_pairs={{1,22},{3,20},{17,6},{19,4}} | collective-permute-start | bytes 393224 | tf_op jit(solution)/shard_map/ppermute | solution.py:361
  49.0 41.3 %collective-permute-start.20 = (bf16[768,1024]{1,0:T(8,128)(2,1)}, bf16[768,1024]{1,0:T(8,128)(2,1)}, u32[]{:S(2)}, u32[]{:S(2)}) collective-permute-start(bf16[768,1024]{1,0:T(8,128)(2,1)} %shard_map.113), channel_id=1, source_target_pairs={{8,24},{9,25},{10,26},{11,27},{12,28},{13,29},{14,30},{15,31},{24,... | collective-permute-start | bytes 4718600 | tf_op jit(solution)/shard_map/ppermute | solution.py:361
  72.0 46.0 %collective-permute-start.31 = (bf16[768,1024]{1,0:T(8,128)(2,1)}, bf16[768,1024]{1,0:T(8,128)(2,1)}, u32[]{:S(2)}, u32[]{:S(2)}) collective-permute-start(bf16[768,1024]{1,0:T(8,128)(2,1)} %shard_map.113), channel_id=1, source_target_pairs={{0,16},{1,17},{2,18},{3,19},{4,20},{5,21},{6,22},{7,23},{16,0},{17... | collective-permute-start | bytes 4718600 | tf_op jit(solution)/shard_map/ppermute | solution.py:361
  81.8 8.6 %collective-permute-start.19 = (bf16[128,1024]{1,0:T(8,128)(2,1)}, bf16[128,1024]{1,0:T(8,128)(2,1)}, u32[]{:S(2)}, u32[]{:S(2)}) collective-permute-start(bf16[128,1024]{1,0:T(8,128)(2,1)} %broadcast_select_fusion.3), channel_id=1, source_target_pairs={{1,0},{3,2},{4,5},{6,7},{17,16},{19,18},{20,21},{22,23}} | collective-permute-start | bytes 786440 | tf_op jit(solution)/shard_map/ppermute | solution.py:361
  97.2 8.3 %collective-permute-start.26 = (bf16[128,1024]{1,0:T(8,128)(2,1)}, bf16[128,1024]{1,0:T(8,128)(2,1)}, u32[]{:S(2)}, u32[]{:S(2)}) collective-permute-start(bf16[128,1024]{1,0:T(8,128)(2,1)} %broadcast_select_fusion.2), channel_id=1, source_target_pairs={{8,9},{10,11},{24,25},{26,27}} | collective-permute-start | bytes 786440 | tf_op jit(solution)/shard_map/ppermute | solution.py:361
  103.5 4.4 %collective-permute-start.22 = (bf16[64,1024]{1,0:T(8,128)(2,1)S(1)}, bf16[64,1024]{1,0:T(8,128)(2,1)S(1)}, u32[]{:S(2)}, u32[]{:S(2)}) collective-permute-start(bf16[64,1024]{1,0:T(8,128)(2,1)S(1)} %get-tuple-element.123), channel_id=1, source_target_pairs={{13,8},{15,10},{29,24},{31,26}} | collective-permute-start | bytes 393224 | tf_op jit(solution)/shard_map/ppermute | solution.py:361
  104.2 3.7 %collective-permute-start.23 = (bf16[64,1024]{1,0:T(8,128)(2,1)S(1)}, bf16[64,1024]{1,0:T(8,128)(2,1)S(1)}, u32[]{:S(2)}, u32[]{:S(2)}) collective-permute-start(bf16[64,1024]{1,0:T(8,128)(2,1)S(1)} %get-tuple-element.123), channel_id=1, source_target_pairs={{13,10},{15,8},{29,26},{31,24}} | collective-permute-start | bytes 393224 | tf_op jit(solution)/shard_map/ppermute | solution.py:361
  107.9 11.4 %collective-permute-start.32 = (bf16[128,1024]{1,0:T(8,128)(2,1)}, bf16[128,1024]{1,0:T(8,128)(2,1)}, u32[]{:S(2)}, u32[]{:S(2)}) collective-permute-start(bf16[128,1024]{1,0:T(8,128)(2,1)} %broadcast_select_fusion.1), channel_id=1, source_target_pairs={{13,12},{15,14},{29,28},{31,30}} | collective-permute-start | bytes 786440 | tf_op jit(solution)/shard_map/ppermute | solution.py:361
  114.1 5.2 %collective-permute-start.27 = (bf16[64,1024]{1,0:T(8,128)(2,1)}, bf16[64,1024]{1,0:T(8,128)(2,1)}, u32[]{:S(2)}, u32[]{:S(2)}) collective-permute-start(bf16[64,1024]{1,0:T(8,128)(2,1)} %get-tuple-element.133), channel_id=1, source_target_pairs={{8,4},{10,6},{24,20},{26,22}} | collective-permute-start | bytes 393224 | tf_op jit(solution)/shard_map/ppermute | solution.py:361
  115.4 3.9 %collective-permute-start.28 = (bf16[64,1024]{1,0:T(8,128)(2,1)}, bf16[64,1024]{1,0:T(8,128)(2,1)}, u32[]{:S(2)}, u32[]{:S(2)}) collective-permute-start(bf16[64,1024]{1,0:T(8,128)(2,1)} %get-tuple-element.133), channel_id=1, source_target_pairs={{8,6},{10,4},{24,22},{26,20}} | collective-permute-start | bytes 393224 | tf_op jit(solution)/shard_map/ppermute | solution.py:361
  127.2 6.3 %collective-permute-start.37 = (bf16[128,896]{1,0:T(8,128)(2,1)}, bf16[128,896]{1,0:T(8,128)(2,1)}, u32[]{:S(2)}, u32[]{:S(2)}) collective-permute-start(bf16[128,896]{1,0:T(8,128)(2,1)} %pad_maximum_fusion), channel_id=1, source_target_pairs={{0,16},{1,17},{2,18},{3,19},{4,20},{5,21},{6,22},{7,23},{8,24},{9,... | collective-permute-start | bytes 688136 | tf_op jit(solution)/shard_map/ppermute | solution.py:361
  127.3 5.2 %collective-permute-start.33 = (bf16[64,1024]{1,0:T(8,128)(2,1)}, bf16[64,1024]{1,0:T(8,128)(2,1)}, u32[]{:S(2)}, u32[]{:S(2)}) collective-permute-start(bf16[64,1024]{1,0:T(8,128)(2,1)} %get-tuple-element.155), channel_id=1, source_target_pairs={{4,1},{6,3},{20,17},{22,19}} | collective-permute-start | bytes 393224 | tf_op jit(solution)/shard_map/ppermute | solution.py:361
  128.6 3.9 %collective-permute-start.34 = (bf16[64,1024]{1,0:T(8,128)(2,1)}, bf16[64,1024]{1,0:T(8,128)(2,1)}, u32[]{:S(2)}, u32[]{:S(2)}) collective-permute-start(bf16[64,1024]{1,0:T(8,128)(2,1)} %get-tuple-element.155), channel_id=1, source_target_pairs={{4,3},{6,1},{20,19},{22,17}} | collective-permute-start | bytes 393224 | tf_op jit(solution)/shard_map/ppermute | solution.py:361
  136.6 76.5 %collective-permute-start.38 = (bf16[128,1024]{1,0:T(8,128)(2,1)S(1)}, bf16[128,1024]{1,0:T(8,128)(2,1)S(1)}, u32[]{:S(2)}, u32[]{:S(2)}) collective-permute-start(bf16[128,1024]{1,0:T(8,128)(2,1)S(1)} %fusion.28), channel_id=1, source_target_pairs={{1,0},{3,2},{4,5},{6,7},{8,9},{10,11},{13,12},{15,14},{17,16},{19,... | collective-permute-start | bytes 786440 | tf_op jit(solution)/shard_map/ppermute | solution.py:361
  214.8 19.6 %collective-permute-start.40 = (bf16[128,1024]{1,0:T(8,128)(2,1)S(1)}, bf16[128,1024]{1,0:T(8,128)(2,1)S(1)}, u32[]{:S(2)}, u32[]{:S(2)}) collective-permute-start(bf16[128,1024]{1,0:T(8,128)(2,1)S(1)} %broadcast_select_fusion.4.refs_0_), channel_id=1, source_target_pairs={{0,16},{1,17},{2,18},{3,19},{4,20},{5,21},{6,22},{7,23},{8,24},{9,... | collective-permute-start | bytes 786440 | tf_op jit(solution)/shard_map/ppermute | solution.py:361
  221.4 10.5 %collective-permute-start.39 = (bf16[128,768]{1,0:T(8,128)(2,1)S(1)}, bf16[128,768]{1,0:T(8,128)(2,1)S(1)}, u32[]{:S(2)}, u32[]{:S(2)}) collective-permute-start(bf16[128,768]{1,0:T(8,128)(2,1)S(1)} %shard_map.121), channel_id=1, source_target_pairs={{0,16},{1,17},{2,18},{3,19},{4,20},{5,21},{6,22},{7,23},{8,24},{9,... | collective-permute-start | bytes 589832 | tf_op jit(solution)/shard_map/ppermute | solution.py:361
  (58 other events, 231.1 us)

commit v3 on v1

--- a/solution.py
+++ b/solution.py
@@ -62,7 +62,7 @@
             pltpu.SemaphoreType.DMA((len(arrays),)),
             pltpu.SemaphoreType.DMA((len(arrays),)),
         ],
-        compiler_params=pltpu.CompilerParams(vmem_limit_bytes=62 * 1024 * 1024),
+        compiler_params=pltpu.CompilerParams(vmem_limit_bytes=58 * 1024 * 1024),
         cost_estimate=pl.CostEstimate(
             flops=0, bytes_accessed=4 * shape[0] * shape[1], transcendentals=0
         ),
@@ -129,8 +129,9 @@
             first_copies.append(
                 pltpu.make_async_copy(source, landing.at[a, rows_there], block_sems.at[i])
             )
-        for d, source in enumerate(edges):
+        for d in range(2 * len(edges)):
             column = pl.ds(pl.multiple_of(table[links + 2, d], panel), panel)
+            source = edges[d // 2].at[pl.ds((d % 2) * sz.row_count, sz.row_count)]
             first_copies.append(
                 pltpu.make_async_copy(source, out.at[:, column], edge_sems.at[d])
             )
@@ -225,13 +226,10 @@
     anywhere = pl.BlockSpec(memory_space=pl.ANY)
     operands = [table, *received, *edges, *(weights[:2] if first else [*weights, state])]
     block = jax.ShapeDtypeStruct((sz.row_count // count, sz.width), jnp.bfloat16)
-    kept = jax.ShapeDtypeStruct((4 * sz.row_count, 2 * sz.local_hidden), jnp.float32)
+    kept = jax.ShapeDtypeStruct((24 * sz.row_count, 2 * sz.local_hidden), jnp.float32)
     fresh = jax.ShapeDtypeStruct((sz.row_count, sz.width), jnp.bfloat16)
     shapes = [block] * count + [fresh, kept]
-    in_hbm = pl.BlockSpec(memory_space=pltpu.HBM)
     in_specs = [pl.BlockSpec(memory_space=pltpu.SMEM)] + [anywhere] * (len(operands) - 1)
-    if not first:
-        in_specs[-1] = in_hbm
     whole = (sz.row_count, sz.width)
     results = pl.pallas_call(
         functools.partial(
@@ -239,7 +237,7 @@
         ),
         out_shape=shapes,
         in_specs=in_specs,
-        out_specs=[anywhere] * (count + 1) + [in_hbm],
+        out_specs=[anywhere] * len(shapes),
         input_output_aliases={} if first else {len(operands) - 1: count + 1},
         scratch_shapes=[
             pltpu.VMEM((2, sz.width, sz.local_hidden), jnp.bfloat16),
@@ -256,7 +254,7 @@
             pltpu.SemaphoreType.DMA((count,)),
             pltpu.SemaphoreType.DMA((3,)),
         ],
-        compiler_params=pltpu.CompilerParams(vmem_limit_bytes=62 * 1024 * 1024),
+        compiler_params=pltpu.CompilerParams(vmem_limit_bytes=58 * 1024 * 1024),
         cost_estimate=pl.CostEstimate(
             flops=8 * sz.row_count * sz.width * sz.local_hidden,
             bytes_accessed=8 * sz.width * sz.local_hidden,
@@ -313,7 +311,7 @@
             pltpu.VMEM(weight.shape, jnp.bfloat16),
             pltpu.SemaphoreType.DMA,
         ],
-        compiler_params=pltpu.CompilerParams(vmem_limit_bytes=62 * 1024 * 1024),
+        compiler_params=pltpu.CompilerParams(vmem_limit_bytes=58 * 1024 * 1024),
         cost_estimate=pl.CostEstimate(
             flops=2 * rows_count * sz.width * hidden_size,
             bytes_accessed=2 * sz.width * hidden_size,
@@ -394,9 +392,12 @@
 
     edge = jnp.where(section_id == 0, inputs[0, 0], targets[0, 0])
     ends = [(s, j) for s in (0, links) for j in range(shards)]
-    edges = [edge] + [
-        move(edge, ends, lambda r, s, j, d=d: (r, s, j ^ d)) for d in range(1, shards)
-    ]
+
+    def at_ends(array, offset):
+        return move(array, ends, lambda r, s, j: (r, s, j ^ offset))
+
+    pair = jnp.concatenate([edge, at_ends(edge, 1)])
+    edges = [pair, at_ends(pair, 2)]
     rest = range(1, sections)
     near = [to_holders(weight_in, 1, rest), to_holders(weight_out, 1, rest)]
 
@@ -487,7 +488,7 @@
         rows = fresh if step == 0 else jnp.where(section_id == step, fresh, rows)
         if step == 0:
             total = sends[0].astype(jnp.float32)
-            total = total + to_holders(sends[0], 1, [0]).astype(jnp.float32)
+            total = total + at_ends(sends[0], 1).astype(jnp.float32)
             sends = [total.astype(jnp.bfloat16)]
             if in_kernel:
                 sends = [piece(sends[0], slots[0, e], block_rows) for e in range(replicas)]
@@ -499,9 +500,9 @@
                 )
                 far_states_out = exchange(packed_out, early)
         else:
-            received = [sends[0], from_holders(sends[0], 2, [links])]
-        if len(late) - 1 <= step < links:
-            received = spread_rows(received, rows, late if step < len(late) else [step])
+            received = [sends[0], at_ends(sends[0], 2)]
+        if step == len(late) - 1:
+            received = spread_rows(received, rows, late)
         if step == len(late) - 1:
             received, packed_out = lax.optimization_barrier((received, packed_out))
             far_late = exchange(packed_out, late)
@@ -515,12 +516,13 @@
         upstream = fresh if step == links else jnp.where(section_id == step, fresh, upstream)
         received = send_blocks(sends, slots[step - 1], back, step, -1)
         if step == links:
-            received = spread_rows(received, rows, [links])
+            received = spread_rows(received, rows, early)
         if step == len(late):
             received, far_late, row_parts = lax.optimization_barrier(
                 (received, far_late, row_parts)
             )
 
+    upstream, rows, row_parts = lax.optimization_barrier((upstream, rows, row_parts))
     own_rows = jnp.where(is_holder, rows, sum(row_parts[1:], row_parts[0]))
     normed, hidden, slope = share_call(sz, [own_rows], weight_in)
 

time: 225 us -> 213 us (0.947)
  starting transfers between devices: 140 us -> 46.2 us
  waiting for transfers between devices: 23.8 us -> 111 us
  other arithmetic: 12 us -> 7.51 us
    ppermute x41 -> x39, starting transfers between devices: 140 us -> 46.2 us  [move(): return lax.ppermute(array, axes, pairs)]
    ppermute x41 -> x39, waiting for transfers between devices: 23.8 us -> 111 us  [move(): return lax.ppermute(array, axes, pairs)]
    select_n x3 -> x2, other arithmetic: 2.72 us -> 0.1 us  [per_device(): rows = fresh if step == 0 else jnp.where(section_id == step, fresh, rows)]
    unnamed x92 -> x100, local copies, waits for them, and re-layouts: 5.91 us -> 6.38 us
  transfers between devices with their start and end apart: 41 -> 39, of which waited for: 7 -> 7; matrix products, arithmetic and copies ran while one was open for 9% -> 6% of each run, Pallas kernels for 8% -> 8%
where the time goes in v3:
time: 213 us; the launch traced here: 212 us
  waiting for transfers between devices  111 us (52%)
  starting transfers between devices  46.2 us (22%)
  Pallas kernels  22.2 us (10%)
  matrix products  10.7 us (5%)
  local copies, waits for them, and re-layouts  9.7 us (5%)
  other arithmetic  7.51 us (4%)
  between operations  4.64 us (2%)
    ppermute x39, waiting for transfers between devices, move(): return lax.ppermute(array, axes, pairs)  111 us
    ppermute x39, starting transfers between devices, move(): return lax.ppermute(array, axes, pairs)  46.2 us
    dot_general x6, matrix products, dot(): lax.dot_general(left, right, dims, preferred_element_type=jnp.float32)  10.7 us
    pallas_call x7, Pallas kernels, chain_step(): pl.pallas_call(functools.partial(chain_kernel, sz, step, forward, (len(re...  9.99 us
    pallas_call x2, Pallas kernels, share_call(): pl.pallas_call(functools.partial(share_kernel, sz, whole), out_shape=shap...  7.47 us
    unnamed x100, local copies, waits for them, and re-layouts  6.38 us
    pallas_call x2, Pallas kernels, pack(): pl.pallas_call(functools.partial(pack_kernel, size), out_shape=jax.ShapeD...  4.73 us
  transfers between devices with their start and end apart: 39, of which 7 were waited for; matrix products, arithmetic and copies ran while one was open for 6% of the time, Pallas kernels for 8%

profile of v3, /device:TPU:0, one launch (start us, length us, event | category | flops | bytes accessed | tf_op | source)
XLA Modules:
  0.0 211.5 jit_solution(11135859291822956402)
XLA Ops:
  1.5 4.9 %collective-permute-start = (bf16[128,256]{1,0:T(8,128)(2,1)S(1)}, bf16[128,256]{1,0:T(8,128)(2,1)S(1)}, u32[]{:S(2)}, u32[]{:S(2)}) collective-permute-start(bf16[128,256]{1,0:T(8,128)(2,1)S(1)} %select_bitcast_fusion), channel_id=1, source_target_pairs={{0,1},{1,0},{2,3},{3,2},{12,13},{13,12},{14,15},{15,14},{16,17},{1... | collective-permute-start | bytes 196616 | tf_op jit(solution)/shard_map/ppermute | solution.py:362
  9.5 2.4 %shard_map.112 = bf16[1024,768]{1,0:T(8,128)(2,1)} custom-call(s32[1]{0:T(128)} %bitcast.9.starts, bf16[1024,768]{1,0:T(8,128)(2,1)} %bitcast.84, bf16[1024,768]{1,0:T(8,128)(2,1)} %bitcast.93), custom_call_target="tpu_custom_call" | custom-call | bytes 3145728 | tf_op jit(solution)/shard_map/pallas_call | solution.py:55
  11.9 1.6 collective-permute-start.7
  13.5 1.8 collective-permute-start.9
  15.7 4.5 %collective-permute-start.1 = (bf16[256,256]{1,0:T(8,128)(2,1)S(1)}, bf16[256,256]{1,0:T(8,128)(2,1)S(1)}, u32[]{:S(2)}, u32[]{:S(2)}) collective-permute-start(bf16[256,256]{1,0:T(8,128)(2,1)S(1)} %pad_maximum_fusion.1.refs_1_.refs_3_), channel_id=1, source_target_pairs={{0,2},{1,3},{2,0},{3,1},{12,14},{13,15},{14,12},{15,13},{16,18},{1... | collective-permute-start | bytes 393224 | tf_op jit(solution)/shard_map/ppermute | solution.py:362
  20.8 4.1 %collective-permute-done.1.refs_2_.refs_4_ = bf16[256,256]{1,0:T(8,128)(2,1)S(1)} collective-permute-done((bf16[256,256]{1,0:T(8,128)(2,1)S(1)}, bf16[256,256]{1,0:T(8,128)(2,1)S(1)}, u32[]{:S(2)}, u32[]{:S(2)}) %collective-permute-start.1) | collective-permute-done | bytes 131104 | tf_op jit(solution)/shard_map/ppermute | solution.py:362
  25.6 4.1 %shard_map.111 = (bf16[128,1024]{1,0:T(8,128)(2,1)}, bf16[128,1024]{1,0:T(8,128)(2,1)}, f32[3072,1536]{1,0:T(8,128)}) custom-call(s32[6,5]{1,0:T(8,128)} %fusion.31.refs_0_, bf16[256,256]{1,0:T(8,128)(2,1)} %copy-done.10, bf16[256,256]{1,0:T(8,128)(2,1)} %copy-done.12, bf16[1024,768]{1,0:T(8,128)(2,1)} %bitcast.85, bf16[768,1024]{1,0:T(8,128)(2,1)} %bitcast.73), custom_call_target="tpu_custom_call" | custom-call | flops 805306368 | bytes 6291456 | tf_op jit(solution)/shard_map/pallas_call | solution.py:234
  29.7 2.3 %collective-permute-start.2 = (bf16[128,1024]{1,0:T(8,128)(2,1)}, bf16[128,1024]{1,0:T(8,128)(2,1)S(1)}, u32[]{:S(2)}, u32[]{:S(2)}) collective-permute-start(bf16[128,1024]{1,0:T(8,128)(2,1)} %get-tuple-element.77), channel_id=1, source_target_pairs={{0,1},{1,0},{2,3},{3,2},{12,13},{13,12},{14,15},{15,14},{16,17},{1... | collective-permute-start | bytes 786440 | tf_op jit(solution)/shard_map/ppermute | solution.py:362
  34.0 7.1 %collective-permute-done.2 = bf16[128,1024]{1,0:T(8,128)(2,1)S(1)} collective-permute-done((bf16[128,1024]{1,0:T(8,128)(2,1)}, bf16[128,1024]{1,0:T(8,128)(2,1)S(1)}, u32[]{:S(2)}, u32[]{:S(2)}) %collective-permute-start.2) | collective-permute-done | bytes 262176 | tf_op jit(solution)/shard_map/ppermute | solution.py:362
  47.6 2.3 %shard_map.113 = bf16[768,1024]{1,0:T(8,128)(2,1)} custom-call(s32[1]{0:T(128)} %bitcast.10.starts, bf16[768,1024]{1,0:T(8,128)(2,1)} %bitcast.74, bf16[768,1024]{1,0:T(8,128)(2,1)} %bitcast.94), custom_call_target="tpu_custom_call" | custom-call | bytes 3145728 | tf_op jit(solution)/shard_map/pallas_call | solution.py:55
  50.0 1.8 collective-permute-start.18
  56.9 2.3 %collective-permute-start.29 = (bf16[768,1024]{1,0:T(8,128)(2,1)}, bf16[768,1024]{1,0:T(8,128)(2,1)S(1)}, u32[]{:S(2)}, u32[]{:S(2)}) collective-permute-start(bf16[768,1024]{1,0:T(8,128)(2,1)} %shard_map.113), channel_id=1, source_target_pairs={{0,16},{1,17},{2,18},{3,19},{4,20},{5,21},{6,22},{7,23},{16,0},{17... | collective-permute-start | bytes 4718600 | tf_op jit(solution)/shard_map/ppermute | solution.py:362
  64.5 3.3 %collective-permute-start.19 = (bf16[128,1024]{1,0:T(8,128)(2,1)}, bf16[128,1024]{1,0:T(8,128)(2,1)S(1)}, u32[]{:S(2)}, u32[]{:S(2)}) collective-permute-start(bf16[128,1024]{1,0:T(8,128)(2,1)} %get-tuple-element.106.refs_1_), channel_id=1, source_target_pairs={{0,2},{1,3},{2,0},{3,1},{12,14},{13,15},{14,12},{15,13},{16,18},{1... | collective-permute-start | bytes 786440 | tf_op jit(solution)/shard_map/ppermute | solution.py:362
  69.1 7.5 %collective-permute-done.19.refs_2_ = bf16[128,1024]{1,0:T(8,128)(2,1)S(1)} collective-permute-done((bf16[128,1024]{1,0:T(8,128)(2,1)}, bf16[128,1024]{1,0:T(8,128)(2,1)S(1)}, u32[]{:S(2)}, u32[]{:S(2)}) %collective-permute-start.19) | collective-permute-done | bytes 262176 | tf_op jit(solution)/shard_map/ppermute | solution.py:362
  80.4 4.5 %collective-permute-done.24 = bf16[128,1024]{1,0:T(8,128)(2,1)S(1)} collective-permute-done((bf16[128,1024]{1,0:T(8,128)(2,1)S(1)}, bf16[128,1024]{1,0:T(8,128)(2,1)S(1)}, u32[]{:S(2)}, u32[]{:S(2)}) %collective-permute-start.24) | collective-permute-done | bytes 262176 | tf_op jit(solution)/shard_map/ppermute | solution.py:362
  92.9 3.7 %shard_map.120 = (bf16[128,1024]{1,0:T(8,128)(2,1)}, bf16[128,768]{1,0:T(8,128)(2,1)}, f32[128,768]{1,0:T(8,128)}) custom-call(bf16[128,1024]{1,0:T(8,128)(2,1)} %add_select_fusion.refs_0_, bf16[1024,768]{1,0:T(8,128)(2,1)} %bitcast.92), custom_call_target="tpu_custom_call" | custom-call | flops 201326592 | bytes 1572864 | tf_op jit(solution)/shard_map/pallas_call | solution.py:305
  101.8 2.7 %collective-permute-done.35 = bf16[128,896]{1,0:T(8,128)(2,1)S(1)} collective-permute-done((bf16[128,896]{1,0:T(8,128)(2,1)S(1)}, bf16[128,896]{1,0:T(8,128)(2,1)S(1)}, u32[]{:S(2)}, u32[]{:S(2)}) %collective-permute-start.35) | collective-permute-done | bytes 229408 | tf_op jit(solution)/shard_map/ppermute | solution.py:362
  107.7 79.9 %collective-permute-done.36 = bf16[128,1024]{1,0:T(8,128)(2,1)S(1)} collective-permute-done((bf16[128,1024]{1,0:T(8,128)(2,1)S(1)}, bf16[128,1024]{1,0:T(8,128)(2,1)S(1)}, u32[]{:S(2)}, u32[]{:S(2)}) %collective-permute-start.36) | collective-permute-done | bytes 262176 | tf_op jit(solution)/shard_map/ppermute | solution.py:362
  188.1 2.9 %fusion.9 = (bf16[1,1,768,1024]{3,2,1,0:T(8,128)(2,1)}, bf16[1,1,768,1024]{3,2,1,0:T(8,128)(2,1)}) fusion(bf16[1,1,768,1024]{3,2,1,0:T(8,128)(2,1)S(1)} %copy-done.8, bf16[1,1,768,1024]{3,2,1,0:T(8,128)(2,1)S(1)} %copy-done.2, bf16[128,768]{1,0:T(8,128)(2,1)S(1)} %copy-done.39, bf16[128,1024]{1,0:T(8,128)(2,1)S(1)} %broadcast_select_fusion.2.refs_0_), kind=kOutput, calls=%fused_computation.15 | convolution fusion | flops 211550208 | bytes 6750208 | tf_op jit(solution)/shard_map/dot_general | solution.py:22
  192.5 3.8 %shard_map.121 = bf16[128,768]{1,0:T(8,128)(2,1)} custom-call(bf16[128,1024]{1,0:T(8,128)(2,1)} %copy-done.6, f32[128,768]{1,0:T(8,128)} %get-tuple-element.145.refs_1_, bf16[768,1024]{1,0:T(8,128)(2,1)} %bitcast.81), custom_call_target="tpu_custom_call" | custom-call | flops 201326592 | bytes 1572864 | tf_op jit(solution)/shard_map/pallas_call | solution.py:305
  196.4 2.2 %fusion.8 = (bf16[1,1,1024,768]{3,2,1,0:T(8,128)(2,1)S(1)}, bf16[1,1,1024,768]{3,2,1,0:T(8,128)(2,1)S(1)}) fusion(bf16[1,1,1024,768]{3,2,1,0:T(8,128)(2,1)S(1)} %copy-done.7, bf16[1,1,1024,768]{3,2,1,0:T(8,128)(2,1)S(1)} %copy-done.4, bf16[128,1024]{1,0:T(8,128)(2,1)S(1)} %copy-done.38, bf16[128,768]{1,0:T(8,128)(2,1)} %shard_map.121), kind=kOutput, calls=%fused_computation.14 | convolution fusion | flops 211550208 | bytes 6750208 | tf_op jit(solution)/shard_map/dot_general | solution.py:22
  199.6 4.7 %collective-permute-done.37 = bf16[128,768]{1,0:T(8,128)(2,1)S(1)} collective-permute-done((bf16[128,768]{1,0:T(8,128)(2,1)S(1)}, bf16[128,768]{1,0:T(8,128)(2,1)S(1)}, u32[]{:S(2)}, u32[]{:S(2)}) %collective-permute-start.37) | collective-permute-done | bytes 196640 | tf_op jit(solution)/shard_map/ppermute | solution.py:362
  204.4 2.7 %fusion.27 = (bf16[1,1,1024,768]{3,2,1,0:T(8,128)(2,1)S(1)}, bf16[1,1,1024,768]{3,2,1,0:T(8,128)(2,1)S(1)}) fusion(bf16[1,1,1024,768]{3,2,1,0:T(8,128)(2,1)S(1)} %get-tuple-element.158, s32[]{:T(128)S(6)} %select_n.155, bf16[1024,768]{1,0:T(8,128)(2,1)} %collective-permute-done.7, bf16[1,1,1024,768]{3,2,1,0:T(8,128)(2,1)S(1)} %copy-done.7, ...), kind=kOutput, calls=%fused_computation.44 | convolution fusion | flops 108920832 | bytes 5832708 | tf_op jit(solution)/shard_map/dot_general | solution.py:22
  207.6 2.2 %fusion.25 = (bf16[1,1,768,1024]{3,2,1,0:T(8,128)(2,1)S(1)}, bf16[1,1,768,1024]{3,2,1,0:T(8,128)(2,1)S(1)}) fusion(bf16[1,1,768,1024]{3,2,1,0:T(8,128)(2,1)S(1)} %copy-done.44, s32[]{:T(128)S(6)} %select_n.156, bf16[768,1024]{1,0:T(8,128)(2,1)S(1)} %copy-done.9, bf16[1,1,768,1024]{3,2,1,0:T(8,128)(2,1)S(1)} %copy-done.8, ...), kind=kOutput, calls=%fused_computation.42 | convolution fusion | flops 108920832 | bytes 5865476 | tf_op jit(solution)/shard_map/dot_general | solution.py:22
  (205 shorter events, 47.5 us)
Async XLA Ops:
  1.5 14.1 %collective-permute-start = (bf16[128,256]{1,0:T(8,128)(2,1)S(1)}, bf16[128,256]{1,0:T(8,128)(2,1)S(1)}, u32[]{:S(2)}, u32[]{:S(2)}) collective-permute-start(bf16[128,256]{1,0:T(8,128)(2,1)S(1)} %select_bitcast_fusion), channel_id=1, source_target_pairs={{0,1},{1,0},{2,3},{3,2},{12,13},{13,12},{14,15},{15,14},{16,17},{1... | collective-permute-start | bytes 196616 | tf_op jit(solution)/shard_map/ppermute | solution.py:362
  6.5 45.4 %collective-permute-start.8 = (bf16[1024,768]{1,0:T(8,128)(2,1)}, bf16[1024,768]{1,0:T(8,128)(2,1)S(1)}, u32[]{:S(2)}, u32[]{:S(2)}) collective-permute-start(bf16[1024,768]{1,0:T(8,128)(2,1)} %bitcast.83), channel_id=1, source_target_pairs={{5,4},{7,6},{9,8},{11,10},{12,13},{14,15},{21,20},{23,22},{25,24},... | collective-permute-start | bytes 4718600 | tf_op jit(solution)/shard_map/ppermute | solution.py:362
  11.9 38.1 %collective-permute-start.7 = (bf16[1024,768]{1,0:T(8,128)(2,1)}, bf16[1024,768]{1,0:T(8,128)(2,1)}, u32[]{:S(2)}, u32[]{:S(2)}) collective-permute-start(bf16[1024,768]{1,0:T(8,128)(2,1)} %shard_map.112), channel_id=1, source_target_pairs={{0,16},{1,17},{2,18},{3,19},{4,20},{5,21},{6,22},{7,23},{8,24},{9,... | collective-permute-start | bytes 4718600 | tf_op jit(solution)/shard_map/ppermute | solution.py:362
  13.5 38.3 %collective-permute-start.9 = (bf16[768,1024]{1,0:T(8,128)(2,1)S(1)}, bf16[768,1024]{1,0:T(8,128)(2,1)}, u32[]{:S(2)}, u32[]{:S(2)}) collective-permute-start(bf16[768,1024]{1,0:T(8,128)(2,1)S(1)} %bitcast.82), channel_id=1, source_target_pairs={{5,4},{7,6},{9,8},{11,10},{12,13},{14,15},{21,20},{23,22},{25,24},... | collective-permute-start | bytes 4718600 | tf_op jit(solution)/shard_map/ppermute | solution.py:362
  15.7 9.2 %collective-permute-start.1 = (bf16[256,256]{1,0:T(8,128)(2,1)S(1)}, bf16[256,256]{1,0:T(8,128)(2,1)S(1)}, u32[]{:S(2)}, u32[]{:S(2)}) collective-permute-start(bf16[256,256]{1,0:T(8,128)(2,1)S(1)} %pad_maximum_fusion.1.refs_1_.refs_3_), channel_id=1, source_target_pairs={{0,2},{1,3},{2,0},{3,1},{12,14},{13,15},{14,12},{15,13},{16,18},{1... | collective-permute-start | bytes 393224 | tf_op jit(solution)/shard_map/ppermute | solution.py:362
  29.7 11.3 %collective-permute-start.2 = (bf16[128,1024]{1,0:T(8,128)(2,1)}, bf16[128,1024]{1,0:T(8,128)(2,1)S(1)}, u32[]{:S(2)}, u32[]{:S(2)}) collective-permute-start(bf16[128,1024]{1,0:T(8,128)(2,1)} %get-tuple-element.77), channel_id=1, source_target_pairs={{0,1},{1,0},{2,3},{3,2},{12,13},{13,12},{14,15},{15,14},{16,17},{1... | collective-permute-start | bytes 786440 | tf_op jit(solution)/shard_map/ppermute | solution.py:362
  44.2 5.8 %collective-permute-start.5 = (bf16[64,1024]{1,0:T(8,128)(2,1)}, bf16[64,1024]{1,0:T(8,128)(2,1)S(1)}, u32[]{:S(2)}, u32[]{:S(2)}) collective-permute-start(bf16[64,1024]{1,0:T(8,128)(2,1)} %get-tuple-element.160), channel_id=1, source_target_pairs={{1,20},{3,22},{17,4},{19,6}} | collective-permute-start | bytes 393224 | tf_op jit(solution)/shard_map/ppermute | solution.py:362
  44.9 5.1 %collective-permute-start.6 = (bf16[64,1024]{1,0:T(8,128)(2,1)}, bf16[64,1024]{1,0:T(8,128)(2,1)}, u32[]{:S(2)}, u32[]{:S(2)}) collective-permute-start(bf16[64,1024]{1,0:T(8,128)(2,1)} %get-tuple-element.160), channel_id=1, source_target_pairs={{1,22},{3,20},{17,6},{19,4}} | collective-permute-start | bytes 393224 | tf_op jit(solution)/shard_map/ppermute | solution.py:362
  50.0 12.9 %collective-permute-start.18 = (bf16[768,1024]{1,0:T(8,128)(2,1)}, bf16[768,1024]{1,0:T(8,128)(2,1)}, u32[]{:S(2)}, u32[]{:S(2)}) collective-permute-start(bf16[768,1024]{1,0:T(8,128)(2,1)} %shard_map.113), channel_id=1, source_target_pairs={{8,24},{9,25},{10,26},{11,27},{12,28},{13,29},{14,30},{15,31},{24,... | collective-permute-start | bytes 4718600 | tf_op jit(solution)/shard_map/ppermute | solution.py:362
  54.0 2.8 %collective-permute-start.10 = (bf16[64,1024]{1,0:T(8,128)(2,1)}, bf16[64,1024]{1,0:T(8,128)(2,1)S(1)}, u32[]{:S(2)}, u32[]{:S(2)}) collective-permute-start(bf16[64,1024]{1,0:T(8,128)(2,1)} %get-tuple-element.85), channel_id=1, source_target_pairs={{4,8},{6,10},{20,24},{22,26}} | collective-permute-start | bytes 393224 | tf_op jit(solution)/shard_map/ppermute | solution.py:362
  54.7 2.1 %collective-permute-start.11 = (bf16[64,1024]{1,0:T(8,128)(2,1)}, bf16[64,1024]{1,0:T(8,128)(2,1)S(1)}, u32[]{:S(2)}, u32[]{:S(2)}) collective-permute-start(bf16[64,1024]{1,0:T(8,128)(2,1)} %get-tuple-element.85), channel_id=1, source_target_pairs={{4,10},{6,8},{20,26},{22,24}} | collective-permute-start | bytes 393224 | tf_op jit(solution)/shard_map/ppermute | solution.py:362
  56.9 32.7 %collective-permute-start.29 = (bf16[768,1024]{1,0:T(8,128)(2,1)}, bf16[768,1024]{1,0:T(8,128)(2,1)S(1)}, u32[]{:S(2)}, u32[]{:S(2)}) collective-permute-start(bf16[768,1024]{1,0:T(8,128)(2,1)} %shard_map.113), channel_id=1, source_target_pairs={{0,16},{1,17},{2,18},{3,19},{4,20},{5,21},{6,22},{7,23},{16,0},{17... | collective-permute-start | bytes 4718600 | tf_op jit(solution)/shard_map/ppermute | solution.py:362
  64.5 12.1 %collective-permute-start.19 = (bf16[128,1024]{1,0:T(8,128)(2,1)}, bf16[128,1024]{1,0:T(8,128)(2,1)S(1)}, u32[]{:S(2)}, u32[]{:S(2)}) collective-permute-start(bf16[128,1024]{1,0:T(8,128)(2,1)} %get-tuple-element.106.refs_1_), channel_id=1, source_target_pairs={{0,2},{1,3},{2,0},{3,1},{12,14},{13,15},{14,12},{15,13},{16,18},{1... | collective-permute-start | bytes 786440 | tf_op jit(solution)/shard_map/ppermute | solution.py:362
  67.8 17.1 %collective-permute-start.24 = (bf16[128,1024]{1,0:T(8,128)(2,1)S(1)}, bf16[128,1024]{1,0:T(8,128)(2,1)S(1)}, u32[]{:S(2)}, u32[]{:S(2)}) collective-permute-start(bf16[128,1024]{1,0:T(8,128)(2,1)S(1)} %broadcast_select_fusion.1), channel_id=1, source_target_pairs={{1,0},{3,2},{4,5},{6,7},{17,16},{19,18},{20,21},{22,23}} | collective-permute-start | bytes 786440 | tf_op jit(solution)/shard_map/ppermute | solution.py:362
  78.4 7.3 %collective-permute-start.20 = (bf16[64,1024]{1,0:T(8,128)(2,1)}, bf16[64,1024]{1,0:T(8,128)(2,1)S(1)}, u32[]{:S(2)}, u32[]{:S(2)}) collective-permute-start(bf16[64,1024]{1,0:T(8,128)(2,1)} %get-tuple-element.108), channel_id=1, source_target_pairs={{13,8},{15,10},{29,24},{31,26}} | collective-permute-start | bytes 393224 | tf_op jit(solution)/shard_map/ppermute | solution.py:362
  79.1 6.6 %collective-permute-start.21 = (bf16[64,1024]{1,0:T(8,128)(2,1)}, bf16[64,1024]{1,0:T(8,128)(2,1)S(1)}, u32[]{:S(2)}, u32[]{:S(2)}) collective-permute-start(bf16[64,1024]{1,0:T(8,128)(2,1)} %get-tuple-element.108), channel_id=1, source_target_pairs={{13,10},{15,8},{29,26},{31,24}} | collective-permute-start | bytes 393224 | tf_op jit(solution)/shard_map/ppermute | solution.py:362
  79.8 5.9 %collective-permute-start.22 = (bf16[64,1024]{1,0:T(8,128)(2,1)}, bf16[64,1024]{1,0:T(8,128)(2,1)S(1)}, u32[]{:S(2)}, u32[]{:S(2)}) collective-permute-start(bf16[64,1024]{1,0:T(8,128)(2,1)} %get-tuple-element.109), channel_id=1, source_target_pairs={{13,24},{15,26},{29,8},{31,10}} | collective-permute-start | bytes 393224 | tf_op jit(solution)/shard_map/ppermute | solution.py:362
  85.7 4.6 %collective-permute-start.30 = (bf16[128,1024]{1,0:T(8,128)(2,1)S(1)}, bf16[128,1024]{1,0:T(8,128)(2,1)S(1)}, u32[]{:S(2)}, u32[]{:S(2)}) collective-permute-start(bf16[128,1024]{1,0:T(8,128)(2,1)S(1)} %select_select_fusion.1), channel_id=1, source_target_pairs={{8,9},{10,11},{13,12},{15,14},{24,25},{26,27},{29,28},{31,30}} | collective-permute-start | bytes 786440 | tf_op jit(solution)/shard_map/ppermute | solution.py:362
  87.5 2.7 %collective-permute-start.25 = (bf16[64,1024]{1,0:T(8,128)(2,1)}, bf16[64,1024]{1,0:T(8,128)(2,1)S(1)}, u32[]{:S(2)}, u32[]{:S(2)}) collective-permute-start(bf16[64,1024]{1,0:T(8,128)(2,1)} %get-tuple-element.118), channel_id=1, source_target_pairs={{8,4},{10,6},{24,20},{26,22}} | collective-permute-start | bytes 393224 | tf_op jit(solution)/shard_map/ppermute | solution.py:362
  98.5 6.1 %collective-permute-start.35 = (bf16[128,896]{1,0:T(8,128)(2,1)S(1)}, bf16[128,896]{1,0:T(8,128)(2,1)S(1)}, u32[]{:S(2)}, u32[]{:S(2)}) collective-permute-start(bf16[128,896]{1,0:T(8,128)(2,1)S(1)} %pad_maximum_fusion), channel_id=1, source_target_pairs={{0,16},{1,17},{2,18},{3,19},{4,20},{5,21},{6,22},{7,23},{8,24},{9,... | collective-permute-start | bytes 688136 | tf_op jit(solution)/shard_map/ppermute | solution.py:362
  99.1 2.7 %collective-permute-start.31 = (bf16[64,1024]{1,0:T(8,128)(2,1)S(1)}, bf16[64,1024]{1,0:T(8,128)(2,1)S(1)}, u32[]{:S(2)}, u32[]{:S(2)}) collective-permute-start(bf16[64,1024]{1,0:T(8,128)(2,1)S(1)} %copy-done.43), channel_id=1, source_target_pairs={{4,1},{6,3},{20,17},{22,19}} | collective-permute-start | bytes 393224 | tf_op jit(solution)/shard_map/ppermute | solution.py:362
  104.8 82.8 %collective-permute-start.36 = (bf16[128,1024]{1,0:T(8,128)(2,1)S(1)}, bf16[128,1024]{1,0:T(8,128)(2,1)S(1)}, u32[]{:S(2)}, u32[]{:S(2)}) collective-permute-start(bf16[128,1024]{1,0:T(8,128)(2,1)S(1)} %fusion.28), channel_id=1, source_target_pairs={{1,0},{3,2},{4,5},{6,7},{8,9},{10,11},{13,12},{15,14},{17,16},{19,... | collective-permute-start | bytes 786440 | tf_op jit(solution)/shard_map/ppermute | solution.py:362
  191.0 16.0 %collective-permute-start.38 = (bf16[128,1024]{1,0:T(8,128)(2,1)S(1)}, bf16[128,1024]{1,0:T(8,128)(2,1)}, u32[]{:S(2)}, u32[]{:S(2)}) collective-permute-start(bf16[128,1024]{1,0:T(8,128)(2,1)S(1)} %broadcast_select_fusion.2.refs_0_), channel_id=1, source_target_pairs={{0,16},{1,17},{2,18},{3,19},{4,20},{5,21},{6,22},{7,23},{8,24},{9,... | collective-permute-start | bytes 786440 | tf_op jit(solution)/shard_map/ppermute | solution.py:362
  198.6 5.7 %collective-permute-start.37 = (bf16[128,768]{1,0:T(8,128)(2,1)S(1)}, bf16[128,768]{1,0:T(8,128)(2,1)S(1)}, u32[]{:S(2)}, u32[]{:S(2)}) collective-permute-start(bf16[128,768]{1,0:T(8,128)(2,1)S(1)} %copy-done.11), channel_id=1, source_target_pairs={{0,16},{1,17},{2,18},{3,19},{4,20},{5,21},{6,22},{7,23},{8,24},{9,... | collective-permute-start | bytes 589832 | tf_op jit(solution)/shard_map/ppermute | solution.py:362
  (65 other events, 415.7 us)

commit v4 on v3

--- a/solution.py
+++ b/solution.py
@@ -62,7 +62,7 @@
             pltpu.SemaphoreType.DMA((len(arrays),)),
             pltpu.SemaphoreType.DMA((len(arrays),)),
         ],
-        compiler_params=pltpu.CompilerParams(vmem_limit_bytes=58 * 1024 * 1024),
+        compiler_params=pltpu.CompilerParams(vmem_limit_bytes=32 * 1024 * 1024),
         cost_estimate=pl.CostEstimate(
             flops=0, bytes_accessed=4 * shape[0] * shape[1], transcendentals=0
         ),
@@ -226,7 +226,7 @@
     anywhere = pl.BlockSpec(memory_space=pl.ANY)
     operands = [table, *received, *edges, *(weights[:2] if first else [*weights, state])]
     block = jax.ShapeDtypeStruct((sz.row_count // count, sz.width), jnp.bfloat16)
-    kept = jax.ShapeDtypeStruct((24 * sz.row_count, 2 * sz.local_hidden), jnp.float32)
+    kept = jax.ShapeDtypeStruct((48 * sz.row_count, 2 * sz.local_hidden), jnp.float32)
     fresh = jax.ShapeDtypeStruct((sz.row_count, sz.width), jnp.bfloat16)
     shapes = [block] * count + [fresh, kept]
     in_specs = [pl.BlockSpec(memory_space=pltpu.SMEM)] + [anywhere] * (len(operands) - 1)
@@ -254,7 +254,7 @@
             pltpu.SemaphoreType.DMA((count,)),
             pltpu.SemaphoreType.DMA((3,)),
         ],
-        compiler_params=pltpu.CompilerParams(vmem_limit_bytes=58 * 1024 * 1024),
+        compiler_params=pltpu.CompilerParams(vmem_limit_bytes=32 * 1024 * 1024),
         cost_estimate=pl.CostEstimate(
             flops=8 * sz.row_count * sz.width * sz.local_hidden,
             bytes_accessed=8 * sz.width * sz.local_hidden,
@@ -311,7 +311,7 @@
             pltpu.VMEM(weight.shape, jnp.bfloat16),
             pltpu.SemaphoreType.DMA,
         ],
-        compiler_params=pltpu.CompilerParams(vmem_limit_bytes=58 * 1024 * 1024),
+        compiler_params=pltpu.CompilerParams(vmem_limit_bytes=32 * 1024 * 1024),
         cost_estimate=pl.CostEstimate(
             flops=2 * rows_count * sz.width * hidden_size,
             bytes_accessed=2 * sz.width * hidden_size,
@@ -479,6 +479,12 @@
         row_parts.append(from_holders(rows, 1, active))
         return received
 
+    def bundle(normed, hidden, e):
+        parts = [
+            piece(normed, pieces_in[e], size_in, 1), piece(hidden, pieces_out[e], size_out, 1)
+        ]
+        return jnp.concatenate(parts, axis=1)
+
     weights = [weight_in, weight_out, *near]
     received, state = [], None
     for step in every:
@@ -501,6 +507,13 @@
                 far_states_out = exchange(packed_out, early)
         else:
             received = [sends[0], at_ends(sends[0], 2)]
+            row_parts.append(from_holders(rows, 1, early))
+            own_rows = jnp.where(is_holder, rows, sum(row_parts[1:], row_parts[0]))
+            received, *shares = lax.optimization_barrier(
+                (received, *share_call(sz, [own_rows], weight_in))
+            )
+            normed, hidden, slope = shares
+            bundles = exchange([bundle(normed, hidden, e) for e in others], every)
         if step == len(late) - 1:
             received = spread_rows(received, rows, late)
         if step == len(late) - 1:
@@ -515,24 +528,11 @@
         )
         upstream = fresh if step == links else jnp.where(section_id == step, fresh, upstream)
         received = send_blocks(sends, slots[step - 1], back, step, -1)
-        if step == links:
-            received = spread_rows(received, rows, early)
         if step == len(late):
-            received, far_late, row_parts = lax.optimization_barrier(
-                (received, far_late, row_parts)
+            received, far_late, bundles = lax.optimization_barrier(
+                (received, far_late, bundles)
             )
 
-    upstream, rows, row_parts = lax.optimization_barrier((upstream, rows, row_parts))
-    own_rows = jnp.where(is_holder, rows, sum(row_parts[1:], row_parts[0]))
-    normed, hidden, slope = share_call(sz, [own_rows], weight_in)
-
-    def bundle(e):
-        first, second = normed, hidden
-        first = piece(first, pieces_in[e], size_in, 1)
-        return jnp.concatenate([first, piece(second, pieces_out[e], size_out, 1)], axis=1)
-
-    bundles = exchange([bundle(e) for e in others], every)
-    received, bundles = lax.optimization_barrier((received, bundles))
     far_normed = [one[:, :size_in] for one in bundles]
     far_hidden = [one[:, size_in:] for one in bundles]
 

time: 213 us -> 201 us (0.944)
  waiting for transfers between devices: 111 us -> 100 us
  Pallas kernels: 22.2 us -> 12 us
  local copies, waits for them, and re-layouts: 9.7 us -> 15.8 us
  starting transfers between devices: 46.2 us -> 51.8 us
  matrix products: 10.7 us -> 6.77 us
    ppermute x39, waiting for transfers between devices: 111 us -> 100 us  [move(): return lax.ppermute(array, axes, pairs)]
    unnamed x100 -> x80, local copies, waits for them, and re-layouts: 6.38 us -> 12.6 us
    pallas_call x2, Pallas kernels: 7.47 us -> 1.47 us  [share_call(): pl.pallas_call(functools.partial(share_kernel, sz, whole), out_shape=shap...]
    ppermute x39, starting transfers between devices: 46.2 us -> 51.8 us  [move(): return lax.ppermute(array, axes, pairs)]
    dot_general x6, matrix products: 10.7 us -> 6.77 us  [dot(): lax.dot_general(left, right, dims, preferred_element_type=jnp.float32)]
    pallas_call x2, Pallas kernels: 4.73 us -> 2.56 us  [pack(): pl.pallas_call(functools.partial(pack_kernel, size), out_shape=jax.ShapeD...]
  transfers between devices with their start and end apart: 39 -> 39, of which waited for: 7 -> 6; matrix products, arithmetic and copies ran while one was open for 6% -> 8% of each run, Pallas kernels for 8% -> 6%
where the time goes in v4:
time: 201 us; the launch traced here: 200 us
  waiting for transfers between devices  100 us (50%)
  starting transfers between devices  51.8 us (26%)
  local copies, waits for them, and re-layouts  15.8 us (8%)
  Pallas kernels  12 us (6%)
  other arithmetic  8.87 us (4%)
  matrix products  6.77 us (3%)
  between operations  4.18 us (2%)
    ppermute x39, waiting for transfers between devices, move(): return lax.ppermute(array, axes, pairs)  100 us
    ppermute x39, starting transfers between devices, move(): return lax.ppermute(array, axes, pairs)  51.8 us
    unnamed x80, local copies, waits for them, and re-layouts  12.6 us
    pallas_call x7, Pallas kernels, chain_step(): pl.pallas_call(functools.partial(chain_kernel, sz, step, forward, (len(re...  7.97 us
    dot_general x6, matrix products, dot(): lax.dot_general(left, right, dims, preferred_element_type=jnp.float32)  6.77 us
  transfers between devices with their start and end apart: 39, of which 6 were waited for; matrix products, arithmetic and copies ran while one was open for 8% of the time, Pallas kernels for 6%

profile of v4, /device:TPU:0, one launch (start us, length us, event | category | flops | bytes accessed | tf_op | source)
XLA Modules:
  0.0 199.7 jit_solution(5063984927124743845)
XLA Ops:
  1.5 4.9 %collective-permute-start = (bf16[128,256]{1,0:T(8,128)(2,1)S(1)}, bf16[128,256]{1,0:T(8,128)(2,1)S(1)}, u32[]{:S(2)}, u32[]{:S(2)}) collective-permute-start(bf16[128,256]{1,0:T(8,128)(2,1)S(1)} %select_bitcast_fusion), channel_id=1, source_target_pairs={{0,1},{1,0},{2,3},{3,2},{12,13},{13,12},{14,15},{15,14},{16,17},{1... | collective-permute-start | bytes 196616 | tf_op jit(solution)/shard_map/ppermute | solution.py:362
  8.7 1.4 copy-done.3
  10.1 1.4 copy-done.5
  12.8 1.6 collective-permute-start.7
  14.7 4.5 %collective-permute-start.1 = (bf16[256,256]{1,0:T(8,128)(2,1)S(1)}, bf16[256,256]{1,0:T(8,128)(2,1)S(1)}, u32[]{:S(2)}, u32[]{:S(2)}) collective-permute-start(bf16[256,256]{1,0:T(8,128)(2,1)S(1)} %pad_maximum_fusion.1.refs_1_.refs_3_), channel_id=1, source_target_pairs={{0,2},{1,3},{2,0},{3,1},{12,14},{13,15},{14,12},{15,13},{16,18},{1... | collective-permute-start | bytes 393224 | tf_op jit(solution)/shard_map/ppermute | solution.py:362
  19.3 4.5 %collective-permute-done.1.refs_2_.refs_4_ = bf16[256,256]{1,0:T(8,128)(2,1)S(1)} collective-permute-done((bf16[256,256]{1,0:T(8,128)(2,1)S(1)}, bf16[256,256]{1,0:T(8,128)(2,1)S(1)}, u32[]{:S(2)}, u32[]{:S(2)}) %collective-permute-start.1) | collective-permute-done | bytes 131104 | tf_op jit(solution)/shard_map/ppermute | solution.py:362
  23.8 3.2 %shard_map.111 = (bf16[128,1024]{1,0:T(8,128)(2,1)}, bf16[128,1024]{1,0:T(8,128)(2,1)S(1)}, f32[6144,1536]{1,0:T(8,128)}) custom-call(s32[6,5]{1,0:T(8,128)S(1)} %fusion.31.refs_0_, bf16[256,256]{1,0:T(8,128)(2,1)S(1)} %pad_maximum_fusion.1.refs_1_.refs_3_, bf16[256,256]{1,0:T(8,128)(2,1)S(1)} %collective-permute-done.1.refs_2_.refs_4_, ...), custom_call_target="tpu_custom_call" | custom-call | flops 805306368 | bytes 6291456 | tf_op jit(solution)/shard_map/pallas_call | solution.py:234
  27.8 1.9 collective-permute-start.2
  29.7 1.8 collective-permute-start.8
  31.5 1.8 collective-permute-start.9
  35.1 4.2 %collective-permute-done.2 = bf16[128,1024]{1,0:T(8,128)(2,1)} collective-permute-done((bf16[128,1024]{1,0:T(8,128)(2,1)}, bf16[128,1024]{1,0:T(8,128)(2,1)}, u32[]{:S(2)}, u32[]{:S(2)}) %collective-permute-start.2) | collective-permute-done | bytes 262176 | tf_op jit(solution)/shard_map/ppermute | solution.py:362
  47.0 1.4 copy-done.7
  49.7 1.8 collective-permute-start.18
  58.8 2.2 %collective-permute-start.30 = (bf16[768,1024]{1,0:T(8,128)(2,1)}, bf16[768,1024]{1,0:T(8,128)(2,1)}, u32[]{:S(2)}, u32[]{:S(2)}) collective-permute-start(bf16[768,1024]{1,0:T(8,128)(2,1)} %shard_map.113), channel_id=1, source_target_pairs={{0,16},{1,17},{2,18},{3,19},{4,20},{5,21},{6,22},{7,23},{16,0},{17... | collective-permute-start | bytes 4718600 | tf_op jit(solution)/shard_map/ppermute | solution.py:362
  69.8 3.6 %collective-permute-start.19 = (bf16[128,1024]{1,0:T(8,128)(2,1)}, bf16[128,1024]{1,0:T(8,128)(2,1)S(1)}, u32[]{:S(2)}, u32[]{:S(2)}) collective-permute-start(bf16[128,1024]{1,0:T(8,128)(2,1)} %copy-done.11), channel_id=1, source_target_pairs={{0,2},{1,3},{2,0},{3,1},{12,14},{13,15},{14,12},{15,13},{16,18},{1... | collective-permute-start | bytes 786440 | tf_op jit(solution)/shard_map/ppermute | solution.py:362
  73.5 10.7 %collective-permute-done.20 = bf16[128,1024]{1,0:T(8,128)(2,1)} collective-permute-done((bf16[128,1024]{1,0:T(8,128)(2,1)}, bf16[128,1024]{1,0:T(8,128)(2,1)}, u32[]{:S(2)}, u32[]{:S(2)}) %collective-permute-start.20) | collective-permute-done | bytes 262176 | tf_op jit(solution)/shard_map/ppermute | solution.py:362
  95.3 3.8 %collective-permute-done.31 = bf16[128,896]{1,0:T(8,128)(2,1)S(1)} collective-permute-done((bf16[128,896]{1,0:T(8,128)(2,1)S(1)}, bf16[128,896]{1,0:T(8,128)(2,1)S(1)}, u32[]{:S(2)}, u32[]{:S(2)}) %collective-permute-start.31) | collective-permute-done | bytes 229408 | tf_op jit(solution)/shard_map/ppermute | solution.py:362
  100.6 1.4 collective-permute-start.32
  107.1 1.6 collective-permute-start.36
  108.8 1.6 broadcast_select_fusion
  110.4 72.2 %collective-permute-done.36 = bf16[128,1024]{1,0:T(8,128)(2,1)S(1)} collective-permute-done((bf16[128,1024]{1,0:T(8,128)(2,1)S(1)}, bf16[128,1024]{1,0:T(8,128)(2,1)S(1)}, u32[]{:S(2)}, u32[]{:S(2)}) %collective-permute-start.36) | collective-permute-done | bytes 262176 | tf_op jit(solution)/shard_map/ppermute | solution.py:362
  184.3 1.8 collective-permute-start.38
  189.1 4.8 %collective-permute-done.37 = bf16[128,768]{1,0:T(8,128)(2,1)S(1)} collective-permute-done((bf16[128,768]{1,0:T(8,128)(2,1)S(1)}, bf16[128,768]{1,0:T(8,128)(2,1)S(1)}, u32[]{:S(2)}, u32[]{:S(2)}) %collective-permute-start.37) | collective-permute-done | bytes 196640 | tf_op jit(solution)/shard_map/ppermute | solution.py:362
  193.9 2.5 %fusion.27 = (bf16[1,1,1024,768]{3,2,1,0:T(8,128)(2,1)S(1)}, bf16[1,1,1024,768]{3,2,1,0:T(8,128)(2,1)S(1)}) fusion(bf16[1,1,1024,768]{3,2,1,0:T(8,128)(2,1)S(1)} %get-tuple-element.136, s32[]{:T(128)S(6)} %select_n.153, bf16[1024,768]{1,0:T(8,128)(2,1)} %collective-permute-done.7, bf16[1,1,1024,768]{3,2,1,0:T(8,128)(2,1)S(1)} %copy-done.6, ...), kind=kOutput, calls=%fused_computation.44 | convolution fusion | flops 108920832 | bytes 5832708 | tf_op jit(solution)/shard_map/dot_general | solution.py:22
  (185 shorter events, 54.8 us)
Async XLA Ops:
  1.5 13.2 %collective-permute-start = (bf16[128,256]{1,0:T(8,128)(2,1)S(1)}, bf16[128,256]{1,0:T(8,128)(2,1)S(1)}, u32[]{:S(2)}, u32[]{:S(2)}) collective-permute-start(bf16[128,256]{1,0:T(8,128)(2,1)S(1)} %select_bitcast_fusion), channel_id=1, source_target_pairs={{0,1},{1,0},{2,3},{3,2},{12,13},{13,12},{14,15},{15,14},{16,17},{1... | collective-permute-start | bytes 196616 | tf_op jit(solution)/shard_map/ppermute | solution.py:362
  12.8 36.8 %collective-permute-start.7 = (bf16[1024,768]{1,0:T(8,128)(2,1)}, bf16[1024,768]{1,0:T(8,128)(2,1)}, u32[]{:S(2)}, u32[]{:S(2)}) collective-permute-start(bf16[1024,768]{1,0:T(8,128)(2,1)} %shard_map.112), channel_id=1, source_target_pairs={{0,16},{1,17},{2,18},{3,19},{4,20},{5,21},{6,22},{7,23},{8,24},{9,... | collective-permute-start | bytes 4718600 | tf_op jit(solution)/shard_map/ppermute | solution.py:362
  14.7 9.1 %collective-permute-start.1 = (bf16[256,256]{1,0:T(8,128)(2,1)S(1)}, bf16[256,256]{1,0:T(8,128)(2,1)S(1)}, u32[]{:S(2)}, u32[]{:S(2)}) collective-permute-start(bf16[256,256]{1,0:T(8,128)(2,1)S(1)} %pad_maximum_fusion.1.refs_1_.refs_3_), channel_id=1, source_target_pairs={{0,2},{1,3},{2,0},{3,1},{12,14},{13,15},{14,12},{15,13},{16,18},{1... | collective-permute-start | bytes 393224 | tf_op jit(solution)/shard_map/ppermute | solution.py:362
  27.8 11.4 %collective-permute-start.2 = (bf16[128,1024]{1,0:T(8,128)(2,1)}, bf16[128,1024]{1,0:T(8,128)(2,1)}, u32[]{:S(2)}, u32[]{:S(2)}) collective-permute-start(bf16[128,1024]{1,0:T(8,128)(2,1)} %get-tuple-element.66), channel_id=1, source_target_pairs={{0,1},{1,0},{2,3},{3,2},{12,13},{13,12},{14,15},{15,14},{16,17},{1... | collective-permute-start | bytes 786440 | tf_op jit(solution)/shard_map/ppermute | solution.py:362
  29.7 21.8 %collective-permute-start.8 = (bf16[1024,768]{1,0:T(8,128)(2,1)S(1)}, bf16[1024,768]{1,0:T(8,128)(2,1)}, u32[]{:S(2)}, u32[]{:S(2)}) collective-permute-start(bf16[1024,768]{1,0:T(8,128)(2,1)S(1)} %bitcast.85), channel_id=1, source_target_pairs={{5,4},{7,6},{9,8},{11,10},{12,13},{14,15},{21,20},{23,22},{25,24},... | collective-permute-start | bytes 4718600 | tf_op jit(solution)/shard_map/ppermute | solution.py:362
  31.5 20.0 %collective-permute-start.9 = (bf16[768,1024]{1,0:T(8,128)(2,1)S(1)}, bf16[768,1024]{1,0:T(8,128)(2,1)}, u32[]{:S(2)}, u32[]{:S(2)}) collective-permute-start(bf16[768,1024]{1,0:T(8,128)(2,1)S(1)} %bitcast.74), channel_id=1, source_target_pairs={{5,4},{7,6},{9,8},{11,10},{12,13},{14,15},{21,20},{23,22},{25,24},... | collective-permute-start | bytes 4718600 | tf_op jit(solution)/shard_map/ppermute | solution.py:362
  42.4 7.3 %collective-permute-start.5 = (bf16[64,1024]{1,0:T(8,128)(2,1)}, bf16[64,1024]{1,0:T(8,128)(2,1)}, u32[]{:S(2)}, u32[]{:S(2)}) collective-permute-start(bf16[64,1024]{1,0:T(8,128)(2,1)} %get-tuple-element.138), channel_id=1, source_target_pairs={{1,20},{3,22},{17,4},{19,6}} | collective-permute-start | bytes 393224 | tf_op jit(solution)/shard_map/ppermute | solution.py:362
  44.3 5.3 %collective-permute-start.6 = (bf16[64,1024]{1,0:T(8,128)(2,1)}, bf16[64,1024]{1,0:T(8,128)(2,1)}, u32[]{:S(2)}, u32[]{:S(2)}) collective-permute-start(bf16[64,1024]{1,0:T(8,128)(2,1)} %get-tuple-element.138), channel_id=1, source_target_pairs={{1,22},{3,20},{17,6},{19,4}} | collective-permute-start | bytes 393224 | tf_op jit(solution)/shard_map/ppermute | solution.py:362
  49.7 16.5 %collective-permute-start.18 = (bf16[768,1024]{1,0:T(8,128)(2,1)}, bf16[768,1024]{1,0:T(8,128)(2,1)}, u32[]{:S(2)}, u32[]{:S(2)}) collective-permute-start(bf16[768,1024]{1,0:T(8,128)(2,1)} %shard_map.113), channel_id=1, source_target_pairs={{8,24},{9,25},{10,26},{11,27},{12,28},{13,29},{14,30},{15,31},{24,... | collective-permute-start | bytes 4718600 | tf_op jit(solution)/shard_map/ppermute | solution.py:362
  58.1 5.5 %collective-permute-start.14 = (bf16[64,1024]{1,0:T(8,128)(2,1)}, bf16[64,1024]{1,0:T(8,128)(2,1)S(1)}, u32[]{:S(2)}, u32[]{:S(2)}) collective-permute-start(bf16[64,1024]{1,0:T(8,128)(2,1)} %get-tuple-element.88), channel_id=1, source_target_pairs={{8,13},{10,15},{24,29},{26,31}} | collective-permute-start | bytes 393224 | tf_op jit(solution)/shard_map/ppermute | solution.py:362
  58.8 35.8 %collective-permute-start.30 = (bf16[768,1024]{1,0:T(8,128)(2,1)}, bf16[768,1024]{1,0:T(8,128)(2,1)}, u32[]{:S(2)}, u32[]{:S(2)}) collective-permute-start(bf16[768,1024]{1,0:T(8,128)(2,1)} %shard_map.113), channel_id=1, source_target_pairs={{0,16},{1,17},{2,18},{3,19},{4,20},{5,21},{6,22},{7,23},{16,0},{17... | collective-permute-start | bytes 4718600 | tf_op jit(solution)/shard_map/ppermute | solution.py:362
  61.0 3.9 %collective-permute-start.15 = (bf16[64,1024]{1,0:T(8,128)(2,1)}, bf16[64,1024]{1,0:T(8,128)(2,1)}, u32[]{:S(2)}, u32[]{:S(2)}) collective-permute-start(bf16[64,1024]{1,0:T(8,128)(2,1)} %get-tuple-element.88), channel_id=1, source_target_pairs={{8,15},{10,13},{24,31},{26,29}} | collective-permute-start | bytes 393224 | tf_op jit(solution)/shard_map/ppermute | solution.py:362
  64.9 19.3 %collective-permute-start.20 = (bf16[128,1024]{1,0:T(8,128)(2,1)}, bf16[128,1024]{1,0:T(8,128)(2,1)}, u32[]{:S(2)}, u32[]{:S(2)}) collective-permute-start(bf16[128,1024]{1,0:T(8,128)(2,1)} %broadcast_select_fusion.2), channel_id=1, source_target_pairs={{1,0},{3,2},{4,5},{6,7},{17,16},{19,18},{20,21},{22,23}} | collective-permute-start | bytes 786440 | tf_op jit(solution)/shard_map/ppermute | solution.py:362
  68.5 15.7 %collective-permute-start.21 = (bf16[128,1024]{1,0:T(8,128)(2,1)}, bf16[128,1024]{1,0:T(8,128)(2,1)}, u32[]{:S(2)}, u32[]{:S(2)}) collective-permute-start(bf16[128,1024]{1,0:T(8,128)(2,1)} %select_select_fusion), channel_id=1, source_target_pairs={{8,9},{10,11},{13,12},{15,14},{24,25},{26,27},{29,28},{31,30}} | collective-permute-start | bytes 786440 | tf_op jit(solution)/shard_map/ppermute | solution.py:362
  69.8 16.1 %collective-permute-start.19 = (bf16[128,1024]{1,0:T(8,128)(2,1)}, bf16[128,1024]{1,0:T(8,128)(2,1)S(1)}, u32[]{:S(2)}, u32[]{:S(2)}) collective-permute-start(bf16[128,1024]{1,0:T(8,128)(2,1)} %copy-done.11), channel_id=1, source_target_pairs={{0,2},{1,3},{2,0},{3,1},{12,14},{13,15},{14,12},{15,13},{16,18},{1... | collective-permute-start | bytes 786440 | tf_op jit(solution)/shard_map/ppermute | solution.py:362
  90.5 8.6 %collective-permute-start.31 = (bf16[128,896]{1,0:T(8,128)(2,1)S(1)}, bf16[128,896]{1,0:T(8,128)(2,1)S(1)}, u32[]{:S(2)}, u32[]{:S(2)}) collective-permute-start(bf16[128,896]{1,0:T(8,128)(2,1)S(1)} %pad_maximum_fusion), channel_id=1, source_target_pairs={{0,16},{1,17},{2,18},{3,19},{4,20},{5,21},{6,22},{7,23},{8,24},{9,... | collective-permute-start | bytes 688136 | tf_op jit(solution)/shard_map/ppermute | solution.py:362
  92.6 6.5 %collective-permute-start.26 = (bf16[64,1024]{1,0:T(8,128)(2,1)S(1)}, bf16[64,1024]{1,0:T(8,128)(2,1)S(1)}, u32[]{:S(2)}, u32[]{:S(2)}) collective-permute-start(bf16[64,1024]{1,0:T(8,128)(2,1)S(1)} %get-tuple-element.109), channel_id=1, source_target_pairs={{8,4},{10,6},{24,20},{26,22}} | collective-permute-start | bytes 393224 | tf_op jit(solution)/shard_map/ppermute | solution.py:362
  93.2 5.9 %collective-permute-start.27 = (bf16[64,1024]{1,0:T(8,128)(2,1)S(1)}, bf16[64,1024]{1,0:T(8,128)(2,1)S(1)}, u32[]{:S(2)}, u32[]{:S(2)}) collective-permute-start(bf16[64,1024]{1,0:T(8,128)(2,1)S(1)} %get-tuple-element.109), channel_id=1, source_target_pairs={{8,6},{10,4},{24,22},{26,20}} | collective-permute-start | bytes 393224 | tf_op jit(solution)/shard_map/ppermute | solution.py:362
  93.9 5.2 %collective-permute-start.28 = (bf16[64,1024]{1,0:T(8,128)(2,1)S(1)}, bf16[64,1024]{1,0:T(8,128)(2,1)S(1)}, u32[]{:S(2)}, u32[]{:S(2)}) collective-permute-start(bf16[64,1024]{1,0:T(8,128)(2,1)S(1)} %get-tuple-element.110), channel_id=1, source_target_pairs={{8,20},{10,22},{24,4},{26,6}} | collective-permute-start | bytes 393224 | tf_op jit(solution)/shard_map/ppermute | solution.py:362
  94.6 4.5 %collective-permute-start.29 = (bf16[64,1024]{1,0:T(8,128)(2,1)S(1)}, bf16[64,1024]{1,0:T(8,128)(2,1)S(1)}, u32[]{:S(2)}, u32[]{:S(2)}) collective-permute-start(bf16[64,1024]{1,0:T(8,128)(2,1)S(1)} %get-tuple-element.110), channel_id=1, source_target_pairs={{8,22},{10,20},{24,6},{26,4}} | collective-permute-start | bytes 393224 | tf_op jit(solution)/shard_map/ppermute | solution.py:362
  100.6 4.2 %collective-permute-start.32 = (bf16[64,1024]{1,0:T(8,128)(2,1)}, bf16[64,1024]{1,0:T(8,128)(2,1)}, u32[]{:S(2)}, u32[]{:S(2)}) collective-permute-start(bf16[64,1024]{1,0:T(8,128)(2,1)} %get-tuple-element.118), channel_id=1, source_target_pairs={{4,1},{6,3},{20,17},{22,19}} | collective-permute-start | bytes 393224 | tf_op jit(solution)/shard_map/ppermute | solution.py:362
  107.1 75.5 %collective-permute-start.36 = (bf16[128,1024]{1,0:T(8,128)(2,1)S(1)}, bf16[128,1024]{1,0:T(8,128)(2,1)S(1)}, u32[]{:S(2)}, u32[]{:S(2)}) collective-permute-start(bf16[128,1024]{1,0:T(8,128)(2,1)S(1)} %fusion.28), channel_id=1, source_target_pairs={{1,0},{3,2},{4,5},{6,7},{8,9},{10,11},{13,12},{15,14},{17,16},{19,... | collective-permute-start | bytes 786440 | tf_op jit(solution)/shard_map/ppermute | solution.py:362
  184.3 12.1 %collective-permute-start.38 = (bf16[128,1024]{1,0:T(8,128)(2,1)S(1)}, bf16[128,1024]{1,0:T(8,128)(2,1)S(1)}, u32[]{:S(2)}, u32[]{:S(2)}) collective-permute-start(bf16[128,1024]{1,0:T(8,128)(2,1)S(1)} %broadcast_select_fusion.1.refs_0_), channel_id=1, source_target_pairs={{0,16},{1,17},{2,18},{3,19},{4,20},{5,21},{6,22},{7,23},{8,24},{9,... | collective-permute-start | bytes 786440 | tf_op jit(solution)/shard_map/ppermute | solution.py:362
  188.1 5.7 %collective-permute-start.37 = (bf16[128,768]{1,0:T(8,128)(2,1)S(1)}, bf16[128,768]{1,0:T(8,128)(2,1)S(1)}, u32[]{:S(2)}, u32[]{:S(2)}) collective-permute-start(bf16[128,768]{1,0:T(8,128)(2,1)S(1)} %shard_map.121), channel_id=1, source_target_pairs={{0,16},{1,17},{2,18},{3,19},{4,20},{5,21},{6,22},{7,23},{8,24},{9,... | collective-permute-start | bytes 589832 | tf_op jit(solution)/shard_map/ppermute | solution.py:362
  (55 other events, 381.2 us)

commit v5 on v4

--- a/solution.py
+++ b/solution.py
@@ -81,6 +81,10 @@
         self.scale_out = 1.0 / math.sqrt(hidden_total)
 
 
+def kept_place(sz, step, forward):
+    return (step if forward else sz.sections + step) * sz.row_count
+
+
 def chain_kernel(sz, step, forward, counts, *refs):
     refs = list(refs)
 
@@ -93,9 +97,9 @@
     parts = 1 if first else 2
     (table,) = take(1)
     received, edges, sources = take(counts[0]), take(counts[1]), take(2 * parts)
-    take(0 if first else 1)
+    take(0 if first else 2)
     sends = take(counts[2])
-    fresh_hbm, state = take(2)
+    kept, state = take(2)
     weights_in, weights_out, landing, rows, up, out, slope, wide_store = take(8)
     weight_sems, block_sems, edge_sems, send_sems, state_sems = take(5)
     panel, width, hidden_size = sz.panel, sz.width, sz.local_hidden
@@ -114,6 +118,7 @@
     def state_part(k, columns):
         return state.at[pl.ds(k * sz.row_count, sz.row_count), pl.ds(0, columns)]
 
+    fresh_hbm = kept.at[pl.ds(kept_place(sz, step, forward), sz.row_count)]
     rows_hbm, slope_hbm = state_part(0, width), state_part(1, 2 * hidden_size)
 
     @pl.when(table[links + 1, step] == 1)
@@ -137,17 +142,16 @@
             )
         if not forward:
             first_copies.append(pltpu.make_async_copy(rows_hbm, wide_store, state_sems.at[0]))
-            first_copies.append(pltpu.make_async_copy(slope_hbm, slope, state_sems.at[1]))
+            slope_copy = pltpu.make_async_copy(slope_hbm, slope, state_sems.at[1])
         for copy in first_copies:
             copy.start()
-        for item in sequence[:2]:
+        for i, item in enumerate(sequence):
             weight_copy(*item).start()
+            if i == 0 and not forward:
+                slope_copy.start()
 
         def arrived(item):
             weight_copy(*item).wait()
-            later = sequence.index(item) + 2
-            if later < len(sequence):
-                weight_copy(*sequence[later]).start()
 
         for copy in first_copies:
             copy.wait()
@@ -198,6 +202,8 @@
             for d in range(parts):
                 arrived((d, 1))
                 grad_hidden = dot(weights_out[d], up_turned)
+                if d == 0:
+                    slope_copy.wait()
                 local_slope = slope[:, d * hidden_size : (d + 1) * hidden_size].T
                 grad_pre = (grad_hidden * sz.scale_out * local_slope).astype(jnp.bfloat16)
                 arrived((d, 0))
@@ -220,15 +226,16 @@
             copy.wait()
 
 
-def chain_step(sz, step, forward, table, received, edges, weights, state):
+def chain_step(sz, step, forward, table, received, edges, weights, stores):
     first = forward and step == 0
     count = 1 if forward and step in (0, sz.sections - 1) else sz.blocks
     anywhere = pl.BlockSpec(memory_space=pl.ANY)
-    operands = [table, *received, *edges, *(weights[:2] if first else [*weights, state])]
+    operands = [table, *received, *edges, *(weights[:2] if first else [*weights, *stores])]
     block = jax.ShapeDtypeStruct((sz.row_count // count, sz.width), jnp.bfloat16)
-    kept = jax.ShapeDtypeStruct((48 * sz.row_count, 2 * sz.local_hidden), jnp.float32)
-    fresh = jax.ShapeDtypeStruct((sz.row_count, sz.width), jnp.bfloat16)
-    shapes = [block] * count + [fresh, kept]
+    shapes = [block] * count + [
+        jax.ShapeDtypeStruct((144 * sz.row_count, sz.width), jnp.bfloat16),
+        jax.ShapeDtypeStruct((48 * sz.row_count, 2 * sz.local_hidden), jnp.float32),
+    ]
     in_specs = [pl.BlockSpec(memory_space=pltpu.SMEM)] + [anywhere] * (len(operands) - 1)
     whole = (sz.row_count, sz.width)
     results = pl.pallas_call(
@@ -238,7 +245,9 @@
         out_shape=shapes,
         in_specs=in_specs,
         out_specs=[anywhere] * len(shapes),
-        input_output_aliases={} if first else {len(operands) - 1: count + 1},
+        input_output_aliases=(
+            {} if first else {len(operands) - 2: count, len(operands) - 1: count + 1}
+        ),
         scratch_shapes=[
             pltpu.VMEM((2, sz.width, sz.local_hidden), jnp.bfloat16),
             pltpu.VMEM((2, sz.local_hidden, sz.width), jnp.bfloat16),
@@ -261,7 +270,7 @@
             transcendentals=0,
         ),
     )(*operands)
-    return list(results[:count]), results[count], results[count + 1]
+    return list(results[:count]), list(results[count:])
 
 
 def share_kernel(sz, whole, *refs):
@@ -470,6 +479,13 @@
                 moved[a] = lax.dynamic_update_index_in_dim(moved[a], got, arrived[e], 0)
         return [one.reshape(row_count, width) for one in moved]
 
+    def kept_of(stores, steps, forward):
+        places = [kept_place(sz, step, forward) for step in steps]
+        result = stores[0][places[0] : places[0] + row_count]
+        for step, place in zip(steps[1:], places[1:]):
+            result = jnp.where(section_id == step, stores[0][place : place + row_count], result)
+        return result
+
     row_parts = []
 
     def spread_rows(received, rows, active):
@@ -486,12 +502,13 @@
         return jnp.concatenate(parts, axis=1)
 
     weights = [weight_in, weight_out, *near]
-    received, state = [], None
+    received, stores = [], []
     for step in every:
-        sends, fresh, state = chain_step(
-            sz, step, True, table, received, edges if step == 0 else [], weights, state
-        )
-        rows = fresh if step == 0 else jnp.where(section_id == step, fresh, rows)
+        sends, stores = chain_step(
+            sz, step, True, table, received, edges if step == 0 else [], weights, stores
+        )
+        if step in (len(late) - 1, links):
+            rows = kept_of(stores, range(step + 1), True)
         if step == 0:
             total = sends[0].astype(jnp.float32)
             total = total + at_ends(sends[0], 1).astype(jnp.float32)
@@ -523,10 +540,9 @@
             received, far_states_out = lax.optimization_barrier((received, far_states_out))
 
     for step in reversed(range(1, sections)):
-        sends, fresh, state = chain_step(
-            sz, step, False, table, received, edges if step == links else [], weights, state
-        )
-        upstream = fresh if step == links else jnp.where(section_id == step, fresh, upstream)
+        sends, stores = chain_step(
+            sz, step, False, table, received, edges if step == links else [], weights, stores
+        )
         received = send_blocks(sends, slots[step - 1], back, step, -1)
         if step == len(late):
             received, far_late, bundles = lax.optimization_barrier(
@@ -547,7 +563,7 @@
                 )
         halves.append(half.astype(jnp.float32))
     first_up = (halves[0] + halves[1]).astype(jnp.bfloat16)
-    upstream = jnp.where(section_id == 0, first_up, upstream)
+    upstream = jnp.where(section_id == 0, first_up, kept_of(stores, rest, False))
     upstream = jnp.where(is_holder, upstream, from_holders(upstream, 1, every))
     far_up = exchange([upstream] * len(others), every)
     (grad_pre,) = share_call(sz, [upstream, slope], weight_out)

time: 201 us -> 197 us (0.980)
  local copies, waits for them, and re-layouts: 15.8 us -> 12 us
  other arithmetic: 8.87 us -> 12.5 us
  waiting for transfers between devices: 100 us -> 96.5 us
    unnamed x80 -> x54, local copies, waits for them, and re-layouts: 12.6 us -> 8.79 us
    ppermute x39, waiting for transfers between devices: 100 us -> 96.5 us  [move(): return lax.ppermute(array, axes, pairs)]
    select_n x3, other arithmetic: 1.7 us -> 5.05 us  [the longest x2 3.7 us: kept_of(): jnp.where(section_id == step, stores[0][place:place + row_count], result)]
  transfers between devices with their start and end apart: 39 -> 39, of which waited for: 6 -> 6; matrix products, arithmetic and copies ran while one was open for 8% -> 9% of each run, Pallas kernels for 6% -> 6%
where the time goes in v5:
time: 197 us; the launch traced here: 196 us
  waiting for transfers between devices  96.5 us (49%)
  starting transfers between devices  52 us (26%)
  other arithmetic  12.5 us (6%)
  local copies, waits for them, and re-layouts  12 us (6%)
  Pallas kernels  11.6 us (6%)
  matrix products  6.76 us (3%)
  between operations  4.04 us (2%)
    ppermute x39, waiting for transfers between devices, move(): return lax.ppermute(array, axes, pairs)  96.5 us
    ppermute x39, starting transfers between devices, move(): return lax.ppermute(array, axes, pairs)  52 us
    unnamed x54, local copies, waits for them, and re-layouts  8.79 us
    pallas_call x7, Pallas kernels, chain_step(): pl.pallas_call(functools.partial(chain_kernel, sz, step, forward, (len(re...  7.6 us
    dot_general x6, matrix products, dot(): lax.dot_general(left, right, dims, preferred_element_type=jnp.float32)  6.76 us
  transfers between devices with their start and end apart: 39, of which 6 were waited for; matrix products, arithmetic and copies ran while one was open for 9% of the time, Pallas kernels for 6%

profile of v5, /device:TPU:0, one launch (start us, length us, event | category | flops | bytes accessed | tf_op | source)
XLA Modules:
  0.0 195.5 jit_solution(4147607071218959085)
XLA Ops:
  1.5 4.9 %collective-permute-start = (bf16[128,256]{1,0:T(8,128)(2,1)S(1)}, bf16[128,256]{1,0:T(8,128)(2,1)S(1)}, u32[]{:S(2)}, u32[]{:S(2)}) collective-permute-start(bf16[128,256]{1,0:T(8,128)(2,1)S(1)} %select_bitcast_fusion), channel_id=1, source_target_pairs={{0,1},{1,0},{2,3},{3,2},{12,13},{13,12},{14,15},{15,14},{16,17},{1... | collective-permute-start | bytes 196616 | tf_op jit(solution)/shard_map/ppermute | solution.py:371
  10.1 1.4 copy-done.5
  12.8 1.6 collective-permute-start.7
  14.7 4.5 %collective-permute-start.1 = (bf16[256,256]{1,0:T(8,128)(2,1)S(1)}, bf16[256,256]{1,0:T(8,128)(2,1)S(1)}, u32[]{:S(2)}, u32[]{:S(2)}) collective-permute-start(bf16[256,256]{1,0:T(8,128)(2,1)S(1)} %pad_maximum_fusion.1.refs_1_.refs_3_), channel_id=1, source_target_pairs={{0,2},{1,3},{2,0},{3,1},{12,14},{13,15},{14,12},{15,13},{16,18},{1... | collective-permute-start | bytes 393224 | tf_op jit(solution)/shard_map/ppermute | solution.py:371
  19.3 4.6 %collective-permute-done.1.refs_2_.refs_4_ = bf16[256,256]{1,0:T(8,128)(2,1)S(1)} collective-permute-done((bf16[256,256]{1,0:T(8,128)(2,1)S(1)}, bf16[256,256]{1,0:T(8,128)(2,1)S(1)}, u32[]{:S(2)}, u32[]{:S(2)}) %collective-permute-start.1) | collective-permute-done | bytes 131104 | tf_op jit(solution)/shard_map/ppermute | solution.py:371
  23.9 2.9 %shard_map.111 = (bf16[128,1024]{1,0:T(8,128)(2,1)}, bf16[18432,1024]{1,0:T(8,128)(2,1)}, f32[6144,1536]{1,0:T(8,128)}) custom-call(s32[6,5]{1,0:T(8,128)S(1)} %fusion.31.refs_0_, bf16[256,256]{1,0:T(8,128)(2,1)S(1)} %pad_maximum_fusion.1.refs_1_.refs_3_, bf16[256,256]{1,0:T(8,128)(2,1)S(1)} %collective-permute-done.1.refs_2_.refs_4_, ...), custom_call_target="tpu_custom_call" | custom-call | flops 805306368 | bytes 6291456 | tf_op jit(solution)/shard_map/pallas_call | solution.py:241
  26.8 2.3 %collective-permute-start.2 = (bf16[128,1024]{1,0:T(8,128)(2,1)}, bf16[128,1024]{1,0:T(8,128)(2,1)}, u32[]{:S(2)}, u32[]{:S(2)}) collective-permute-start(bf16[128,1024]{1,0:T(8,128)(2,1)} %get-tuple-element.66), channel_id=1, source_target_pairs={{0,1},{1,0},{2,3},{3,2},{12,13},{13,12},{14,15},{15,14},{16,17},{1... | collective-permute-start | bytes 786440 | tf_op jit(solution)/shard_map/ppermute | solution.py:371
  29.1 1.9 collective-permute-start.8
  31.0 1.8 collective-permute-start.9
  34.7 3.6 %collective-permute-done.2 = bf16[128,1024]{1,0:T(8,128)(2,1)} collective-permute-done((bf16[128,1024]{1,0:T(8,128)(2,1)}, bf16[128,1024]{1,0:T(8,128)(2,1)}, u32[]{:S(2)}, u32[]{:S(2)}) %collective-permute-start.2) | collective-permute-done | bytes 262176 | tf_op jit(solution)/shard_map/ppermute | solution.py:371
  48.6 1.8 collective-permute-start.18
  54.9 1.8 slice_select_fusion
  58.1 2.2 %collective-permute-start.30 = (bf16[768,1024]{1,0:T(8,128)(2,1)}, bf16[768,1024]{1,0:T(8,128)(2,1)}, u32[]{:S(2)}, u32[]{:S(2)}) collective-permute-start(bf16[768,1024]{1,0:T(8,128)(2,1)} %shard_map.113), channel_id=1, source_target_pairs={{0,16},{1,17},{2,18},{3,19},{4,20},{5,21},{6,22},{7,23},{16,0},{17... | collective-permute-start | bytes 4718600 | tf_op jit(solution)/shard_map/ppermute | solution.py:371
  67.0 1.9 select_select_fusion
  70.3 3.7 %collective-permute-start.19 = (bf16[128,1024]{1,0:T(8,128)(2,1)}, bf16[128,1024]{1,0:T(8,128)(2,1)S(1)}, u32[]{:S(2)}, u32[]{:S(2)}) collective-permute-start(bf16[128,1024]{1,0:T(8,128)(2,1)} %copy-done.11), channel_id=1, source_target_pairs={{0,2},{1,3},{2,0},{3,1},{12,14},{13,15},{14,12},{15,13},{16,18},{1... | collective-permute-start | bytes 786440 | tf_op jit(solution)/shard_map/ppermute | solution.py:371
  74.0 9.3 %collective-permute-done.20 = bf16[128,1024]{1,0:T(8,128)(2,1)} collective-permute-done((bf16[128,1024]{1,0:T(8,128)(2,1)}, bf16[128,1024]{1,0:T(8,128)(2,1)}, u32[]{:S(2)}, u32[]{:S(2)}) %collective-permute-start.20) | collective-permute-done | bytes 262176 | tf_op jit(solution)/shard_map/ppermute | solution.py:371
  83.3 1.4 add_select_fusion.refs_0_
  93.1 4.8 %collective-permute-done.31 = bf16[128,896]{1,0:T(8,128)(2,1)S(1)} collective-permute-done((bf16[128,896]{1,0:T(8,128)(2,1)S(1)}, bf16[128,896]{1,0:T(8,128)(2,1)S(1)}, u32[]{:S(2)}, u32[]{:S(2)}) %collective-permute-start.31) | collective-permute-done | bytes 229408 | tf_op jit(solution)/shard_map/ppermute | solution.py:371
  106.0 1.6 collective-permute-start.36
  107.7 1.6 broadcast_select_fusion
  109.3 70.1 %collective-permute-done.36 = bf16[128,1024]{1,0:T(8,128)(2,1)S(1)} collective-permute-done((bf16[128,1024]{1,0:T(8,128)(2,1)S(1)}, bf16[128,1024]{1,0:T(8,128)(2,1)S(1)}, u32[]{:S(2)}, u32[]{:S(2)}) %collective-permute-start.36) | collective-permute-done | bytes 262176 | tf_op jit(solution)/shard_map/ppermute | solution.py:371
  183.8 1.6 collective-permute-start.37
  185.7 4.0 %collective-permute-done.37 = bf16[128,768]{1,0:T(8,128)(2,1)S(1)} collective-permute-done((bf16[128,768]{1,0:T(8,128)(2,1)S(1)}, bf16[128,768]{1,0:T(8,128)(2,1)S(1)}, u32[]{:S(2)}, u32[]{:S(2)}) %collective-permute-start.37) | collective-permute-done | bytes 196640 | tf_op jit(solution)/shard_map/ppermute | solution.py:371
  189.7 2.5 %fusion.27 = (bf16[1,1,1024,768]{3,2,1,0:T(8,128)(2,1)S(1)}, bf16[1,1,1024,768]{3,2,1,0:T(8,128)(2,1)S(1)}) fusion(bf16[1,1,1024,768]{3,2,1,0:T(8,128)(2,1)S(1)} %get-tuple-element.136, s32[]{:T(128)S(6)} %select_n.158, bf16[1024,768]{1,0:T(8,128)(2,1)} %collective-permute-done.7, bf16[1,1,1024,768]{3,2,1,0:T(8,128)(2,1)S(1)} %copy-done.6, ...), kind=kOutput, calls=%fused_computation.44 | convolution fusion | flops 108920832 | bytes 5832708 | tf_op jit(solution)/shard_map/dot_general | solution.py:22
  (159 shorter events, 53.7 us)
Async XLA Ops:
  1.5 13.2 %collective-permute-start = (bf16[128,256]{1,0:T(8,128)(2,1)S(1)}, bf16[128,256]{1,0:T(8,128)(2,1)S(1)}, u32[]{:S(2)}, u32[]{:S(2)}) collective-permute-start(bf16[128,256]{1,0:T(8,128)(2,1)S(1)} %select_bitcast_fusion), channel_id=1, source_target_pairs={{0,1},{1,0},{2,3},{3,2},{12,13},{13,12},{14,15},{15,14},{16,17},{1... | collective-permute-start | bytes 196616 | tf_op jit(solution)/shard_map/ppermute | solution.py:371
  12.8 35.8 %collective-permute-start.7 = (bf16[1024,768]{1,0:T(8,128)(2,1)}, bf16[1024,768]{1,0:T(8,128)(2,1)}, u32[]{:S(2)}, u32[]{:S(2)}) collective-permute-start(bf16[1024,768]{1,0:T(8,128)(2,1)} %shard_map.112), channel_id=1, source_target_pairs={{0,16},{1,17},{2,18},{3,19},{4,20},{5,21},{6,22},{7,23},{8,24},{9,... | collective-permute-start | bytes 4718600 | tf_op jit(solution)/shard_map/ppermute | solution.py:371
  14.7 9.2 %collective-permute-start.1 = (bf16[256,256]{1,0:T(8,128)(2,1)S(1)}, bf16[256,256]{1,0:T(8,128)(2,1)S(1)}, u32[]{:S(2)}, u32[]{:S(2)}) collective-permute-start(bf16[256,256]{1,0:T(8,128)(2,1)S(1)} %pad_maximum_fusion.1.refs_1_.refs_3_), channel_id=1, source_target_pairs={{0,2},{1,3},{2,0},{3,1},{12,14},{13,15},{14,12},{15,13},{16,18},{1... | collective-permute-start | bytes 393224 | tf_op jit(solution)/shard_map/ppermute | solution.py:371
  26.8 11.5 %collective-permute-start.2 = (bf16[128,1024]{1,0:T(8,128)(2,1)}, bf16[128,1024]{1,0:T(8,128)(2,1)}, u32[]{:S(2)}, u32[]{:S(2)}) collective-permute-start(bf16[128,1024]{1,0:T(8,128)(2,1)} %get-tuple-element.66), channel_id=1, source_target_pairs={{0,1},{1,0},{2,3},{3,2},{12,13},{13,12},{14,15},{15,14},{16,17},{1... | collective-permute-start | bytes 786440 | tf_op jit(solution)/shard_map/ppermute | solution.py:371
  29.1 21.3 %collective-permute-start.8 = (bf16[1024,768]{1,0:T(8,128)(2,1)S(1)}, bf16[1024,768]{1,0:T(8,128)(2,1)}, u32[]{:S(2)}, u32[]{:S(2)}) collective-permute-start(bf16[1024,768]{1,0:T(8,128)(2,1)S(1)} %bitcast.85), channel_id=1, source_target_pairs={{5,4},{7,6},{9,8},{11,10},{12,13},{14,15},{21,20},{23,22},{25,24},... | collective-permute-start | bytes 4718600 | tf_op jit(solution)/shard_map/ppermute | solution.py:371
  31.0 19.4 %collective-permute-start.9 = (bf16[768,1024]{1,0:T(8,128)(2,1)S(1)}, bf16[768,1024]{1,0:T(8,128)(2,1)}, u32[]{:S(2)}, u32[]{:S(2)}) collective-permute-start(bf16[768,1024]{1,0:T(8,128)(2,1)S(1)} %bitcast.74), channel_id=1, source_target_pairs={{5,4},{7,6},{9,8},{11,10},{12,13},{14,15},{21,20},{23,22},{25,24},... | collective-permute-start | bytes 4718600 | tf_op jit(solution)/shard_map/ppermute | solution.py:371
  41.4 7.2 %collective-permute-start.5 = (bf16[64,1024]{1,0:T(8,128)(2,1)}, bf16[64,1024]{1,0:T(8,128)(2,1)}, u32[]{:S(2)}, u32[]{:S(2)}) collective-permute-start(bf16[64,1024]{1,0:T(8,128)(2,1)} %get-tuple-element.138), channel_id=1, source_target_pairs={{1,20},{3,22},{17,4},{19,6}} | collective-permute-start | bytes 393224 | tf_op jit(solution)/shard_map/ppermute | solution.py:371
  43.4 5.2 %collective-permute-start.6 = (bf16[64,1024]{1,0:T(8,128)(2,1)}, bf16[64,1024]{1,0:T(8,128)(2,1)}, u32[]{:S(2)}, u32[]{:S(2)}) collective-permute-start(bf16[64,1024]{1,0:T(8,128)(2,1)} %get-tuple-element.138), channel_id=1, source_target_pairs={{1,22},{3,20},{17,6},{19,4}} | collective-permute-start | bytes 393224 | tf_op jit(solution)/shard_map/ppermute | solution.py:371
  48.6 16.9 %collective-permute-start.18 = (bf16[768,1024]{1,0:T(8,128)(2,1)}, bf16[768,1024]{1,0:T(8,128)(2,1)}, u32[]{:S(2)}, u32[]{:S(2)}) collective-permute-start(bf16[768,1024]{1,0:T(8,128)(2,1)} %shard_map.113), channel_id=1, source_target_pairs={{8,24},{9,25},{10,26},{11,27},{12,28},{13,29},{14,30},{15,31},{24,... | collective-permute-start | bytes 4718600 | tf_op jit(solution)/shard_map/ppermute | solution.py:371
  52.1 4.5 %collective-permute-start.10 = (bf16[64,1024]{1,0:T(8,128)(2,1)S(1)}, bf16[64,1024]{1,0:T(8,128)(2,1)S(1)}, u32[]{:S(2)}, u32[]{:S(2)}) collective-permute-start(bf16[64,1024]{1,0:T(8,128)(2,1)S(1)} %get-tuple-element.75), channel_id=1, source_target_pairs={{4,8},{6,10},{20,24},{22,26}} | collective-permute-start | bytes 393224 | tf_op jit(solution)/shard_map/ppermute | solution.py:371
  57.4 5.5 %collective-permute-start.14 = (bf16[64,1024]{1,0:T(8,128)(2,1)}, bf16[64,1024]{1,0:T(8,128)(2,1)S(1)}, u32[]{:S(2)}, u32[]{:S(2)}) collective-permute-start(bf16[64,1024]{1,0:T(8,128)(2,1)} %get-tuple-element.88), channel_id=1, source_target_pairs={{8,13},{10,15},{24,29},{26,31}} | collective-permute-start | bytes 393224 | tf_op jit(solution)/shard_map/ppermute | solution.py:371
  58.1 34.3 %collective-permute-start.30 = (bf16[768,1024]{1,0:T(8,128)(2,1)}, bf16[768,1024]{1,0:T(8,128)(2,1)}, u32[]{:S(2)}, u32[]{:S(2)}) collective-permute-start(bf16[768,1024]{1,0:T(8,128)(2,1)} %shard_map.113), channel_id=1, source_target_pairs={{0,16},{1,17},{2,18},{3,19},{4,20},{5,21},{6,22},{7,23},{16,0},{17... | collective-permute-start | bytes 4718600 | tf_op jit(solution)/shard_map/ppermute | solution.py:371
  64.2 19.1 %collective-permute-start.20 = (bf16[128,1024]{1,0:T(8,128)(2,1)}, bf16[128,1024]{1,0:T(8,128)(2,1)}, u32[]{:S(2)}, u32[]{:S(2)}) collective-permute-start(bf16[128,1024]{1,0:T(8,128)(2,1)} %slice_select_fusion), channel_id=1, source_target_pairs={{1,0},{3,2},{4,5},{6,7},{17,16},{19,18},{20,21},{22,23}} | collective-permute-start | bytes 786440 | tf_op jit(solution)/shard_map/ppermute | solution.py:371
  68.9 14.4 %collective-permute-start.21 = (bf16[128,1024]{1,0:T(8,128)(2,1)}, bf16[128,1024]{1,0:T(8,128)(2,1)}, u32[]{:S(2)}, u32[]{:S(2)}) collective-permute-start(bf16[128,1024]{1,0:T(8,128)(2,1)} %select_select_fusion), channel_id=1, source_target_pairs={{8,9},{10,11},{13,12},{15,14},{24,25},{26,27},{29,28},{31,30}} | collective-permute-start | bytes 786440 | tf_op jit(solution)/shard_map/ppermute | solution.py:371
  70.3 15.2 %collective-permute-start.19 = (bf16[128,1024]{1,0:T(8,128)(2,1)}, bf16[128,1024]{1,0:T(8,128)(2,1)S(1)}, u32[]{:S(2)}, u32[]{:S(2)}) collective-permute-start(bf16[128,1024]{1,0:T(8,128)(2,1)} %copy-done.11), channel_id=1, source_target_pairs={{0,2},{1,3},{2,0},{3,1},{12,14},{13,15},{14,12},{15,13},{16,18},{1... | collective-permute-start | bytes 786440 | tf_op jit(solution)/shard_map/ppermute | solution.py:371
  89.3 8.6 %collective-permute-start.31 = (bf16[128,896]{1,0:T(8,128)(2,1)S(1)}, bf16[128,896]{1,0:T(8,128)(2,1)S(1)}, u32[]{:S(2)}, u32[]{:S(2)}) collective-permute-start(bf16[128,896]{1,0:T(8,128)(2,1)S(1)} %pad_maximum_fusion), channel_id=1, source_target_pairs={{0,16},{1,17},{2,18},{3,19},{4,20},{5,21},{6,22},{7,23},{8,24},{9,... | collective-permute-start | bytes 688136 | tf_op jit(solution)/shard_map/ppermute | solution.py:371
  90.4 7.5 %collective-permute-start.26 = (bf16[64,1024]{1,0:T(8,128)(2,1)S(1)}, bf16[64,1024]{1,0:T(8,128)(2,1)S(1)}, u32[]{:S(2)}, u32[]{:S(2)}) collective-permute-start(bf16[64,1024]{1,0:T(8,128)(2,1)S(1)} %get-tuple-element.110), channel_id=1, source_target_pairs={{8,4},{10,6},{24,20},{26,22}} | collective-permute-start | bytes 393224 | tf_op jit(solution)/shard_map/ppermute | solution.py:371
  91.1 6.9 %collective-permute-start.27 = (bf16[64,1024]{1,0:T(8,128)(2,1)S(1)}, bf16[64,1024]{1,0:T(8,128)(2,1)S(1)}, u32[]{:S(2)}, u32[]{:S(2)}) collective-permute-start(bf16[64,1024]{1,0:T(8,128)(2,1)S(1)} %get-tuple-element.110), channel_id=1, source_target_pairs={{8,6},{10,4},{24,22},{26,20}} | collective-permute-start | bytes 393224 | tf_op jit(solution)/shard_map/ppermute | solution.py:371
  91.7 6.2 %collective-permute-start.28 = (bf16[64,1024]{1,0:T(8,128)(2,1)S(1)}, bf16[64,1024]{1,0:T(8,128)(2,1)S(1)}, u32[]{:S(2)}, u32[]{:S(2)}) collective-permute-start(bf16[64,1024]{1,0:T(8,128)(2,1)S(1)} %get-tuple-element.111), channel_id=1, source_target_pairs={{8,20},{10,22},{24,4},{26,6}} | collective-permute-start | bytes 393224 | tf_op jit(solution)/shard_map/ppermute | solution.py:371
  92.4 5.5 %collective-permute-start.29 = (bf16[64,1024]{1,0:T(8,128)(2,1)S(1)}, bf16[64,1024]{1,0:T(8,128)(2,1)S(1)}, u32[]{:S(2)}, u32[]{:S(2)}) collective-permute-start(bf16[64,1024]{1,0:T(8,128)(2,1)S(1)} %get-tuple-element.111), channel_id=1, source_target_pairs={{8,22},{10,20},{24,6},{26,4}} | collective-permute-start | bytes 393224 | tf_op jit(solution)/shard_map/ppermute | solution.py:371
  98.7 4.0 %collective-permute-start.32 = (bf16[64,1024]{1,0:T(8,128)(2,1)S(1)}, bf16[64,1024]{1,0:T(8,128)(2,1)}, u32[]{:S(2)}, u32[]{:S(2)}) collective-permute-start(bf16[64,1024]{1,0:T(8,128)(2,1)S(1)} %get-tuple-element.120), channel_id=1, source_target_pairs={{4,1},{6,3},{20,17},{22,19}} | collective-permute-start | bytes 393224 | tf_op jit(solution)/shard_map/ppermute | solution.py:371
  106.0 73.4 %collective-permute-start.36 = (bf16[128,1024]{1,0:T(8,128)(2,1)S(1)}, bf16[128,1024]{1,0:T(8,128)(2,1)S(1)}, u32[]{:S(2)}, u32[]{:S(2)}) collective-permute-start(bf16[128,1024]{1,0:T(8,128)(2,1)S(1)} %fusion.28), channel_id=1, source_target_pairs={{1,0},{3,2},{4,5},{6,7},{8,9},{10,11},{13,12},{15,14},{17,16},{19,... | collective-permute-start | bytes 786440 | tf_op jit(solution)/shard_map/ppermute | solution.py:371
  181.2 11.1 %collective-permute-start.38 = (bf16[128,1024]{1,0:T(8,128)(2,1)S(1)}, bf16[128,1024]{1,0:T(8,128)(2,1)S(1)}, u32[]{:S(2)}, u32[]{:S(2)}) collective-permute-start(bf16[128,1024]{1,0:T(8,128)(2,1)S(1)} %broadcast_select_fusion.1.refs_0_), channel_id=1, source_target_pairs={{0,16},{1,17},{2,18},{3,19},{4,20},{5,21},{6,22},{7,23},{8,24},{9,... | collective-permute-start | bytes 786440 | tf_op jit(solution)/shard_map/ppermute | solution.py:371
  183.8 5.9 %collective-permute-start.37 = (bf16[128,768]{1,0:T(8,128)(2,1)S(1)}, bf16[128,768]{1,0:T(8,128)(2,1)S(1)}, u32[]{:S(2)}, u32[]{:S(2)}) collective-permute-start(bf16[128,768]{1,0:T(8,128)(2,1)S(1)} %shard_map.121), channel_id=1, source_target_pairs={{0,16},{1,17},{2,18},{3,19},{4,20},{5,21},{6,22},{7,23},{8,24},{9,... | collective-permute-start | bytes 589832 | tf_op jit(solution)/shard_map/ppermute | solution.py:371
  (42 other events, 346.9 us)

commit v6 on v5

--- a/solution.py
+++ b/solution.py
@@ -408,7 +408,9 @@
     pair = jnp.concatenate([edge, at_ends(edge, 1)])
     edges = [pair, at_ends(pair, 2)]
     rest = range(1, sections)
-    near = [to_holders(weight_in, 1, rest), to_holders(weight_out, 1, rest)]
+    near_in = to_holders(weight_in, 1, rest)
+    near_in, next_out = lax.optimization_barrier((near_in, weight_out))
+    near = [near_in, to_holders(next_out, 1, rest)]
 
     tables = lax.dynamic_index_in_dim(partners, section_id, 0, keepdims=False)
 

time: 197 us -> 190 us (0.964)
  waiting for transfers between devices: 96.5 us -> 89.3 us
    ppermute x39, waiting for transfers between devices: 96.5 us -> 89.3 us  [move(): return lax.ppermute(array, axes, pairs)]
    unnamed x54 -> x50, local copies, waits for them, and re-layouts: 8.79 us -> 8.13 us
  transfers between devices with their start and end apart: 39 -> 39, of which waited for: 6 -> 7; matrix products, arithmetic and copies ran while one was open for 9% -> 9% of each run, Pallas kernels for 6% -> 6%
where the time goes in v6:
time: 190 us; the launch traced here: 189 us
  waiting for transfers between devices  89.3 us (47%)
  starting transfers between devices  53.5 us (28%)
  other arithmetic  12.6 us (7%)
  Pallas kernels  11.6 us (6%)
  local copies, waits for them, and re-layouts  11.4 us (6%)
  matrix products  6.75 us (4%)
  between operations  4.09 us (2%)
    ppermute x39, waiting for transfers between devices, move(): return lax.ppermute(array, axes, pairs)  89.3 us
    ppermute x39, starting transfers between devices, move(): return lax.ppermute(array, axes, pairs)  53.5 us
    unnamed x50, local copies, waits for them, and re-layouts  8.13 us
    pallas_call x7, Pallas kernels, chain_step(): pl.pallas_call(functools.partial(chain_kernel, sz, step, forward, (len(re...  7.6 us
    dot_general x6, matrix products, dot(): lax.dot_general(left, right, dims, preferred_element_type=jnp.float32)  6.75 us
  transfers between devices with their start and end apart: 39, of which 7 were waited for; matrix products, arithmetic and copies ran while one was open for 9% of the time, Pallas kernels for 6%

profile of v6, /device:TPU:0, one launch (start us, length us, event | category | flops | bytes accessed | tf_op | source)
XLA Modules:
  0.0 189.3 jit_solution(640909519647311023)
XLA Ops:
  1.5 4.9 %collective-permute-start = (bf16[128,256]{1,0:T(8,128)(2,1)S(1)}, bf16[128,256]{1,0:T(8,128)(2,1)S(1)}, u32[]{:S(2)}, u32[]{:S(2)}) collective-permute-start(bf16[128,256]{1,0:T(8,128)(2,1)S(1)} %select_bitcast_fusion), channel_id=1, source_target_pairs={{0,1},{1,0},{2,3},{3,2},{12,13},{13,12},{14,15},{15,14},{16,17},{1... | collective-permute-start | bytes 196616 | tf_op jit(solution)/shard_map/ppermute | solution.py:371
  6.5 1.8 collective-permute-start.8
  14.6 1.6 collective-permute-start.7
  16.5 4.5 %collective-permute-start.1 = (bf16[256,256]{1,0:T(8,128)(2,1)S(1)}, bf16[256,256]{1,0:T(8,128)(2,1)S(1)}, u32[]{:S(2)}, u32[]{:S(2)}) collective-permute-start(bf16[256,256]{1,0:T(8,128)(2,1)S(1)} %pad_maximum_fusion.1.refs_1_.refs_3_), channel_id=1, source_target_pairs={{0,2},{1,3},{2,0},{3,1},{12,14},{13,15},{14,12},{15,13},{16,18},{1... | collective-permute-start | bytes 393224 | tf_op jit(solution)/shard_map/ppermute | solution.py:371
  21.1 4.7 %collective-permute-done.1.refs_2_.refs_4_ = bf16[256,256]{1,0:T(8,128)(2,1)S(1)} collective-permute-done((bf16[256,256]{1,0:T(8,128)(2,1)S(1)}, bf16[256,256]{1,0:T(8,128)(2,1)S(1)}, u32[]{:S(2)}, u32[]{:S(2)}) %collective-permute-start.1) | collective-permute-done | bytes 131104 | tf_op jit(solution)/shard_map/ppermute | solution.py:371
  25.7 2.9 %shard_map.111 = (bf16[128,1024]{1,0:T(8,128)(2,1)}, bf16[18432,1024]{1,0:T(8,128)(2,1)}, f32[6144,1536]{1,0:T(8,128)}) custom-call(s32[6,5]{1,0:T(8,128)S(1)} %fusion.31.refs_0_, bf16[256,256]{1,0:T(8,128)(2,1)S(1)} %pad_maximum_fusion.1.refs_1_.refs_3_, bf16[256,256]{1,0:T(8,128)(2,1)S(1)} %collective-permute-done.1.refs_2_.refs_4_, ...), custom_call_target="tpu_custom_call" | custom-call | flops 805306368 | bytes 6291456 | tf_op jit(solution)/shard_map/pallas_call | solution.py:241
  28.6 2.3 %collective-permute-start.2 = (bf16[128,1024]{1,0:T(8,128)(2,1)}, bf16[128,1024]{1,0:T(8,128)(2,1)}, u32[]{:S(2)}, u32[]{:S(2)}) collective-permute-start(bf16[128,1024]{1,0:T(8,128)(2,1)} %get-tuple-element.68), channel_id=1, source_target_pairs={{0,1},{1,0},{2,3},{3,2},{12,13},{13,12},{14,15},{15,14},{16,17},{1... | collective-permute-start | bytes 786440 | tf_op jit(solution)/shard_map/ppermute | solution.py:371
  32.8 1.8 collective-permute-start.9
  34.6 5.5 %collective-permute-done.2 = bf16[128,1024]{1,0:T(8,128)(2,1)} collective-permute-done((bf16[128,1024]{1,0:T(8,128)(2,1)}, bf16[128,1024]{1,0:T(8,128)(2,1)}, u32[]{:S(2)}, u32[]{:S(2)}) %collective-permute-start.2) | collective-permute-done | bytes 262176 | tf_op jit(solution)/shard_map/ppermute | solution.py:371
  50.6 1.9 %collective-permute-start.18 = (bf16[768,1024]{1,0:T(8,128)(2,1)}, bf16[768,1024]{1,0:T(8,128)(2,1)}, u32[]{:S(2)}, u32[]{:S(2)}) collective-permute-start(bf16[768,1024]{1,0:T(8,128)(2,1)} %shard_map.113), channel_id=1, source_target_pairs={{8,24},{9,25},{10,26},{11,27},{12,28},{13,29},{14,30},{15,31},{24,... | collective-permute-start | bytes 4718600 | tf_op jit(solution)/shard_map/ppermute | solution.py:371
  56.0 1.8 slice_select_fusion
  64.5 2.3 %collective-permute-start.30 = (bf16[768,1024]{1,0:T(8,128)(2,1)}, bf16[768,1024]{1,0:T(8,128)(2,1)}, u32[]{:S(2)}, u32[]{:S(2)}) collective-permute-start(bf16[768,1024]{1,0:T(8,128)(2,1)} %shard_map.113), channel_id=1, source_target_pairs={{0,16},{1,17},{2,18},{3,19},{4,20},{5,21},{6,22},{7,23},{16,0},{17... | collective-permute-start | bytes 4718600 | tf_op jit(solution)/shard_map/ppermute | solution.py:371
  68.3 1.9 %select_select_fusion = bf16[128,1024]{1,0:T(8,128)(2,1)} fusion(bf16[18432,1024]{1,0:T(8,128)(2,1)} %get-tuple-element.101.refs_9_, pred[]{:T(512)S(6)} %eq.98, pred[]{:T(512)S(6)} %eq.97, pred[]{:T(512)S(6)} %eq.96), kind=kLoop, calls=%fused_computation.51 | loop fusion | flops 393216 | bytes 1310723 | tf_op jit(solution)/shard_map/jit(_where)/select_n | solution.py:488
  71.6 3.3 %collective-permute-start.19 = (bf16[128,1024]{1,0:T(8,128)(2,1)}, bf16[128,1024]{1,0:T(8,128)(2,1)S(1)}, u32[]{:S(2)}, u32[]{:S(2)}) collective-permute-start(bf16[128,1024]{1,0:T(8,128)(2,1)} %copy-done.11), channel_id=1, source_target_pairs={{0,2},{1,3},{2,0},{3,1},{12,14},{13,15},{14,12},{15,13},{16,18},{1... | collective-permute-start | bytes 786440 | tf_op jit(solution)/shard_map/ppermute | solution.py:371
  75.3 1.4 add_select_fusion.refs_0_
  77.5 3.6 %collective-permute-done.19.refs_2_ = bf16[128,1024]{1,0:T(8,128)(2,1)S(1)} collective-permute-done((bf16[128,1024]{1,0:T(8,128)(2,1)}, bf16[128,1024]{1,0:T(8,128)(2,1)S(1)}, u32[]{:S(2)}, u32[]{:S(2)}) %collective-permute-start.19) | collective-permute-done | bytes 262176 | tf_op jit(solution)/shard_map/ppermute | solution.py:371
  83.4 1.7 collective-permute-start.31
  89.9 8.2 %collective-permute-done.31 = bf16[128,896]{1,0:T(8,128)(2,1)S(1)} collective-permute-done((bf16[128,896]{1,0:T(8,128)(2,1)S(1)}, bf16[128,896]{1,0:T(8,128)(2,1)S(1)}, u32[]{:S(2)}, u32[]{:S(2)}) %collective-permute-start.31) | collective-permute-done | bytes 229408 | tf_op jit(solution)/shard_map/ppermute | solution.py:371
  107.0 1.6 collective-permute-start.36
  108.7 1.6 broadcast_select_fusion
  110.3 62.9 %collective-permute-done.36 = bf16[128,1024]{1,0:T(8,128)(2,1)S(1)} collective-permute-done((bf16[128,1024]{1,0:T(8,128)(2,1)S(1)}, bf16[128,1024]{1,0:T(8,128)(2,1)S(1)}, u32[]{:S(2)}, u32[]{:S(2)}) %collective-permute-start.36) | collective-permute-done | bytes 262176 | tf_op jit(solution)/shard_map/ppermute | solution.py:371
  177.5 1.6 collective-permute-start.37
  179.5 4.0 %collective-permute-done.37 = bf16[128,768]{1,0:T(8,128)(2,1)S(1)} collective-permute-done((bf16[128,768]{1,0:T(8,128)(2,1)S(1)}, bf16[128,768]{1,0:T(8,128)(2,1)S(1)}, u32[]{:S(2)}, u32[]{:S(2)}) %collective-permute-start.37) | collective-permute-done | bytes 196640 | tf_op jit(solution)/shard_map/ppermute | solution.py:371
  183.5 2.5 %fusion.27 = (bf16[1,1,1024,768]{3,2,1,0:T(8,128)(2,1)S(1)}, bf16[1,1,1024,768]{3,2,1,0:T(8,128)(2,1)S(1)}) fusion(bf16[1,1,1024,768]{3,2,1,0:T(8,128)(2,1)S(1)} %get-tuple-element.140, s32[]{:T(128)S(6)} %select_n.158, bf16[1024,768]{1,0:T(8,128)(2,1)} %collective-permute-done.7, bf16[1,1,1024,768]{3,2,1,0:T(8,128)(2,1)S(1)} %copy-done.6, ...), kind=kOutput, calls=%fused_computation.44 | convolution fusion | flops 108920832 | bytes 5832708 | tf_op jit(solution)/shard_map/dot_general | solution.py:22
  (155 shorter events, 54.9 us)
Async XLA Ops:
  1.5 15.0 %collective-permute-start = (bf16[128,256]{1,0:T(8,128)(2,1)S(1)}, bf16[128,256]{1,0:T(8,128)(2,1)S(1)}, u32[]{:S(2)}, u32[]{:S(2)}) collective-permute-start(bf16[128,256]{1,0:T(8,128)(2,1)S(1)} %select_bitcast_fusion), channel_id=1, source_target_pairs={{0,1},{1,0},{2,3},{3,2},{12,13},{13,12},{14,15},{15,14},{16,17},{1... | collective-permute-start | bytes 196616 | tf_op jit(solution)/shard_map/ppermute | solution.py:371
  6.5 26.3 %collective-permute-start.8 = (bf16[1024,768]{1,0:T(8,128)(2,1)}, bf16[1024,768]{1,0:T(8,128)(2,1)}, u32[]{:S(2)}, u32[]{:S(2)}) collective-permute-start(bf16[1024,768]{1,0:T(8,128)(2,1)} %bitcast.83), channel_id=1, source_target_pairs={{5,4},{7,6},{9,8},{11,10},{12,13},{14,15},{21,20},{23,22},{25,24},... | collective-permute-start | bytes 4718600 | tf_op jit(solution)/shard_map/ppermute | solution.py:371
  14.6 36.0 %collective-permute-start.7 = (bf16[1024,768]{1,0:T(8,128)(2,1)}, bf16[1024,768]{1,0:T(8,128)(2,1)}, u32[]{:S(2)}, u32[]{:S(2)}) collective-permute-start(bf16[1024,768]{1,0:T(8,128)(2,1)} %shard_map.112), channel_id=1, source_target_pairs={{0,16},{1,17},{2,18},{3,19},{4,20},{5,21},{6,22},{7,23},{8,24},{9,... | collective-permute-start | bytes 4718600 | tf_op jit(solution)/shard_map/ppermute | solution.py:371
  16.5 9.2 %collective-permute-start.1 = (bf16[256,256]{1,0:T(8,128)(2,1)S(1)}, bf16[256,256]{1,0:T(8,128)(2,1)S(1)}, u32[]{:S(2)}, u32[]{:S(2)}) collective-permute-start(bf16[256,256]{1,0:T(8,128)(2,1)S(1)} %pad_maximum_fusion.1.refs_1_.refs_3_), channel_id=1, source_target_pairs={{0,2},{1,3},{2,0},{3,1},{12,14},{13,15},{14,12},{15,13},{16,18},{1... | collective-permute-start | bytes 393224 | tf_op jit(solution)/shard_map/ppermute | solution.py:371
  28.6 11.5 %collective-permute-start.2 = (bf16[128,1024]{1,0:T(8,128)(2,1)}, bf16[128,1024]{1,0:T(8,128)(2,1)}, u32[]{:S(2)}, u32[]{:S(2)}) collective-permute-start(bf16[128,1024]{1,0:T(8,128)(2,1)} %get-tuple-element.68), channel_id=1, source_target_pairs={{0,1},{1,0},{2,3},{3,2},{12,13},{13,12},{14,15},{15,14},{16,17},{1... | collective-permute-start | bytes 786440 | tf_op jit(solution)/shard_map/ppermute | solution.py:371
  32.8 19.7 %collective-permute-start.9 = (bf16[768,1024]{1,0:T(8,128)(2,1)S(1)}, bf16[768,1024]{1,0:T(8,128)(2,1)}, u32[]{:S(2)}, u32[]{:S(2)}) collective-permute-start(bf16[768,1024]{1,0:T(8,128)(2,1)S(1)} %bitcast.74), channel_id=1, source_target_pairs={{5,4},{7,6},{9,8},{11,10},{12,13},{14,15},{21,20},{23,22},{25,24},... | collective-permute-start | bytes 4718600 | tf_op jit(solution)/shard_map/ppermute | solution.py:371
  42.6 8.0 %collective-permute-start.4 = (bf16[64,1024]{1,0:T(8,128)(2,1)}, bf16[64,1024]{1,0:T(8,128)(2,1)}, u32[]{:S(2)}, u32[]{:S(2)}) collective-permute-start(bf16[64,1024]{1,0:T(8,128)(2,1)} %get-tuple-element.143), channel_id=1, source_target_pairs={{1,6},{3,4},{17,22},{19,20}} | collective-permute-start | bytes 393224 | tf_op jit(solution)/shard_map/ppermute | solution.py:371
  43.9 6.7 %collective-permute-start.5 = (bf16[64,1024]{1,0:T(8,128)(2,1)}, bf16[64,1024]{1,0:T(8,128)(2,1)}, u32[]{:S(2)}, u32[]{:S(2)}) collective-permute-start(bf16[64,1024]{1,0:T(8,128)(2,1)} %get-tuple-element.142), channel_id=1, source_target_pairs={{1,20},{3,22},{17,4},{19,6}} | collective-permute-start | bytes 393224 | tf_op jit(solution)/shard_map/ppermute | solution.py:371
  45.2 5.4 %collective-permute-start.6 = (bf16[64,1024]{1,0:T(8,128)(2,1)}, bf16[64,1024]{1,0:T(8,128)(2,1)}, u32[]{:S(2)}, u32[]{:S(2)}) collective-permute-start(bf16[64,1024]{1,0:T(8,128)(2,1)} %get-tuple-element.142), channel_id=1, source_target_pairs={{1,22},{3,20},{17,6},{19,4}} | collective-permute-start | bytes 393224 | tf_op jit(solution)/shard_map/ppermute | solution.py:371
  50.6 12.6 %collective-permute-start.18 = (bf16[768,1024]{1,0:T(8,128)(2,1)}, bf16[768,1024]{1,0:T(8,128)(2,1)}, u32[]{:S(2)}, u32[]{:S(2)}) collective-permute-start(bf16[768,1024]{1,0:T(8,128)(2,1)} %shard_map.113), channel_id=1, source_target_pairs={{8,24},{9,25},{10,26},{11,27},{12,28},{13,29},{14,30},{15,31},{24,... | collective-permute-start | bytes 4718600 | tf_op jit(solution)/shard_map/ppermute | solution.py:371
  58.6 5.9 %collective-permute-start.14 = (bf16[64,1024]{1,0:T(8,128)(2,1)}, bf16[64,1024]{1,0:T(8,128)(2,1)S(1)}, u32[]{:S(2)}, u32[]{:S(2)}) collective-permute-start(bf16[64,1024]{1,0:T(8,128)(2,1)} %get-tuple-element.92), channel_id=1, source_target_pairs={{8,13},{10,15},{24,29},{26,31}} | collective-permute-start | bytes 393224 | tf_op jit(solution)/shard_map/ppermute | solution.py:371
  59.2 7.5 %collective-permute-start.15 = (bf16[64,1024]{1,0:T(8,128)(2,1)}, bf16[64,1024]{1,0:T(8,128)(2,1)}, u32[]{:S(2)}, u32[]{:S(2)}) collective-permute-start(bf16[64,1024]{1,0:T(8,128)(2,1)} %get-tuple-element.92), channel_id=1, source_target_pairs={{8,15},{10,13},{24,31},{26,29}} | collective-permute-start | bytes 393224 | tf_op jit(solution)/shard_map/ppermute | solution.py:371
  60.6 6.2 %collective-permute-start.16 = (bf16[64,1024]{1,0:T(8,128)(2,1)}, bf16[64,1024]{1,0:T(8,128)(2,1)}, u32[]{:S(2)}, u32[]{:S(2)}) collective-permute-start(bf16[64,1024]{1,0:T(8,128)(2,1)} %get-tuple-element.93), channel_id=1, source_target_pairs={{8,29},{10,31},{24,13},{26,15}} | collective-permute-start | bytes 393224 | tf_op jit(solution)/shard_map/ppermute | solution.py:371
  63.2 12.1 %collective-permute-start.20 = (bf16[128,1024]{1,0:T(8,128)(2,1)}, bf16[128,1024]{1,0:T(8,128)(2,1)}, u32[]{:S(2)}, u32[]{:S(2)}) collective-permute-start(bf16[128,1024]{1,0:T(8,128)(2,1)} %slice_select_fusion), channel_id=1, source_target_pairs={{1,0},{3,2},{4,5},{6,7},{17,16},{19,18},{20,21},{22,23}} | collective-permute-start | bytes 786440 | tf_op jit(solution)/shard_map/ppermute | solution.py:371
  64.5 34.4 %collective-permute-start.30 = (bf16[768,1024]{1,0:T(8,128)(2,1)}, bf16[768,1024]{1,0:T(8,128)(2,1)}, u32[]{:S(2)}, u32[]{:S(2)}) collective-permute-start(bf16[768,1024]{1,0:T(8,128)(2,1)} %shard_map.113), channel_id=1, source_target_pairs={{0,16},{1,17},{2,18},{3,19},{4,20},{5,21},{6,22},{7,23},{16,0},{17... | collective-permute-start | bytes 4718600 | tf_op jit(solution)/shard_map/ppermute | solution.py:371
  70.2 5.1 %collective-permute-start.21 = (bf16[128,1024]{1,0:T(8,128)(2,1)}, bf16[128,1024]{1,0:T(8,128)(2,1)}, u32[]{:S(2)}, u32[]{:S(2)}) collective-permute-start(bf16[128,1024]{1,0:T(8,128)(2,1)} %select_select_fusion), channel_id=1, source_target_pairs={{8,9},{10,11},{13,12},{15,14},{24,25},{26,27},{29,28},{31,30}} | collective-permute-start | bytes 786440 | tf_op jit(solution)/shard_map/ppermute | solution.py:371
  71.6 9.5 %collective-permute-start.19 = (bf16[128,1024]{1,0:T(8,128)(2,1)}, bf16[128,1024]{1,0:T(8,128)(2,1)S(1)}, u32[]{:S(2)}, u32[]{:S(2)}) collective-permute-start(bf16[128,1024]{1,0:T(8,128)(2,1)} %copy-done.11), channel_id=1, source_target_pairs={{0,2},{1,3},{2,0},{3,1},{12,14},{13,15},{14,12},{15,13},{16,18},{1... | collective-permute-start | bytes 786440 | tf_op jit(solution)/shard_map/ppermute | solution.py:371
  83.4 14.8 %collective-permute-start.31 = (bf16[128,896]{1,0:T(8,128)(2,1)S(1)}, bf16[128,896]{1,0:T(8,128)(2,1)S(1)}, u32[]{:S(2)}, u32[]{:S(2)}) collective-permute-start(bf16[128,896]{1,0:T(8,128)(2,1)S(1)} %pad_maximum_fusion), channel_id=1, source_target_pairs={{0,16},{1,17},{2,18},{3,19},{4,20},{5,21},{6,22},{7,23},{8,24},{9,... | collective-permute-start | bytes 688136 | tf_op jit(solution)/shard_map/ppermute | solution.py:371
  87.9 10.9 %collective-permute-start.26 = (bf16[64,1024]{1,0:T(8,128)(2,1)S(1)}, bf16[64,1024]{1,0:T(8,128)(2,1)S(1)}, u32[]{:S(2)}, u32[]{:S(2)}) collective-permute-start(bf16[64,1024]{1,0:T(8,128)(2,1)S(1)} %get-tuple-element.114), channel_id=1, source_target_pairs={{8,4},{10,6},{24,20},{26,22}} | collective-permute-start | bytes 393224 | tf_op jit(solution)/shard_map/ppermute | solution.py:371
  88.6 10.3 %collective-permute-start.27 = (bf16[64,1024]{1,0:T(8,128)(2,1)S(1)}, bf16[64,1024]{1,0:T(8,128)(2,1)S(1)}, u32[]{:S(2)}, u32[]{:S(2)}) collective-permute-start(bf16[64,1024]{1,0:T(8,128)(2,1)S(1)} %get-tuple-element.114), channel_id=1, source_target_pairs={{8,6},{10,4},{24,22},{26,20}} | collective-permute-start | bytes 393224 | tf_op jit(solution)/shard_map/ppermute | solution.py:371
  89.2 9.6 %collective-permute-start.28 = (bf16[64,1024]{1,0:T(8,128)(2,1)S(1)}, bf16[64,1024]{1,0:T(8,128)(2,1)S(1)}, u32[]{:S(2)}, u32[]{:S(2)}) collective-permute-start(bf16[64,1024]{1,0:T(8,128)(2,1)S(1)} %get-tuple-element.115), channel_id=1, source_target_pairs={{8,20},{10,22},{24,4},{26,6}} | collective-permute-start | bytes 393224 | tf_op jit(solution)/shard_map/ppermute | solution.py:371
  107.0 66.2 %collective-permute-start.36 = (bf16[128,1024]{1,0:T(8,128)(2,1)S(1)}, bf16[128,1024]{1,0:T(8,128)(2,1)S(1)}, u32[]{:S(2)}, u32[]{:S(2)}) collective-permute-start(bf16[128,1024]{1,0:T(8,128)(2,1)S(1)} %fusion.28), channel_id=1, source_target_pairs={{1,0},{3,2},{4,5},{6,7},{8,9},{10,11},{13,12},{15,14},{17,16},{19,... | collective-permute-start | bytes 786440 | tf_op jit(solution)/shard_map/ppermute | solution.py:371
  174.9 11.1 %collective-permute-start.38 = (bf16[128,1024]{1,0:T(8,128)(2,1)S(1)}, bf16[128,1024]{1,0:T(8,128)(2,1)S(1)}, u32[]{:S(2)}, u32[]{:S(2)}) collective-permute-start(bf16[128,1024]{1,0:T(8,128)(2,1)S(1)} %broadcast_select_fusion.1.refs_0_), channel_id=1, source_target_pairs={{0,16},{1,17},{2,18},{3,19},{4,20},{5,21},{6,22},{7,23},{8,24},{9,... | collective-permute-start | bytes 786440 | tf_op jit(solution)/shard_map/ppermute | solution.py:371
  177.5 5.9 %collective-permute-start.37 = (bf16[128,768]{1,0:T(8,128)(2,1)S(1)}, bf16[128,768]{1,0:T(8,128)(2,1)S(1)}, u32[]{:S(2)}, u32[]{:S(2)}) collective-permute-start(bf16[128,768]{1,0:T(8,128)(2,1)S(1)} %shard_map.121), channel_id=1, source_target_pairs={{0,16},{1,17},{2,18},{3,19},{4,20},{5,21},{6,22},{7,23},{8,24},{9,... | collective-permute-start | bytes 589832 | tf_op jit(solution)/shard_map/ppermute | solution.py:371
  (40 other events, 330.2 us)

commit v7 on v6

--- a/solution.py
+++ b/solution.py
@@ -406,6 +406,7 @@
         return move(array, ends, lambda r, s, j: (r, s, j ^ offset))
 
     pair = jnp.concatenate([edge, at_ends(edge, 1)])
+    pair, packed_weight = lax.optimization_barrier((pair, weight_in))
     edges = [pair, at_ends(pair, 2)]
     rest = range(1, sections)
     near_in = to_holders(weight_in, 1, rest)
@@ -430,7 +431,7 @@
         return [across_replicas(array, e, active) for e, array in zip(others, arrays)]
 
     packed_in = [
-        pack([weight_in, moment_a[0, 0]], pieces_in[e] * size_in, size_in) for e in others
+        pack([packed_weight, moment_a[0, 0]], pieces_in[e] * size_in, size_in) for e in others
     ]
     packed_out = [
         pack([weight_out, moment_b[0, 0]], pieces_out[e] * size_out, size_out) for e in others
@@ -570,6 +571,7 @@
     far_up = exchange([upstream] * len(others), every)
     (grad_pre,) = share_call(sz, [upstream, slope], weight_out)
     far_pre = exchange([grad_pre] * len(others), every)
+    far_up, upstream, grad_pre = lax.optimization_barrier((far_up, upstream, grad_pre))
     far_states_out = [
         jnp.where(section_id < len(late), one, two)
         for one, two in zip(far_late, far_states_out)

time: 190 us -> 190 us (level)
  local copies, waits for them, and re-layouts: 11.4 us -> 8.31 us
  waiting for transfers between devices: 89.3 us -> 91.2 us
    ppermute x39, waiting for transfers between devices: 89.3 us -> 91.2 us  [move(): return lax.ppermute(array, axes, pairs)]
where the time goes in v7:
time: 190 us; the launch traced here: 189 us
  waiting for transfers between devices  91.2 us (48%)
  starting transfers between devices  52.4 us (28%)
  other arithmetic  13.5 us (7%)
  Pallas kernels  11.6 us (6%)
  local copies, waits for them, and re-layouts  8.31 us (4%)
  matrix products  7.45 us (4%)
  between operations  4.16 us (2%)
    ppermute x39, waiting for transfers between devices, move(): return lax.ppermute(array, axes, pairs)  91.2 us
    ppermute x39, starting transfers between devices, move(): return lax.ppermute(array, axes, pairs)  52.4 us
    pallas_call x7, Pallas kernels, chain_step(): pl.pallas_call(functools.partial(chain_kernel, sz, step, forward, (len(re...  7.6 us
    dot_general x6, matrix products, dot(): lax.dot_general(left, right, dims, preferred_element_type=jnp.float32)  7.45 us
    unnamed x50, local copies, waits for them, and re-layouts  6.82 us
  transfers between devices with their start and end apart: 39, of which 7 were waited for; matrix products, arithmetic and copies ran while one was open for 9% of the time, Pallas kernels for 6%

profile of v7, /device:TPU:0, one launch (start us, length us, event | category | flops | bytes accessed | tf_op | source)
XLA Modules:
  0.0 188.8 jit_solution(989037059962803629)
XLA Ops:
  1.5 4.9 %collective-permute-start = (bf16[128,256]{1,0:T(8,128)(2,1)S(1)}, bf16[128,256]{1,0:T(8,128)(2,1)S(1)}, u32[]{:S(2)}, u32[]{:S(2)}) collective-permute-start(bf16[128,256]{1,0:T(8,128)(2,1)S(1)} %select_bitcast_fusion), channel_id=1, source_target_pairs={{0,1},{1,0},{2,3},{3,2},{12,13},{13,12},{14,15},{15,14},{16,17},{1... | collective-permute-start | bytes 196616 | tf_op jit(solution)/shard_map/ppermute | solution.py:371
  6.5 1.8 collective-permute-start.8
  14.9 1.6 collective-permute-start.7
  16.5 4.5 %collective-permute-start.1 = (bf16[256,256]{1,0:T(8,128)(2,1)S(1)}, bf16[256,256]{1,0:T(8,128)(2,1)S(1)}, u32[]{:S(2)}, u32[]{:S(2)}) collective-permute-start(bf16[256,256]{1,0:T(8,128)(2,1)S(1)} %pad_maximum_fusion.1.refs_1_.refs_3_), channel_id=1, source_target_pairs={{0,2},{1,3},{2,0},{3,1},{12,14},{13,15},{14,12},{15,13},{16,18},{1... | collective-permute-start | bytes 393224 | tf_op jit(solution)/shard_map/ppermute | solution.py:371
  21.1 4.7 %collective-permute-done.1.refs_2_.refs_4_ = bf16[256,256]{1,0:T(8,128)(2,1)S(1)} collective-permute-done((bf16[256,256]{1,0:T(8,128)(2,1)S(1)}, bf16[256,256]{1,0:T(8,128)(2,1)S(1)}, u32[]{:S(2)}, u32[]{:S(2)}) %collective-permute-start.1) | collective-permute-done | bytes 131104 | tf_op jit(solution)/shard_map/ppermute | solution.py:371
  25.7 2.9 %shard_map.111 = (bf16[128,1024]{1,0:T(8,128)(2,1)}, bf16[18432,1024]{1,0:T(8,128)(2,1)}, f32[6144,1536]{1,0:T(8,128)}) custom-call(s32[6,5]{1,0:T(8,128)S(1)} %fusion.31.refs_0_, bf16[256,256]{1,0:T(8,128)(2,1)S(1)} %pad_maximum_fusion.1.refs_1_.refs_3_, bf16[256,256]{1,0:T(8,128)(2,1)S(1)} %collective-permute-done.1.refs_2_.refs_4_, ...), custom_call_target="tpu_custom_call" | custom-call | flops 805306368 | bytes 6291456 | tf_op jit(solution)/shard_map/pallas_call | solution.py:241
  28.6 2.3 %collective-permute-start.2 = (bf16[128,1024]{1,0:T(8,128)(2,1)}, bf16[128,1024]{1,0:T(8,128)(2,1)}, u32[]{:S(2)}, u32[]{:S(2)}) collective-permute-start(bf16[128,1024]{1,0:T(8,128)(2,1)} %get-tuple-element.74), channel_id=1, source_target_pairs={{0,1},{1,0},{2,3},{3,2},{12,13},{13,12},{14,15},{15,14},{16,17},{1... | collective-permute-start | bytes 786440 | tf_op jit(solution)/shard_map/ppermute | solution.py:371
  32.8 1.9 %collective-permute-start.9 = (bf16[768,1024]{1,0:T(8,128)(2,1)S(1)}, bf16[768,1024]{1,0:T(8,128)(2,1)}, u32[]{:S(2)}, u32[]{:S(2)}) collective-permute-start(bf16[768,1024]{1,0:T(8,128)(2,1)S(1)} %bitcast.74), channel_id=1, source_target_pairs={{5,4},{7,6},{9,8},{11,10},{12,13},{14,15},{21,20},{23,22},{25,24},... | collective-permute-start | bytes 4718600 | tf_op jit(solution)/shard_map/ppermute | solution.py:371
  34.7 5.3 %collective-permute-done.2 = bf16[128,1024]{1,0:T(8,128)(2,1)} collective-permute-done((bf16[128,1024]{1,0:T(8,128)(2,1)}, bf16[128,1024]{1,0:T(8,128)(2,1)}, u32[]{:S(2)}, u32[]{:S(2)}) %collective-permute-start.2) | collective-permute-done | bytes 262176 | tf_op jit(solution)/shard_map/ppermute | solution.py:371
  50.6 1.8 collective-permute-start.18
  55.9 1.8 slice_select_fusion
  64.4 2.3 %collective-permute-start.30 = (bf16[768,1024]{1,0:T(8,128)(2,1)}, bf16[768,1024]{1,0:T(8,128)(2,1)}, u32[]{:S(2)}, u32[]{:S(2)}) collective-permute-start(bf16[768,1024]{1,0:T(8,128)(2,1)} %shard_map.113), channel_id=1, source_target_pairs={{0,16},{1,17},{2,18},{3,19},{4,20},{5,21},{6,22},{7,23},{16,0},{17... | collective-permute-start | bytes 4718600 | tf_op jit(solution)/shard_map/ppermute | solution.py:371
  68.2 1.9 %select_select_fusion = bf16[128,1024]{1,0:T(8,128)(2,1)} fusion(bf16[18432,1024]{1,0:T(8,128)(2,1)} %get-tuple-element.108.refs_9_, pred[]{:T(512)S(6)} %eq.98, pred[]{:T(512)S(6)} %eq.97, pred[]{:T(512)S(6)} %eq.96), kind=kLoop, calls=%fused_computation.51 | loop fusion | flops 393216 | bytes 1310723 | tf_op jit(solution)/shard_map/jit(_where)/select_n | solution.py:489
  71.5 3.3 %collective-permute-start.19 = (bf16[128,1024]{1,0:T(8,128)(2,1)}, bf16[128,1024]{1,0:T(8,128)(2,1)S(1)}, u32[]{:S(2)}, u32[]{:S(2)}) collective-permute-start(bf16[128,1024]{1,0:T(8,128)(2,1)} %copy-done.11), channel_id=1, source_target_pairs={{0,2},{1,3},{2,0},{3,1},{12,14},{13,15},{14,12},{15,13},{16,18},{1... | collective-permute-start | bytes 786440 | tf_op jit(solution)/shard_map/ppermute | solution.py:371
  75.3 1.4 add_select_fusion.refs_0_
  77.5 3.5 %collective-permute-done.19.refs_2_ = bf16[128,1024]{1,0:T(8,128)(2,1)S(1)} collective-permute-done((bf16[128,1024]{1,0:T(8,128)(2,1)}, bf16[128,1024]{1,0:T(8,128)(2,1)S(1)}, u32[]{:S(2)}, u32[]{:S(2)}) %collective-permute-start.19) | collective-permute-done | bytes 262176 | tf_op jit(solution)/shard_map/ppermute | solution.py:371
  82.7 1.7 collective-permute-start.31
  89.3 8.8 %collective-permute-done.31 = bf16[128,896]{1,0:T(8,128)(2,1)S(1)} collective-permute-done((bf16[128,896]{1,0:T(8,128)(2,1)S(1)}, bf16[128,896]{1,0:T(8,128)(2,1)S(1)}, u32[]{:S(2)}, u32[]{:S(2)}) %collective-permute-start.31) | collective-permute-done | bytes 229408 | tf_op jit(solution)/shard_map/ppermute | solution.py:371
  103.8 1.5 collective-permute-start.36
  105.3 66.6 %collective-permute-done.36 = bf16[128,1024]{1,0:T(8,128)(2,1)} collective-permute-done((bf16[128,1024]{1,0:T(8,128)(2,1)S(1)}, bf16[128,1024]{1,0:T(8,128)(2,1)}, u32[]{:S(2)}, u32[]{:S(2)}) %collective-permute-start.36) | collective-permute-done | bytes 262176 | tf_op jit(solution)/shard_map/ppermute | solution.py:371
  173.2 1.6 broadcast_select_fusion
  175.6 1.9 collective-permute-start.38
  177.4 1.9 collective-permute-done.37
  183.9 3.2 %fusion.27 = (bf16[1,1,1024,768]{3,2,1,0:T(8,128)(2,1)S(1)}, bf16[1,1,1024,768]{3,2,1,0:T(8,128)(2,1)S(1)}) fusion(bf16[1,1,1024,768]{3,2,1,0:T(8,128)(2,1)S(1)} %get-tuple-element.150, s32[]{:T(128)S(6)} %select_n.158, bf16[1024,768]{1,0:T(8,128)(2,1)} %collective-permute-done.7, bf16[1,1,1024,768]{3,2,1,0:T(8,128)(2,1)S(1)} %copy-done.8, ...), kind=kOutput, calls=%fused_computation.44 | convolution fusion | flops 108920832 | bytes 5832708 | tf_op jit(solution)/shard_map/dot_general | solution.py:22
  (155 shorter events, 51.6 us)
Async XLA Ops:
  1.5 9.3 %collective-permute-start = (bf16[128,256]{1,0:T(8,128)(2,1)S(1)}, bf16[128,256]{1,0:T(8,128)(2,1)S(1)}, u32[]{:S(2)}, u32[]{:S(2)}) collective-permute-start(bf16[128,256]{1,0:T(8,128)(2,1)S(1)} %select_bitcast_fusion), channel_id=1, source_target_pairs={{0,1},{1,0},{2,3},{3,2},{12,13},{13,12},{14,15},{15,14},{16,17},{1... | collective-permute-start | bytes 196616 | tf_op jit(solution)/shard_map/ppermute | solution.py:371
  6.5 26.3 %collective-permute-start.8 = (bf16[1024,768]{1,0:T(8,128)(2,1)}, bf16[1024,768]{1,0:T(8,128)(2,1)}, u32[]{:S(2)}, u32[]{:S(2)}) collective-permute-start(bf16[1024,768]{1,0:T(8,128)(2,1)} %bitcast.83), channel_id=1, source_target_pairs={{5,4},{7,6},{9,8},{11,10},{12,13},{14,15},{21,20},{23,22},{25,24},... | collective-permute-start | bytes 4718600 | tf_op jit(solution)/shard_map/ppermute | solution.py:371
  14.9 35.7 %collective-permute-start.7 = (bf16[1024,768]{1,0:T(8,128)(2,1)}, bf16[1024,768]{1,0:T(8,128)(2,1)}, u32[]{:S(2)}, u32[]{:S(2)}) collective-permute-start(bf16[1024,768]{1,0:T(8,128)(2,1)} %shard_map.112), channel_id=1, source_target_pairs={{0,16},{1,17},{2,18},{3,19},{4,20},{5,21},{6,22},{7,23},{8,24},{9,... | collective-permute-start | bytes 4718600 | tf_op jit(solution)/shard_map/ppermute | solution.py:371
  16.5 9.2 %collective-permute-start.1 = (bf16[256,256]{1,0:T(8,128)(2,1)S(1)}, bf16[256,256]{1,0:T(8,128)(2,1)S(1)}, u32[]{:S(2)}, u32[]{:S(2)}) collective-permute-start(bf16[256,256]{1,0:T(8,128)(2,1)S(1)} %pad_maximum_fusion.1.refs_1_.refs_3_), channel_id=1, source_target_pairs={{0,2},{1,3},{2,0},{3,1},{12,14},{13,15},{14,12},{15,13},{16,18},{1... | collective-permute-start | bytes 393224 | tf_op jit(solution)/shard_map/ppermute | solution.py:371
  28.6 11.5 %collective-permute-start.2 = (bf16[128,1024]{1,0:T(8,128)(2,1)}, bf16[128,1024]{1,0:T(8,128)(2,1)}, u32[]{:S(2)}, u32[]{:S(2)}) collective-permute-start(bf16[128,1024]{1,0:T(8,128)(2,1)} %get-tuple-element.74), channel_id=1, source_target_pairs={{0,1},{1,0},{2,3},{3,2},{12,13},{13,12},{14,15},{15,14},{16,17},{1... | collective-permute-start | bytes 786440 | tf_op jit(solution)/shard_map/ppermute | solution.py:371
  32.8 19.6 %collective-permute-start.9 = (bf16[768,1024]{1,0:T(8,128)(2,1)S(1)}, bf16[768,1024]{1,0:T(8,128)(2,1)}, u32[]{:S(2)}, u32[]{:S(2)}) collective-permute-start(bf16[768,1024]{1,0:T(8,128)(2,1)S(1)} %bitcast.74), channel_id=1, source_target_pairs={{5,4},{7,6},{9,8},{11,10},{12,13},{14,15},{21,20},{23,22},{25,24},... | collective-permute-start | bytes 4718600 | tf_op jit(solution)/shard_map/ppermute | solution.py:371
  42.6 8.0 %collective-permute-start.4 = (bf16[64,1024]{1,0:T(8,128)(2,1)}, bf16[64,1024]{1,0:T(8,128)(2,1)}, u32[]{:S(2)}, u32[]{:S(2)}) collective-permute-start(bf16[64,1024]{1,0:T(8,128)(2,1)} %get-tuple-element.153), channel_id=1, source_target_pairs={{1,6},{3,4},{17,22},{19,20}} | collective-permute-start | bytes 393224 | tf_op jit(solution)/shard_map/ppermute | solution.py:371
  43.9 6.7 %collective-permute-start.5 = (bf16[64,1024]{1,0:T(8,128)(2,1)}, bf16[64,1024]{1,0:T(8,128)(2,1)}, u32[]{:S(2)}, u32[]{:S(2)}) collective-permute-start(bf16[64,1024]{1,0:T(8,128)(2,1)} %get-tuple-element.152), channel_id=1, source_target_pairs={{1,20},{3,22},{17,4},{19,6}} | collective-permute-start | bytes 393224 | tf_op jit(solution)/shard_map/ppermute | solution.py:371
  45.2 5.4 %collective-permute-start.6 = (bf16[64,1024]{1,0:T(8,128)(2,1)}, bf16[64,1024]{1,0:T(8,128)(2,1)}, u32[]{:S(2)}, u32[]{:S(2)}) collective-permute-start(bf16[64,1024]{1,0:T(8,128)(2,1)} %get-tuple-element.152), channel_id=1, source_target_pairs={{1,22},{3,20},{17,6},{19,4}} | collective-permute-start | bytes 393224 | tf_op jit(solution)/shard_map/ppermute | solution.py:371
  50.6 12.5 %collective-permute-start.18 = (bf16[768,1024]{1,0:T(8,128)(2,1)}, bf16[768,1024]{1,0:T(8,128)(2,1)}, u32[]{:S(2)}, u32[]{:S(2)}) collective-permute-start(bf16[768,1024]{1,0:T(8,128)(2,1)} %shard_map.113), channel_id=1, source_target_pairs={{8,24},{9,25},{10,26},{11,27},{12,28},{13,29},{14,30},{15,31},{24,... | collective-permute-start | bytes 4718600 | tf_op jit(solution)/shard_map/ppermute | solution.py:371
  58.4 5.9 %collective-permute-start.14 = (bf16[64,1024]{1,0:T(8,128)(2,1)}, bf16[64,1024]{1,0:T(8,128)(2,1)S(1)}, u32[]{:S(2)}, u32[]{:S(2)}) collective-permute-start(bf16[64,1024]{1,0:T(8,128)(2,1)} %get-tuple-element.99), channel_id=1, source_target_pairs={{8,13},{10,15},{24,29},{26,31}} | collective-permute-start | bytes 393224 | tf_op jit(solution)/shard_map/ppermute | solution.py:371
  59.1 7.6 %collective-permute-start.15 = (bf16[64,1024]{1,0:T(8,128)(2,1)}, bf16[64,1024]{1,0:T(8,128)(2,1)}, u32[]{:S(2)}, u32[]{:S(2)}) collective-permute-start(bf16[64,1024]{1,0:T(8,128)(2,1)} %get-tuple-element.99), channel_id=1, source_target_pairs={{8,15},{10,13},{24,31},{26,29}} | collective-permute-start | bytes 393224 | tf_op jit(solution)/shard_map/ppermute | solution.py:371
  60.4 6.2 %collective-permute-start.16 = (bf16[64,1024]{1,0:T(8,128)(2,1)}, bf16[64,1024]{1,0:T(8,128)(2,1)}, u32[]{:S(2)}, u32[]{:S(2)}) collective-permute-start(bf16[64,1024]{1,0:T(8,128)(2,1)} %get-tuple-element.100), channel_id=1, source_target_pairs={{8,29},{10,31},{24,13},{26,15}} | collective-permute-start | bytes 393224 | tf_op jit(solution)/shard_map/ppermute | solution.py:371
  63.1 12.2 %collective-permute-start.20 = (bf16[128,1024]{1,0:T(8,128)(2,1)}, bf16[128,1024]{1,0:T(8,128)(2,1)}, u32[]{:S(2)}, u32[]{:S(2)}) collective-permute-start(bf16[128,1024]{1,0:T(8,128)(2,1)} %slice_select_fusion), channel_id=1, source_target_pairs={{1,0},{3,2},{4,5},{6,7},{17,16},{19,18},{20,21},{22,23}} | collective-permute-start | bytes 786440 | tf_op jit(solution)/shard_map/ppermute | solution.py:371
  64.4 34.4 %collective-permute-start.30 = (bf16[768,1024]{1,0:T(8,128)(2,1)}, bf16[768,1024]{1,0:T(8,128)(2,1)}, u32[]{:S(2)}, u32[]{:S(2)}) collective-permute-start(bf16[768,1024]{1,0:T(8,128)(2,1)} %shard_map.113), channel_id=1, source_target_pairs={{0,16},{1,17},{2,18},{3,19},{4,20},{5,21},{6,22},{7,23},{16,0},{17... | collective-permute-start | bytes 4718600 | tf_op jit(solution)/shard_map/ppermute | solution.py:371
  70.1 5.2 %collective-permute-start.21 = (bf16[128,1024]{1,0:T(8,128)(2,1)}, bf16[128,1024]{1,0:T(8,128)(2,1)}, u32[]{:S(2)}, u32[]{:S(2)}) collective-permute-start(bf16[128,1024]{1,0:T(8,128)(2,1)} %select_select_fusion), channel_id=1, source_target_pairs={{8,9},{10,11},{13,12},{15,14},{24,25},{26,27},{29,28},{31,30}} | collective-permute-start | bytes 786440 | tf_op jit(solution)/shard_map/ppermute | solution.py:371
  71.5 9.5 %collective-permute-start.19 = (bf16[128,1024]{1,0:T(8,128)(2,1)}, bf16[128,1024]{1,0:T(8,128)(2,1)S(1)}, u32[]{:S(2)}, u32[]{:S(2)}) collective-permute-start(bf16[128,1024]{1,0:T(8,128)(2,1)} %copy-done.11), channel_id=1, source_target_pairs={{0,2},{1,3},{2,0},{3,1},{12,14},{13,15},{14,12},{15,13},{16,18},{1... | collective-permute-start | bytes 786440 | tf_op jit(solution)/shard_map/ppermute | solution.py:371
  82.7 15.4 %collective-permute-start.31 = (bf16[128,896]{1,0:T(8,128)(2,1)S(1)}, bf16[128,896]{1,0:T(8,128)(2,1)S(1)}, u32[]{:S(2)}, u32[]{:S(2)}) collective-permute-start(bf16[128,896]{1,0:T(8,128)(2,1)S(1)} %pad_maximum_fusion), channel_id=1, source_target_pairs={{0,16},{1,17},{2,18},{3,19},{4,20},{5,21},{6,22},{7,23},{8,24},{9,... | collective-permute-start | bytes 688136 | tf_op jit(solution)/shard_map/ppermute | solution.py:371
  87.3 11.5 %collective-permute-start.26 = (bf16[64,1024]{1,0:T(8,128)(2,1)S(1)}, bf16[64,1024]{1,0:T(8,128)(2,1)S(1)}, u32[]{:S(2)}, u32[]{:S(2)}) collective-permute-start(bf16[64,1024]{1,0:T(8,128)(2,1)S(1)} %get-tuple-element.121), channel_id=1, source_target_pairs={{8,4},{10,6},{24,20},{26,22}} | collective-permute-start | bytes 393224 | tf_op jit(solution)/shard_map/ppermute | solution.py:371
  87.9 10.8 %collective-permute-start.27 = (bf16[64,1024]{1,0:T(8,128)(2,1)S(1)}, bf16[64,1024]{1,0:T(8,128)(2,1)S(1)}, u32[]{:S(2)}, u32[]{:S(2)}) collective-permute-start(bf16[64,1024]{1,0:T(8,128)(2,1)S(1)} %get-tuple-element.121), channel_id=1, source_target_pairs={{8,6},{10,4},{24,22},{26,20}} | collective-permute-start | bytes 393224 | tf_op jit(solution)/shard_map/ppermute | solution.py:371
  88.6 10.1 %collective-permute-start.28 = (bf16[64,1024]{1,0:T(8,128)(2,1)S(1)}, bf16[64,1024]{1,0:T(8,128)(2,1)S(1)}, u32[]{:S(2)}, u32[]{:S(2)}) collective-permute-start(bf16[64,1024]{1,0:T(8,128)(2,1)S(1)} %get-tuple-element.122), channel_id=1, source_target_pairs={{8,20},{10,22},{24,4},{26,6}} | collective-permute-start | bytes 393224 | tf_op jit(solution)/shard_map/ppermute | solution.py:371
  103.8 68.1 %collective-permute-start.36 = (bf16[128,1024]{1,0:T(8,128)(2,1)S(1)}, bf16[128,1024]{1,0:T(8,128)(2,1)}, u32[]{:S(2)}, u32[]{:S(2)}) collective-permute-start(bf16[128,1024]{1,0:T(8,128)(2,1)S(1)} %fusion.28), channel_id=1, source_target_pairs={{1,0},{3,2},{4,5},{6,7},{8,9},{10,11},{13,12},{15,14},{17,16},{19,... | collective-permute-start | bytes 786440 | tf_op jit(solution)/shard_map/ppermute | solution.py:371
  172.9 6.4 %collective-permute-start.37 = (bf16[128,1024]{1,0:T(8,128)(2,1)S(1)}, bf16[128,1024]{1,0:T(8,128)(2,1)S(1)}, u32[]{:S(2)}, u32[]{:S(2)}) collective-permute-start(bf16[128,1024]{1,0:T(8,128)(2,1)S(1)} %broadcast_select_fusion.1.refs_0_), channel_id=1, source_target_pairs={{0,16},{1,17},{2,18},{3,19},{4,20},{5,21},{6,22},{7,23},{8,24},{9,... | collective-permute-start | bytes 786440 | tf_op jit(solution)/shard_map/ppermute | solution.py:371
  175.6 8.3 %collective-permute-start.38 = (bf16[128,768]{1,0:T(8,128)(2,1)S(1)}, bf16[128,768]{1,0:T(8,128)(2,1)S(1)}, u32[]{:S(2)}, u32[]{:S(2)}) collective-permute-start(bf16[128,768]{1,0:T(8,128)(2,1)S(1)} %shard_map.121), channel_id=1, source_target_pairs={{0,16},{1,17},{2,18},{3,19},{4,20},{5,21},{6,22},{7,23},{8,24},{9,... | collective-permute-start | bytes 589832 | tf_op jit(solution)/shard_map/ppermute | solution.py:371
  (40 other events, 139.5 us)

commit v8 on v7

--- a/solution.py
+++ b/solution.py
@@ -510,8 +510,11 @@
         sends, stores = chain_step(
             sz, step, True, table, received, edges if step == 0 else [], weights, stores
         )
-        if step in (len(late) - 1, links):
-            rows = kept_of(stores, range(step + 1), True)
+        if step == len(late) - 1:
+            rows = kept_of(stores, late, True)
+        if step == links:
+            rows = kept_of(stores, early, True)
+            late_rows = kept_of(stores, late, True)
         if step == 0:
             total = sends[0].astype(jnp.float32)
             total = total + at_ends(sends[0], 1).astype(jnp.float32)
@@ -528,7 +531,8 @@
         else:
             received = [sends[0], at_ends(sends[0], 2)]
             row_parts.append(from_holders(rows, 1, early))
-            own_rows = jnp.where(is_holder, rows, sum(row_parts[1:], row_parts[0]))
+            own_rows = jnp.where(section_id < len(late), late_rows, rows)
+            own_rows = jnp.where(is_holder, own_rows, sum(row_parts[1:], row_parts[0]))
             received, *shares = lax.optimization_barrier(
                 (received, *share_call(sz, [own_rows], weight_in))
             )
@@ -571,7 +575,7 @@
     far_up = exchange([upstream] * len(others), every)
     (grad_pre,) = share_call(sz, [upstream, slope], weight_out)
     far_pre = exchange([grad_pre] * len(others), every)
-    far_up, upstream, grad_pre = lax.optimization_barrier((far_up, upstream, grad_pre))
+    upstream, grad_pre = lax.optimization_barrier((upstream, grad_pre))
     far_states_out = [
         jnp.where(section_id < len(late), one, two)
         for one, two in zip(far_late, far_states_out)

time: 190 us -> 191 us (level)
  local copies, waits for them, and re-layouts: 8.31 us -> 11.3 us
  transfers between devices with their start and end apart: 39 -> 39, of which waited for: 7 -> 7; matrix products, arithmetic and copies ran while one was open for 9% -> 9% of each run, Pallas kernels for 6% -> 5%
where the time goes in v8:
time: 191 us; the launch traced here: 190 us
  waiting for transfers between devices  90.2 us (47%)
  starting transfers between devices  53.7 us (28%)
  other arithmetic  12.4 us (6%)
  Pallas kernels  11.6 us (6%)
  local copies, waits for them, and re-layouts  11.3 us (6%)
  matrix products  6.74 us (4%)
  between operations  4.08 us (2%)
    ppermute x39, waiting for transfers between devices, move(): return lax.ppermute(array, axes, pairs)  90.2 us
    ppermute x39, starting transfers between devices, move(): return lax.ppermute(array, axes, pairs)  53.7 us
    unnamed x50, local copies, waits for them, and re-layouts  8 us
    pallas_call x7, Pallas kernels, chain_step(): pl.pallas_call(functools.partial(chain_kernel, sz, step, forward, (len(re...  7.6 us
    dot_general x6, matrix products, dot(): lax.dot_general(left, right, dims, preferred_element_type=jnp.float32)  6.74 us
  transfers between devices with their start and end apart: 39, of which 7 were waited for; matrix products, arithmetic and copies ran while one was open for 9% of the time, Pallas kernels for 5%

profile of v8, /device:TPU:0, one launch (start us, length us, event | category | flops | bytes accessed | tf_op | source)
XLA Modules:
  0.0 190.1 jit_solution(11775325682332755054)
XLA Ops:
  1.5 4.9 %collective-permute-start = (bf16[128,256]{1,0:T(8,128)(2,1)S(1)}, bf16[128,256]{1,0:T(8,128)(2,1)S(1)}, u32[]{:S(2)}, u32[]{:S(2)}) collective-permute-start(bf16[128,256]{1,0:T(8,128)(2,1)S(1)} %select_bitcast_fusion), channel_id=1, source_target_pairs={{0,1},{1,0},{2,3},{3,2},{12,13},{13,12},{14,15},{15,14},{16,17},{1... | collective-permute-start | bytes 196616 | tf_op jit(solution)/shard_map/ppermute | solution.py:371
  6.5 1.8 collective-permute-start.8
  14.9 1.6 collective-permute-start.7
  16.5 4.5 %collective-permute-start.1 = (bf16[256,256]{1,0:T(8,128)(2,1)S(1)}, bf16[256,256]{1,0:T(8,128)(2,1)S(1)}, u32[]{:S(2)}, u32[]{:S(2)}) collective-permute-start(bf16[256,256]{1,0:T(8,128)(2,1)S(1)} %pad_maximum_fusion.1.refs_1_.refs_3_), channel_id=1, source_target_pairs={{0,2},{1,3},{2,0},{3,1},{12,14},{13,15},{14,12},{15,13},{16,18},{1... | collective-permute-start | bytes 393224 | tf_op jit(solution)/shard_map/ppermute | solution.py:371
  21.1 4.7 %collective-permute-done.1.refs_2_.refs_4_ = bf16[256,256]{1,0:T(8,128)(2,1)S(1)} collective-permute-done((bf16[256,256]{1,0:T(8,128)(2,1)S(1)}, bf16[256,256]{1,0:T(8,128)(2,1)S(1)}, u32[]{:S(2)}, u32[]{:S(2)}) %collective-permute-start.1) | collective-permute-done | bytes 131104 | tf_op jit(solution)/shard_map/ppermute | solution.py:371
  25.7 2.9 %shard_map.111 = (bf16[128,1024]{1,0:T(8,128)(2,1)}, bf16[18432,1024]{1,0:T(8,128)(2,1)}, f32[6144,1536]{1,0:T(8,128)}) custom-call(s32[6,5]{1,0:T(8,128)S(1)} %fusion.31.refs_0_, bf16[256,256]{1,0:T(8,128)(2,1)S(1)} %pad_maximum_fusion.1.refs_1_.refs_3_, bf16[256,256]{1,0:T(8,128)(2,1)S(1)} %collective-permute-done.1.refs_2_.refs_4_, ...), custom_call_target="tpu_custom_call" | custom-call | flops 805306368 | bytes 6291456 | tf_op jit(solution)/shard_map/pallas_call | solution.py:241
  28.6 2.3 %collective-permute-start.2 = (bf16[128,1024]{1,0:T(8,128)(2,1)}, bf16[128,1024]{1,0:T(8,128)(2,1)}, u32[]{:S(2)}, u32[]{:S(2)}) collective-permute-start(bf16[128,1024]{1,0:T(8,128)(2,1)} %get-tuple-element.73), channel_id=1, source_target_pairs={{0,1},{1,0},{2,3},{3,2},{12,13},{13,12},{14,15},{15,14},{16,17},{1... | collective-permute-start | bytes 786440 | tf_op jit(solution)/shard_map/ppermute | solution.py:371
  32.8 1.8 collective-permute-start.9
  34.6 5.5 %collective-permute-done.2 = bf16[128,1024]{1,0:T(8,128)(2,1)} collective-permute-done((bf16[128,1024]{1,0:T(8,128)(2,1)}, bf16[128,1024]{1,0:T(8,128)(2,1)}, u32[]{:S(2)}, u32[]{:S(2)}) %collective-permute-start.2) | collective-permute-done | bytes 262176 | tf_op jit(solution)/shard_map/ppermute | solution.py:371
  50.6 1.9 %collective-permute-start.18 = (bf16[768,1024]{1,0:T(8,128)(2,1)}, bf16[768,1024]{1,0:T(8,128)(2,1)}, u32[]{:S(2)}, u32[]{:S(2)}) collective-permute-start(bf16[768,1024]{1,0:T(8,128)(2,1)} %shard_map.113), channel_id=1, source_target_pairs={{8,24},{9,25},{10,26},{11,27},{12,28},{13,29},{14,30},{15,31},{24,... | collective-permute-start | bytes 4718600 | tf_op jit(solution)/shard_map/ppermute | solution.py:371
  56.0 1.8 slice_select_fusion.1
  64.5 2.3 %collective-permute-start.30 = (bf16[768,1024]{1,0:T(8,128)(2,1)}, bf16[768,1024]{1,0:T(8,128)(2,1)}, u32[]{:S(2)}, u32[]{:S(2)}) collective-permute-start(bf16[768,1024]{1,0:T(8,128)(2,1)} %shard_map.113), channel_id=1, source_target_pairs={{0,16},{1,17},{2,18},{3,19},{4,20},{5,21},{6,22},{7,23},{16,0},{17... | collective-permute-start | bytes 4718600 | tf_op jit(solution)/shard_map/ppermute | solution.py:371
  68.3 1.8 slice_select_fusion
  71.4 3.3 %collective-permute-start.19 = (bf16[128,1024]{1,0:T(8,128)(2,1)}, bf16[128,1024]{1,0:T(8,128)(2,1)S(1)}, u32[]{:S(2)}, u32[]{:S(2)}) collective-permute-start(bf16[128,1024]{1,0:T(8,128)(2,1)} %copy-done.11), channel_id=1, source_target_pairs={{0,2},{1,3},{2,0},{3,1},{12,14},{13,15},{14,12},{15,13},{16,18},{1... | collective-permute-start | bytes 786440 | tf_op jit(solution)/shard_map/ppermute | solution.py:371
  75.3 1.4 add_select_fusion.refs_0_
  77.5 3.4 %collective-permute-done.19.refs_2_ = bf16[128,1024]{1,0:T(8,128)(2,1)S(1)} collective-permute-done((bf16[128,1024]{1,0:T(8,128)(2,1)}, bf16[128,1024]{1,0:T(8,128)(2,1)S(1)}, u32[]{:S(2)}, u32[]{:S(2)}) %collective-permute-start.19) | collective-permute-done | bytes 262176 | tf_op jit(solution)/shard_map/ppermute | solution.py:371
  83.2 1.7 collective-permute-start.31
  89.7 8.4 %collective-permute-done.31 = bf16[128,896]{1,0:T(8,128)(2,1)S(1)} collective-permute-done((bf16[128,896]{1,0:T(8,128)(2,1)S(1)}, bf16[128,896]{1,0:T(8,128)(2,1)S(1)}, u32[]{:S(2)}, u32[]{:S(2)}) %collective-permute-start.31) | collective-permute-done | bytes 229408 | tf_op jit(solution)/shard_map/ppermute | solution.py:371
  107.0 1.6 collective-permute-start.36
  108.7 1.6 broadcast_select_fusion
  110.3 62.8 %collective-permute-done.36 = bf16[128,1024]{1,0:T(8,128)(2,1)S(1)} collective-permute-done((bf16[128,1024]{1,0:T(8,128)(2,1)S(1)}, bf16[128,1024]{1,0:T(8,128)(2,1)S(1)}, u32[]{:S(2)}, u32[]{:S(2)}) %collective-permute-start.36) | collective-permute-done | bytes 262176 | tf_op jit(solution)/shard_map/ppermute | solution.py:371
  176.0 1.8 collective-permute-start.37
  179.4 4.8 %collective-permute-done.37 = bf16[128,768]{1,0:T(8,128)(2,1)S(1)} collective-permute-done((bf16[128,768]{1,0:T(8,128)(2,1)S(1)}, bf16[128,768]{1,0:T(8,128)(2,1)S(1)}, u32[]{:S(2)}, u32[]{:S(2)}) %collective-permute-start.37) | collective-permute-done | bytes 196640 | tf_op jit(solution)/shard_map/ppermute | solution.py:371
  184.3 2.5 %fusion.27 = (bf16[1,1,1024,768]{3,2,1,0:T(8,128)(2,1)S(1)}, bf16[1,1,1024,768]{3,2,1,0:T(8,128)(2,1)S(1)}) fusion(bf16[1,1,1024,768]{3,2,1,0:T(8,128)(2,1)S(1)} %get-tuple-element.148, s32[]{:T(128)S(6)} %select_n.160, bf16[1024,768]{1,0:T(8,128)(2,1)} %collective-permute-done.7, bf16[1,1,1024,768]{3,2,1,0:T(8,128)(2,1)S(1)} %copy-done.6, ...), kind=kOutput, calls=%fused_computation.44 | convolution fusion | flops 108920832 | bytes 5832708 | tf_op jit(solution)/shard_map/dot_general | solution.py:22
  (155 shorter events, 55.0 us)
Async XLA Ops:
  1.5 9.3 %collective-permute-start = (bf16[128,256]{1,0:T(8,128)(2,1)S(1)}, bf16[128,256]{1,0:T(8,128)(2,1)S(1)}, u32[]{:S(2)}, u32[]{:S(2)}) collective-permute-start(bf16[128,256]{1,0:T(8,128)(2,1)S(1)} %select_bitcast_fusion), channel_id=1, source_target_pairs={{0,1},{1,0},{2,3},{3,2},{12,13},{13,12},{14,15},{15,14},{16,17},{1... | collective-permute-start | bytes 196616 | tf_op jit(solution)/shard_map/ppermute | solution.py:371
  6.5 26.3 %collective-permute-start.8 = (bf16[1024,768]{1,0:T(8,128)(2,1)}, bf16[1024,768]{1,0:T(8,128)(2,1)}, u32[]{:S(2)}, u32[]{:S(2)}) collective-permute-start(bf16[1024,768]{1,0:T(8,128)(2,1)} %bitcast.83), channel_id=1, source_target_pairs={{5,4},{7,6},{9,8},{11,10},{12,13},{14,15},{21,20},{23,22},{25,24},... | collective-permute-start | bytes 4718600 | tf_op jit(solution)/shard_map/ppermute | solution.py:371
  14.9 35.7 %collective-permute-start.7 = (bf16[1024,768]{1,0:T(8,128)(2,1)}, bf16[1024,768]{1,0:T(8,128)(2,1)}, u32[]{:S(2)}, u32[]{:S(2)}) collective-permute-start(bf16[1024,768]{1,0:T(8,128)(2,1)} %shard_map.112), channel_id=1, source_target_pairs={{0,16},{1,17},{2,18},{3,19},{4,20},{5,21},{6,22},{7,23},{8,24},{9,... | collective-permute-start | bytes 4718600 | tf_op jit(solution)/shard_map/ppermute | solution.py:371
  16.5 9.2 %collective-permute-start.1 = (bf16[256,256]{1,0:T(8,128)(2,1)S(1)}, bf16[256,256]{1,0:T(8,128)(2,1)S(1)}, u32[]{:S(2)}, u32[]{:S(2)}) collective-permute-start(bf16[256,256]{1,0:T(8,128)(2,1)S(1)} %pad_maximum_fusion.1.refs_1_.refs_3_), channel_id=1, source_target_pairs={{0,2},{1,3},{2,0},{3,1},{12,14},{13,15},{14,12},{15,13},{16,18},{1... | collective-permute-start | bytes 393224 | tf_op jit(solution)/shard_map/ppermute | solution.py:371
  28.6 11.5 %collective-permute-start.2 = (bf16[128,1024]{1,0:T(8,128)(2,1)}, bf16[128,1024]{1,0:T(8,128)(2,1)}, u32[]{:S(2)}, u32[]{:S(2)}) collective-permute-start(bf16[128,1024]{1,0:T(8,128)(2,1)} %get-tuple-element.73), channel_id=1, source_target_pairs={{0,1},{1,0},{2,3},{3,2},{12,13},{13,12},{14,15},{15,14},{16,17},{1... | collective-permute-start | bytes 786440 | tf_op jit(solution)/shard_map/ppermute | solution.py:371
  32.8 19.7 %collective-permute-start.9 = (bf16[768,1024]{1,0:T(8,128)(2,1)S(1)}, bf16[768,1024]{1,0:T(8,128)(2,1)}, u32[]{:S(2)}, u32[]{:S(2)}) collective-permute-start(bf16[768,1024]{1,0:T(8,128)(2,1)S(1)} %bitcast.74), channel_id=1, source_target_pairs={{5,4},{7,6},{9,8},{11,10},{12,13},{14,15},{21,20},{23,22},{25,24},... | collective-permute-start | bytes 4718600 | tf_op jit(solution)/shard_map/ppermute | solution.py:371
  42.6 8.0 %collective-permute-start.4 = (bf16[64,1024]{1,0:T(8,128)(2,1)}, bf16[64,1024]{1,0:T(8,128)(2,1)}, u32[]{:S(2)}, u32[]{:S(2)}) collective-permute-start(bf16[64,1024]{1,0:T(8,128)(2,1)} %get-tuple-element.151), channel_id=1, source_target_pairs={{1,6},{3,4},{17,22},{19,20}} | collective-permute-start | bytes 393224 | tf_op jit(solution)/shard_map/ppermute | solution.py:371
  43.9 6.7 %collective-permute-start.5 = (bf16[64,1024]{1,0:T(8,128)(2,1)}, bf16[64,1024]{1,0:T(8,128)(2,1)}, u32[]{:S(2)}, u32[]{:S(2)}) collective-permute-start(bf16[64,1024]{1,0:T(8,128)(2,1)} %get-tuple-element.150), channel_id=1, source_target_pairs={{1,20},{3,22},{17,4},{19,6}} | collective-permute-start | bytes 393224 | tf_op jit(solution)/shard_map/ppermute | solution.py:371
  45.2 5.4 %collective-permute-start.6 = (bf16[64,1024]{1,0:T(8,128)(2,1)}, bf16[64,1024]{1,0:T(8,128)(2,1)}, u32[]{:S(2)}, u32[]{:S(2)}) collective-permute-start(bf16[64,1024]{1,0:T(8,128)(2,1)} %get-tuple-element.150), channel_id=1, source_target_pairs={{1,22},{3,20},{17,6},{19,4}} | collective-permute-start | bytes 393224 | tf_op jit(solution)/shard_map/ppermute | solution.py:371
  50.6 12.6 %collective-permute-start.18 = (bf16[768,1024]{1,0:T(8,128)(2,1)}, bf16[768,1024]{1,0:T(8,128)(2,1)}, u32[]{:S(2)}, u32[]{:S(2)}) collective-permute-start(bf16[768,1024]{1,0:T(8,128)(2,1)} %shard_map.113), channel_id=1, source_target_pairs={{8,24},{9,25},{10,26},{11,27},{12,28},{13,29},{14,30},{15,31},{24,... | collective-permute-start | bytes 4718600 | tf_op jit(solution)/shard_map/ppermute | solution.py:371
  58.6 5.9 %collective-permute-start.14 = (bf16[64,1024]{1,0:T(8,128)(2,1)}, bf16[64,1024]{1,0:T(8,128)(2,1)S(1)}, u32[]{:S(2)}, u32[]{:S(2)}) collective-permute-start(bf16[64,1024]{1,0:T(8,128)(2,1)} %get-tuple-element.98), channel_id=1, source_target_pairs={{8,13},{10,15},{24,29},{26,31}} | collective-permute-start | bytes 393224 | tf_op jit(solution)/shard_map/ppermute | solution.py:371
  59.2 7.6 %collective-permute-start.15 = (bf16[64,1024]{1,0:T(8,128)(2,1)}, bf16[64,1024]{1,0:T(8,128)(2,1)}, u32[]{:S(2)}, u32[]{:S(2)}) collective-permute-start(bf16[64,1024]{1,0:T(8,128)(2,1)} %get-tuple-element.98), channel_id=1, source_target_pairs={{8,15},{10,13},{24,31},{26,29}} | collective-permute-start | bytes 393224 | tf_op jit(solution)/shard_map/ppermute | solution.py:371
  60.6 6.2 %collective-permute-start.16 = (bf16[64,1024]{1,0:T(8,128)(2,1)}, bf16[64,1024]{1,0:T(8,128)(2,1)}, u32[]{:S(2)}, u32[]{:S(2)}) collective-permute-start(bf16[64,1024]{1,0:T(8,128)(2,1)} %get-tuple-element.99), channel_id=1, source_target_pairs={{8,29},{10,31},{24,13},{26,15}} | collective-permute-start | bytes 393224 | tf_op jit(solution)/shard_map/ppermute | solution.py:371
  63.2 12.1 %collective-permute-start.20 = (bf16[128,1024]{1,0:T(8,128)(2,1)}, bf16[128,1024]{1,0:T(8,128)(2,1)}, u32[]{:S(2)}, u32[]{:S(2)}) collective-permute-start(bf16[128,1024]{1,0:T(8,128)(2,1)} %slice_select_fusion.1), channel_id=1, source_target_pairs={{1,0},{3,2},{4,5},{6,7},{17,16},{19,18},{20,21},{22,23}} | collective-permute-start | bytes 786440 | tf_op jit(solution)/shard_map/ppermute | solution.py:371
  64.5 34.4 %collective-permute-start.30 = (bf16[768,1024]{1,0:T(8,128)(2,1)}, bf16[768,1024]{1,0:T(8,128)(2,1)}, u32[]{:S(2)}, u32[]{:S(2)}) collective-permute-start(bf16[768,1024]{1,0:T(8,128)(2,1)} %shard_map.113), channel_id=1, source_target_pairs={{0,16},{1,17},{2,18},{3,19},{4,20},{5,21},{6,22},{7,23},{16,0},{17... | collective-permute-start | bytes 4718600 | tf_op jit(solution)/shard_map/ppermute | solution.py:371
  70.0 5.3 %collective-permute-start.21 = (bf16[128,1024]{1,0:T(8,128)(2,1)}, bf16[128,1024]{1,0:T(8,128)(2,1)}, u32[]{:S(2)}, u32[]{:S(2)}) collective-permute-start(bf16[128,1024]{1,0:T(8,128)(2,1)} %slice_select_fusion), channel_id=1, source_target_pairs={{8,9},{10,11},{13,12},{15,14},{24,25},{26,27},{29,28},{31,30}} | collective-permute-start | bytes 786440 | tf_op jit(solution)/shard_map/ppermute | solution.py:371
  71.4 9.5 %collective-permute-start.19 = (bf16[128,1024]{1,0:T(8,128)(2,1)}, bf16[128,1024]{1,0:T(8,128)(2,1)S(1)}, u32[]{:S(2)}, u32[]{:S(2)}) collective-permute-start(bf16[128,1024]{1,0:T(8,128)(2,1)} %copy-done.11), channel_id=1, source_target_pairs={{0,2},{1,3},{2,0},{3,1},{12,14},{13,15},{14,12},{15,13},{16,18},{1... | collective-permute-start | bytes 786440 | tf_op jit(solution)/shard_map/ppermute | solution.py:371
  83.2 14.9 %collective-permute-start.31 = (bf16[128,896]{1,0:T(8,128)(2,1)S(1)}, bf16[128,896]{1,0:T(8,128)(2,1)S(1)}, u32[]{:S(2)}, u32[]{:S(2)}) collective-permute-start(bf16[128,896]{1,0:T(8,128)(2,1)S(1)} %pad_maximum_fusion), channel_id=1, source_target_pairs={{0,16},{1,17},{2,18},{3,19},{4,20},{5,21},{6,22},{7,23},{8,24},{9,... | collective-permute-start | bytes 688136 | tf_op jit(solution)/shard_map/ppermute | solution.py:371
  87.7 11.1 %collective-permute-start.26 = (bf16[64,1024]{1,0:T(8,128)(2,1)S(1)}, bf16[64,1024]{1,0:T(8,128)(2,1)S(1)}, u32[]{:S(2)}, u32[]{:S(2)}) collective-permute-start(bf16[64,1024]{1,0:T(8,128)(2,1)S(1)} %get-tuple-element.120), channel_id=1, source_target_pairs={{8,4},{10,6},{24,20},{26,22}} | collective-permute-start | bytes 393224 | tf_op jit(solution)/shard_map/ppermute | solution.py:371
  88.4 10.5 %collective-permute-start.27 = (bf16[64,1024]{1,0:T(8,128)(2,1)S(1)}, bf16[64,1024]{1,0:T(8,128)(2,1)S(1)}, u32[]{:S(2)}, u32[]{:S(2)}) collective-permute-start(bf16[64,1024]{1,0:T(8,128)(2,1)S(1)} %get-tuple-element.120), channel_id=1, source_target_pairs={{8,6},{10,4},{24,22},{26,20}} | collective-permute-start | bytes 393224 | tf_op jit(solution)/shard_map/ppermute | solution.py:371
  89.1 9.8 %collective-permute-start.28 = (bf16[64,1024]{1,0:T(8,128)(2,1)S(1)}, bf16[64,1024]{1,0:T(8,128)(2,1)S(1)}, u32[]{:S(2)}, u32[]{:S(2)}) collective-permute-start(bf16[64,1024]{1,0:T(8,128)(2,1)S(1)} %get-tuple-element.121), channel_id=1, source_target_pairs={{8,20},{10,22},{24,4},{26,6}} | collective-permute-start | bytes 393224 | tf_op jit(solution)/shard_map/ppermute | solution.py:371
  107.0 66.0 %collective-permute-start.36 = (bf16[128,1024]{1,0:T(8,128)(2,1)S(1)}, bf16[128,1024]{1,0:T(8,128)(2,1)S(1)}, u32[]{:S(2)}, u32[]{:S(2)}) collective-permute-start(bf16[128,1024]{1,0:T(8,128)(2,1)S(1)} %fusion.28), channel_id=1, source_target_pairs={{1,0},{3,2},{4,5},{6,7},{8,9},{10,11},{13,12},{15,14},{17,16},{19,... | collective-permute-start | bytes 786440 | tf_op jit(solution)/shard_map/ppermute | solution.py:371
  175.7 11.1 %collective-permute-start.38 = (bf16[128,1024]{1,0:T(8,128)(2,1)S(1)}, bf16[128,1024]{1,0:T(8,128)(2,1)S(1)}, u32[]{:S(2)}, u32[]{:S(2)}) collective-permute-start(bf16[128,1024]{1,0:T(8,128)(2,1)S(1)} %broadcast_select_fusion.1.refs_0_), channel_id=1, source_target_pairs={{0,16},{1,17},{2,18},{3,19},{4,20},{5,21},{6,22},{7,23},{8,24},{9,... | collective-permute-start | bytes 786440 | tf_op jit(solution)/shard_map/ppermute | solution.py:371
  176.0 8.3 %collective-permute-start.37 = (bf16[128,768]{1,0:T(8,128)(2,1)S(1)}, bf16[128,768]{1,0:T(8,128)(2,1)S(1)}, u32[]{:S(2)}, u32[]{:S(2)}) collective-permute-start(bf16[128,768]{1,0:T(8,128)(2,1)S(1)} %shard_map.121), channel_id=1, source_target_pairs={{0,16},{1,17},{2,18},{3,19},{4,20},{5,21},{6,22},{7,23},{8,24},{9,... | collective-permute-start | bytes 589832 | tf_op jit(solution)/shard_map/ppermute | solution.py:371
  (40 other events, 264.4 us)

commit v9 on v7

--- a/solution.py
+++ b/solution.py
@@ -406,8 +406,8 @@
         return move(array, ends, lambda r, s, j: (r, s, j ^ offset))
 
     pair = jnp.concatenate([edge, at_ends(edge, 1)])
-    pair, packed_weight = lax.optimization_barrier((pair, weight_in))
-    edges = [pair, at_ends(pair, 2)]
+    second, packed_weight = lax.optimization_barrier((at_ends(pair, 2), weight_in))
+    edges = [pair, second]
     rest = range(1, sections)
     near_in = to_holders(weight_in, 1, rest)
     near_in, next_out = lax.optimization_barrier((near_in, weight_out))
@@ -512,6 +512,11 @@
         )
         if step in (len(late) - 1, links):
             rows = kept_of(stores, range(step + 1), True)
+        if step == 1:
+            sends, far_states_in, packed_out = lax.optimization_barrier(
+                (sends, far_states_in, packed_out)
+            )
+            far_states_out = exchange(packed_out, early)
         if step == 0:
             total = sends[0].astype(jnp.float32)
             total = total + at_ends(sends[0], 1).astype(jnp.float32)
@@ -520,11 +525,6 @@
                 sends = [piece(sends[0], slots[0, e], block_rows) for e in range(replicas)]
         if step < links:
             received = send_blocks(sends, back, slots[step], step, 1)
-            if step == 0:
-                received, far_states_in, packed_out = lax.optimization_barrier(
-                    (received, far_states_in, packed_out)
-                )
-                far_states_out = exchange(packed_out, early)
         else:
             received = [sends[0], at_ends(sends[0], 2)]
             row_parts.append(from_holders(rows, 1, early))

time: 190 us -> 212 us (1.12)
  waiting for transfers between devices: 91.2 us -> 107 us
  local copies, waits for them, and re-layouts: 8.31 us -> 14.3 us
    ppermute x39, waiting for transfers between devices: 91.2 us -> 107 us  [move(): return lax.ppermute(array, axes, pairs)]
    unnamed x50 -> x64, local copies, waits for them, and re-layouts: 6.82 us -> 12.7 us
  transfers between devices with their start and end apart: 39 -> 39, of which waited for: 7 -> 8; matrix products, arithmetic and copies ran while one was open for 9% -> 8% of each run, Pallas kernels for 6% -> 5%
where the time goes in v9:
time: 212 us; the launch traced here: 210 us
  waiting for transfers between devices  107 us (50%)
  starting transfers between devices  52.7 us (25%)
  local copies, waits for them, and re-layouts  14.3 us (7%)
  other arithmetic  13.5 us (6%)
  Pallas kernels  11.6 us (5%)
  matrix products  7.45 us (4%)
  between operations  4.27 us (2%)
    ppermute x39, waiting for transfers between devices, move(): return lax.ppermute(array, axes, pairs)  107 us
    ppermute x39, starting transfers between devices, move(): return lax.ppermute(array, axes, pairs)  52.7 us
    unnamed x64, local copies, waits for them, and re-layouts  12.7 us
    pallas_call x7, Pallas kernels, chain_step(): pl.pallas_call(functools.partial(chain_kernel, sz, step, forward, (len(re...  7.59 us
    dot_general x6, matrix products, dot(): lax.dot_general(left, right, dims, preferred_element_type=jnp.float32)  7.45 us
  transfers between devices with their start and end apart: 39, of which 8 were waited for; matrix products, arithmetic and copies ran while one was open for 8% of the time, Pallas kernels for 5%

profile of v9, /device:TPU:0, one launch (start us, length us, event | category | flops | bytes accessed | tf_op | source)
XLA Modules:
  0.0 210.4 jit_solution(9595565623981849880)
XLA Ops:
  2.3 4.9 %collective-permute-start = (bf16[128,256]{1,0:T(8,128)(2,1)S(1)}, bf16[128,256]{1,0:T(8,128)(2,1)S(1)}, u32[]{:S(2)}, u32[]{:S(2)}) collective-permute-start(bf16[128,256]{1,0:T(8,128)(2,1)S(1)} %select_bitcast_fusion), channel_id=1, source_target_pairs={{0,1},{1,0},{2,3},{3,2},{12,13},{13,12},{14,15},{15,14},{16,17},{1... | collective-permute-start | bytes 196616 | tf_op jit(solution)/shard_map/ppermute | solution.py:371
  10.2 4.9 %collective-permute-start.1 = (bf16[256,256]{1,0:T(8,128)(2,1)S(1)}, bf16[256,256]{1,0:T(8,128)(2,1)S(1)}, u32[]{:S(2)}, u32[]{:S(2)}) collective-permute-start(bf16[256,256]{1,0:T(8,128)(2,1)S(1)} %pad_maximum_fusion.1.refs_1_.refs_3_), channel_id=1, source_target_pairs={{0,2},{1,3},{2,0},{3,1},{12,14},{13,15},{14,12},{15,13},{16,18},{1... | collective-permute-start | bytes 393224 | tf_op jit(solution)/shard_map/ppermute | solution.py:371
  17.1 1.8 collective-permute-start.8
  20.3 1.4 copy-done.12
  23.0 2.1 %collective-permute-start.9 = (bf16[1024,768]{1,0:T(8,128)(2,1)}, bf16[1024,768]{1,0:T(8,128)(2,1)}, u32[]{:S(2)}, u32[]{:S(2)}) collective-permute-start(bf16[1024,768]{1,0:T(8,128)(2,1)} %shard_map.113), channel_id=1, source_target_pairs={{0,16},{1,17},{2,18},{3,19},{4,20},{5,21},{6,22},{7,23},{8,24},{9,... | collective-permute-start | bytes 4718600 | tf_op jit(solution)/shard_map/ppermute | solution.py:371
  25.3 2.9 %shard_map.111 = (bf16[128,1024]{1,0:T(8,128)(2,1)}, bf16[18432,1024]{1,0:T(8,128)(2,1)}, f32[6144,1536]{1,0:T(8,128)}) custom-call(s32[6,5]{1,0:T(8,128)S(1)} %fusion.31.refs_0_, bf16[256,256]{1,0:T(8,128)(2,1)S(1)} %pad_maximum_fusion.1.refs_1_.refs_3_, bf16[256,256]{1,0:T(8,128)(2,1)S(1)} %collective-permute-done.1.refs_2_.refs_4_, ...), custom_call_target="tpu_custom_call" | custom-call | flops 805306368 | bytes 6291456 | tf_op jit(solution)/shard_map/pallas_call | solution.py:241
  28.2 3.1 %collective-permute-start.2 = (bf16[128,1024]{1,0:T(8,128)(2,1)}, bf16[128,1024]{1,0:T(8,128)(2,1)}, u32[]{:S(2)}, u32[]{:S(2)}) collective-permute-start(bf16[128,1024]{1,0:T(8,128)(2,1)} %get-tuple-element.72), channel_id=1, source_target_pairs={{0,1},{1,0},{2,3},{3,2},{12,13},{13,12},{14,15},{15,14},{16,17},{1... | collective-permute-start | bytes 786440 | tf_op jit(solution)/shard_map/ppermute | solution.py:371
  33.2 6.4 %collective-permute-done.2 = bf16[128,1024]{1,0:T(8,128)(2,1)} collective-permute-done((bf16[128,1024]{1,0:T(8,128)(2,1)}, bf16[128,1024]{1,0:T(8,128)(2,1)}, u32[]{:S(2)}, u32[]{:S(2)}) %collective-permute-start.2) | collective-permute-done | bytes 262176 | tf_op jit(solution)/shard_map/ppermute | solution.py:371
  52.8 1.6 collective-permute-done.9
  54.4 1.9 collective-permute-start.18
  59.0 1.8 slice_select_fusion
  63.7 4.2 %collective-permute-start.30 = (bf16[768,1024]{1,0:T(8,128)(2,1)}, bf16[768,1024]{1,0:T(8,128)(2,1)}, u32[]{:S(2)}, u32[]{:S(2)}) collective-permute-start(bf16[768,1024]{1,0:T(8,128)(2,1)} %shard_map.114), channel_id=1, source_target_pairs={{0,16},{1,17},{2,18},{3,19},{4,20},{5,21},{6,22},{7,23},{16,0},{17... | collective-permute-start | bytes 4718600 | tf_op jit(solution)/shard_map/ppermute | solution.py:371
  76.0 1.9 select_select_fusion
  79.3 2.6 %collective-permute-start.19 = (bf16[128,1024]{1,0:T(8,128)(2,1)}, bf16[128,1024]{1,0:T(8,128)(2,1)S(1)}, u32[]{:S(2)}, u32[]{:S(2)}) collective-permute-start(bf16[128,1024]{1,0:T(8,128)(2,1)} %copy-done.16), channel_id=1, source_target_pairs={{0,2},{1,3},{2,0},{3,1},{12,14},{13,15},{14,12},{15,13},{16,18},{1... | collective-permute-start | bytes 786440 | tf_op jit(solution)/shard_map/ppermute | solution.py:371
  81.9 1.6 collective-permute-done.20
  83.6 1.4 add_select_fusion.refs_0_
  85.7 3.0 %collective-permute-done.19.refs_2_ = bf16[128,1024]{1,0:T(8,128)(2,1)S(1)} collective-permute-done((bf16[128,1024]{1,0:T(8,128)(2,1)}, bf16[128,1024]{1,0:T(8,128)(2,1)S(1)}, u32[]{:S(2)}, u32[]{:S(2)}) %collective-permute-start.19) | collective-permute-done | bytes 262176 | tf_op jit(solution)/shard_map/ppermute | solution.py:371
  96.2 5.0 %collective-permute-done.31 = bf16[128,896]{1,0:T(8,128)(2,1)S(1)} collective-permute-done((bf16[128,896]{1,0:T(8,128)(2,1)S(1)}, bf16[128,896]{1,0:T(8,128)(2,1)S(1)}, u32[]{:S(2)}, u32[]{:S(2)}) %collective-permute-start.31) | collective-permute-done | bytes 229408 | tf_op jit(solution)/shard_map/ppermute | solution.py:371
  106.2 1.5 collective-permute-start.36
  107.8 85.7 %collective-permute-done.36 = bf16[128,1024]{1,0:T(8,128)(2,1)} collective-permute-done((bf16[128,1024]{1,0:T(8,128)(2,1)S(1)}, bf16[128,1024]{1,0:T(8,128)(2,1)}, u32[]{:S(2)}, u32[]{:S(2)}) %collective-permute-start.36) | collective-permute-done | bytes 262176 | tf_op jit(solution)/shard_map/ppermute | solution.py:371
  195.1 1.6 broadcast_select_fusion
  197.5 1.6 collective-permute-start.38
  199.0 1.9 collective-permute-done.37
  205.5 3.2 %fusion.27 = (bf16[1,1,1024,768]{3,2,1,0:T(8,128)(2,1)S(1)}, bf16[1,1,1024,768]{3,2,1,0:T(8,128)(2,1)S(1)}) fusion(bf16[1,1,1024,768]{3,2,1,0:T(8,128)(2,1)S(1)} %get-tuple-element.146, s32[]{:T(128)S(6)} %select_n.158, bf16[1024,768]{1,0:T(8,128)(2,1)} %collective-permute-done.9, bf16[1,1,1024,768]{3,2,1,0:T(8,128)(2,1)S(1)} %copy-done.13, ...), kind=kOutput, calls=%fused_computation.44 | convolution fusion | flops 108920832 | bytes 5832708 | tf_op jit(solution)/shard_map/dot_general | solution.py:22
  (169 shorter events, 57.9 us)
Async XLA Ops:
  0.6 15.3 %collective-permute-start.7 = (bf16[1024,768]{1,0:T(8,128)(2,1)}, bf16[1024,768]{1,0:T(8,128)(2,1)S(1)}, u32[]{:S(2)}, u32[]{:S(2)}) collective-permute-start(bf16[1024,768]{1,0:T(8,128)(2,1)} %bitcast.83), channel_id=1, source_target_pairs={{5,4},{7,6},{9,8},{11,10},{12,13},{14,15},{21,20},{23,22},{25,24},... | collective-permute-start | bytes 4718600 | tf_op jit(solution)/shard_map/ppermute | solution.py:371
  2.3 7.9 %collective-permute-start = (bf16[128,256]{1,0:T(8,128)(2,1)S(1)}, bf16[128,256]{1,0:T(8,128)(2,1)S(1)}, u32[]{:S(2)}, u32[]{:S(2)}) collective-permute-start(bf16[128,256]{1,0:T(8,128)(2,1)S(1)} %select_bitcast_fusion), channel_id=1, source_target_pairs={{0,1},{1,0},{2,3},{3,2},{12,13},{13,12},{14,15},{15,14},{16,17},{1... | collective-permute-start | bytes 196616 | tf_op jit(solution)/shard_map/ppermute | solution.py:371
  10.2 8.7 %collective-permute-start.1 = (bf16[256,256]{1,0:T(8,128)(2,1)S(1)}, bf16[256,256]{1,0:T(8,128)(2,1)S(1)}, u32[]{:S(2)}, u32[]{:S(2)}) collective-permute-start(bf16[256,256]{1,0:T(8,128)(2,1)S(1)} %pad_maximum_fusion.1.refs_1_.refs_3_), channel_id=1, source_target_pairs={{0,2},{1,3},{2,0},{3,1},{12,14},{13,15},{14,12},{15,13},{16,18},{1... | collective-permute-start | bytes 393224 | tf_op jit(solution)/shard_map/ppermute | solution.py:371
  17.1 33.0 %collective-permute-start.8 = (bf16[768,1024]{1,0:T(8,128)(2,1)}, bf16[768,1024]{1,0:T(8,128)(2,1)}, u32[]{:S(2)}, u32[]{:S(2)}) collective-permute-start(bf16[768,1024]{1,0:T(8,128)(2,1)} %bitcast.73), channel_id=1, source_target_pairs={{5,4},{7,6},{9,8},{11,10},{12,13},{14,15},{21,20},{23,22},{25,24},... | collective-permute-start | bytes 4718600 | tf_op jit(solution)/shard_map/ppermute | solution.py:371
  23.0 31.4 %collective-permute-start.9 = (bf16[1024,768]{1,0:T(8,128)(2,1)}, bf16[1024,768]{1,0:T(8,128)(2,1)}, u32[]{:S(2)}, u32[]{:S(2)}) collective-permute-start(bf16[1024,768]{1,0:T(8,128)(2,1)} %shard_map.113), channel_id=1, source_target_pairs={{0,16},{1,17},{2,18},{3,19},{4,20},{5,21},{6,22},{7,23},{8,24},{9,... | collective-permute-start | bytes 4718600 | tf_op jit(solution)/shard_map/ppermute | solution.py:371
  28.2 11.5 %collective-permute-start.2 = (bf16[128,1024]{1,0:T(8,128)(2,1)}, bf16[128,1024]{1,0:T(8,128)(2,1)}, u32[]{:S(2)}, u32[]{:S(2)}) collective-permute-start(bf16[128,1024]{1,0:T(8,128)(2,1)} %get-tuple-element.72), channel_id=1, source_target_pairs={{0,1},{1,0},{2,3},{3,2},{12,13},{13,12},{14,15},{15,14},{16,17},{1... | collective-permute-start | bytes 786440 | tf_op jit(solution)/shard_map/ppermute | solution.py:371
  42.1 8.0 %collective-permute-start.4 = (bf16[64,1024]{1,0:T(8,128)(2,1)}, bf16[64,1024]{1,0:T(8,128)(2,1)}, u32[]{:S(2)}, u32[]{:S(2)}) collective-permute-start(bf16[64,1024]{1,0:T(8,128)(2,1)} %get-tuple-element.149), channel_id=1, source_target_pairs={{1,6},{3,4},{17,22},{19,20}} | collective-permute-start | bytes 393224 | tf_op jit(solution)/shard_map/ppermute | solution.py:371
  43.4 6.6 %collective-permute-start.5 = (bf16[64,1024]{1,0:T(8,128)(2,1)}, bf16[64,1024]{1,0:T(8,128)(2,1)}, u32[]{:S(2)}, u32[]{:S(2)}) collective-permute-start(bf16[64,1024]{1,0:T(8,128)(2,1)} %get-tuple-element.148), channel_id=1, source_target_pairs={{1,20},{3,22},{17,4},{19,6}} | collective-permute-start | bytes 393224 | tf_op jit(solution)/shard_map/ppermute | solution.py:371
  44.8 5.3 %collective-permute-start.6 = (bf16[64,1024]{1,0:T(8,128)(2,1)}, bf16[64,1024]{1,0:T(8,128)(2,1)}, u32[]{:S(2)}, u32[]{:S(2)}) collective-permute-start(bf16[64,1024]{1,0:T(8,128)(2,1)} %get-tuple-element.148), channel_id=1, source_target_pairs={{1,22},{3,20},{17,6},{19,4}} | collective-permute-start | bytes 393224 | tf_op jit(solution)/shard_map/ppermute | solution.py:371
  54.4 18.7 %collective-permute-start.18 = (bf16[768,1024]{1,0:T(8,128)(2,1)}, bf16[768,1024]{1,0:T(8,128)(2,1)}, u32[]{:S(2)}, u32[]{:S(2)}) collective-permute-start(bf16[768,1024]{1,0:T(8,128)(2,1)} %shard_map.114), channel_id=1, source_target_pairs={{8,24},{9,25},{10,26},{11,27},{12,28},{13,29},{14,30},{15,31},{24,... | collective-permute-start | bytes 4718600 | tf_op jit(solution)/shard_map/ppermute | solution.py:371
  56.3 4.5 %collective-permute-start.10 = (bf16[64,1024]{1,0:T(8,128)(2,1)}, bf16[64,1024]{1,0:T(8,128)(2,1)S(1)}, u32[]{:S(2)}, u32[]{:S(2)}) collective-permute-start(bf16[64,1024]{1,0:T(8,128)(2,1)} %copy-done.23), channel_id=1, source_target_pairs={{4,8},{6,10},{20,24},{22,26}} | collective-permute-start | bytes 393224 | tf_op jit(solution)/shard_map/ppermute | solution.py:371
  63.0 7.5 %collective-permute-start.14 = (bf16[64,1024]{1,0:T(8,128)(2,1)}, bf16[64,1024]{1,0:T(8,128)(2,1)S(1)}, u32[]{:S(2)}, u32[]{:S(2)}) collective-permute-start(bf16[64,1024]{1,0:T(8,128)(2,1)} %get-tuple-element.95), channel_id=1, source_target_pairs={{8,13},{10,15},{24,29},{26,31}} | collective-permute-start | bytes 393224 | tf_op jit(solution)/shard_map/ppermute | solution.py:371
  63.7 31.8 %collective-permute-start.30 = (bf16[768,1024]{1,0:T(8,128)(2,1)}, bf16[768,1024]{1,0:T(8,128)(2,1)}, u32[]{:S(2)}, u32[]{:S(2)}) collective-permute-start(bf16[768,1024]{1,0:T(8,128)(2,1)} %shard_map.114), channel_id=1, source_target_pairs={{0,16},{1,17},{2,18},{3,19},{4,20},{5,21},{6,22},{7,23},{16,0},{17... | collective-permute-start | bytes 4718600 | tf_op jit(solution)/shard_map/ppermute | solution.py:371
  71.8 11.8 %collective-permute-start.20 = (bf16[128,1024]{1,0:T(8,128)(2,1)}, bf16[128,1024]{1,0:T(8,128)(2,1)}, u32[]{:S(2)}, u32[]{:S(2)}) collective-permute-start(bf16[128,1024]{1,0:T(8,128)(2,1)} %slice_select_fusion), channel_id=1, source_target_pairs={{1,0},{3,2},{4,5},{6,7},{17,16},{19,18},{20,21},{22,23}} | collective-permute-start | bytes 786440 | tf_op jit(solution)/shard_map/ppermute | solution.py:371
  77.9 5.6 %collective-permute-start.21 = (bf16[128,1024]{1,0:T(8,128)(2,1)}, bf16[128,1024]{1,0:T(8,128)(2,1)}, u32[]{:S(2)}, u32[]{:S(2)}) collective-permute-start(bf16[128,1024]{1,0:T(8,128)(2,1)} %select_select_fusion), channel_id=1, source_target_pairs={{8,9},{10,11},{13,12},{15,14},{24,25},{26,27},{29,28},{31,30}} | collective-permute-start | bytes 786440 | tf_op jit(solution)/shard_map/ppermute | solution.py:371
  79.3 9.5 %collective-permute-start.19 = (bf16[128,1024]{1,0:T(8,128)(2,1)}, bf16[128,1024]{1,0:T(8,128)(2,1)S(1)}, u32[]{:S(2)}, u32[]{:S(2)}) collective-permute-start(bf16[128,1024]{1,0:T(8,128)(2,1)} %copy-done.16), channel_id=1, source_target_pairs={{0,2},{1,3},{2,0},{3,1},{12,14},{13,15},{14,12},{15,13},{16,18},{1... | collective-permute-start | bytes 786440 | tf_op jit(solution)/shard_map/ppermute | solution.py:371
  92.6 8.6 %collective-permute-start.31 = (bf16[128,896]{1,0:T(8,128)(2,1)S(1)}, bf16[128,896]{1,0:T(8,128)(2,1)S(1)}, u32[]{:S(2)}, u32[]{:S(2)}) collective-permute-start(bf16[128,896]{1,0:T(8,128)(2,1)S(1)} %pad_maximum_fusion), channel_id=1, source_target_pairs={{0,16},{1,17},{2,18},{3,19},{4,20},{5,21},{6,22},{7,23},{8,24},{9,... | collective-permute-start | bytes 688136 | tf_op jit(solution)/shard_map/ppermute | solution.py:371
  93.4 7.7 %collective-permute-start.26 = (bf16[64,1024]{1,0:T(8,128)(2,1)S(1)}, bf16[64,1024]{1,0:T(8,128)(2,1)S(1)}, u32[]{:S(2)}, u32[]{:S(2)}) collective-permute-start(bf16[64,1024]{1,0:T(8,128)(2,1)S(1)} %get-tuple-element.117), channel_id=1, source_target_pairs={{8,4},{10,6},{24,20},{26,22}} | collective-permute-start | bytes 393224 | tf_op jit(solution)/shard_map/ppermute | solution.py:371
  94.1 7.0 %collective-permute-start.27 = (bf16[64,1024]{1,0:T(8,128)(2,1)S(1)}, bf16[64,1024]{1,0:T(8,128)(2,1)S(1)}, u32[]{:S(2)}, u32[]{:S(2)}) collective-permute-start(bf16[64,1024]{1,0:T(8,128)(2,1)S(1)} %get-tuple-element.117), channel_id=1, source_target_pairs={{8,6},{10,4},{24,22},{26,20}} | collective-permute-start | bytes 393224 | tf_op jit(solution)/shard_map/ppermute | solution.py:371
  94.8 6.4 %collective-permute-start.28 = (bf16[64,1024]{1,0:T(8,128)(2,1)S(1)}, bf16[64,1024]{1,0:T(8,128)(2,1)S(1)}, u32[]{:S(2)}, u32[]{:S(2)}) collective-permute-start(bf16[64,1024]{1,0:T(8,128)(2,1)S(1)} %get-tuple-element.118), channel_id=1, source_target_pairs={{8,20},{10,22},{24,4},{26,6}} | collective-permute-start | bytes 393224 | tf_op jit(solution)/shard_map/ppermute | solution.py:371
  95.5 5.7 %collective-permute-start.29 = (bf16[64,1024]{1,0:T(8,128)(2,1)S(1)}, bf16[64,1024]{1,0:T(8,128)(2,1)S(1)}, u32[]{:S(2)}, u32[]{:S(2)}) collective-permute-start(bf16[64,1024]{1,0:T(8,128)(2,1)S(1)} %get-tuple-element.118), channel_id=1, source_target_pairs={{8,22},{10,20},{24,6},{26,4}} | collective-permute-start | bytes 393224 | tf_op jit(solution)/shard_map/ppermute | solution.py:371
  106.2 87.2 %collective-permute-start.36 = (bf16[128,1024]{1,0:T(8,128)(2,1)S(1)}, bf16[128,1024]{1,0:T(8,128)(2,1)}, u32[]{:S(2)}, u32[]{:S(2)}) collective-permute-start(bf16[128,1024]{1,0:T(8,128)(2,1)S(1)} %fusion.28), channel_id=1, source_target_pairs={{1,0},{3,2},{4,5},{6,7},{8,9},{10,11},{13,12},{15,14},{17,16},{19,... | collective-permute-start | bytes 786440 | tf_op jit(solution)/shard_map/ppermute | solution.py:371
  194.5 6.4 %collective-permute-start.37 = (bf16[128,1024]{1,0:T(8,128)(2,1)S(1)}, bf16[128,1024]{1,0:T(8,128)(2,1)S(1)}, u32[]{:S(2)}, u32[]{:S(2)}) collective-permute-start(bf16[128,1024]{1,0:T(8,128)(2,1)S(1)} %broadcast_select_fusion.1.refs_0_), channel_id=1, source_target_pairs={{0,16},{1,17},{2,18},{3,19},{4,20},{5,21},{6,22},{7,23},{8,24},{9,... | collective-permute-start | bytes 786440 | tf_op jit(solution)/shard_map/ppermute | solution.py:371
  197.5 8.0 %collective-permute-start.38 = (bf16[128,768]{1,0:T(8,128)(2,1)S(1)}, bf16[128,768]{1,0:T(8,128)(2,1)S(1)}, u32[]{:S(2)}, u32[]{:S(2)}) collective-permute-start(bf16[128,768]{1,0:T(8,128)(2,1)S(1)} %shard_map.121), channel_id=1, source_target_pairs={{0,16},{1,17},{2,18},{3,19},{4,20},{5,21},{6,22},{7,23},{8,24},{9,... | collective-permute-start | bytes 589832 | tf_op jit(solution)/shard_map/ppermute | solution.py:371
  (47 other events, 137.4 us)
